TPU v7x, 32 devices: a whole 2x2x4 slice. The times are simulated.
32 devices in a mesh: grp: 2 (over y), ctx: 4 (over z), head: 4 (over x, core).
Axes of the slice: x: 2, y: 2, z: 4, core: 2. Of those that a mesh axis runs over, the one named last changes fastest.
Arguments:
- queries: bfloat16 [1024, 4096], P(('grp', 'ctx', 'head')), parts along dimension 0, may hold values from -80 to 80
- span_key_value: bfloat16 [1024, 1024], P(('grp', 'ctx', 'head')), parts along dimension 0, may hold values from -4 to 4
- cache: bfloat16 [4, 16384, 256], P('head', ('grp', 'ctx')), parts along dimension 1, may hold values from -4 to 4
- pattern: int32 [8, 2], P('grp'), parts along dimension 0, may hold values from 0 to 63, as said below
- counts: int32 [8], P('grp'), parts along dimension 0, may hold values from 1 to 2
Outputs:
- attended: bfloat16 [1024, 4096], P(('grp', 'ctx', 'head')), parts along dimension 0
There are 2 independent parts, one for each index of `grp`. A program takes and returns all parts, laid end to end along the dimension named above; each array names one. Nothing has to cross between parts.
Inputs may be any that keep to these rules, and one draw needn't show every extreme that they name: Entries of pattern[b, i] for i < counts[b] are distinct and no two have the same value of pattern[b, i] // 16; unused entries are 0.
All inputs are finite; a program needn't handle non-finite values.
Results may differ from a plain program's by a relative error of at most 0.0045.
Values may be sent and summed in bfloat16 or wider, within the bound.
No kernel may reach another device: no remote copies, remote signals or barrier semaphores. Data moves between devices by JAX's collectives and lax.ppermute only.
A program may use at most 64 MiB of HBM per device.

v0:
```python
import math

import jax
import jax.numpy as jnp
from jax import lax
from jax.sharding import PartitionSpec as P


def absorb(carried, query_head_rows, key_rows, values, allowed, score_scale):
    running_max, denom, weighted = carried
    scores = (
        jnp.einsum("tgjd,gkd->gjtk", query_head_rows, key_rows, preferred_element_type=jnp.float32)
        * score_scale
    )
    masked = jnp.where(allowed, scores, -jnp.inf)
    new_max = jnp.maximum(running_max, jnp.max(masked, axis=-1))
    factor = jnp.exp(running_max - new_max)
    weights = jnp.where(allowed, jnp.exp(scores - new_max[..., None]), 0.0)
    denom = denom * factor + jnp.sum(weights, axis=-1)
    weighted = weighted * factor[..., None] + jnp.einsum(
        "gjtk,gkd->gjtd", weights.astype(jnp.bfloat16), values, preferred_element_type=jnp.float32
    )
    return (new_max, denom, weighted)


def local(queries, span_key_value, cache, pattern, counts):
    q_block, kv_block = (
        lax.all_to_all(queries, "head", split_axis=1, concat_axis=0, tiled=True),
        lax.all_to_all(span_key_value, "head", split_axis=1, concat_axis=0, tiled=True),
    )
    blk_rows = q_block.shape[0]
    kv_heads = cache.shape[0]
    head_dim = cache.shape[2] // 2
    heads_per_group = q_block.shape[1] // (kv_heads * head_dim)
    score_scale = 1.0 / math.sqrt(head_dim)
    position = lax.axis_index("ctx")
    dev_blocks = cache.shape[1] // blk_rows
    list_width = pattern.shape[1]
    is_listed = jnp.arange(list_width)[None, :] < counts[:, None]
    owners = pattern // dev_blocks
    matches = is_listed & (owners == position)
    wanted = jnp.any(matches, axis=1)
    local_index = jnp.sum(jnp.where(matches, pattern % dev_blocks, 0), axis=1)
    cache_block_list = cache.reshape(kv_heads, dev_blocks, blk_rows, 2 * head_dim)
    outgoing = jnp.take(cache_block_list, local_index, axis=1)
    outgoing = jnp.where(wanted[None, :, None, None], outgoing, jnp.zeros_like(outgoing))
    incoming = lax.all_to_all(outgoing, "ctx", split_axis=1, concat_axis=1, tiled=True)
    my_blocks = lax.dynamic_index_in_dim(pattern, position, 0, keepdims=False)
    my_count = lax.dynamic_index_in_dim(counts, position, 0, keepdims=False)
    my_listed = jnp.arange(list_width) < my_count
    query_head_rows = q_block.reshape(blk_rows, kv_heads, heads_per_group, head_dim)
    self_key_value = kv_block.reshape(blk_rows, kv_heads, 2 * head_dim).transpose(1, 0, 2)
    causal = jnp.arange(blk_rows)[:, None] >= jnp.arange(blk_rows)[None, :]
    carried = (
        jnp.full((kv_heads, heads_per_group, blk_rows), -jnp.inf, jnp.float32),
        jnp.zeros((kv_heads, heads_per_group, blk_rows), jnp.float32),
        jnp.zeros((kv_heads, heads_per_group, blk_rows, head_dim), jnp.float32),
    )
    carried = absorb(
        carried,
        query_head_rows,
        self_key_value[..., :head_dim],
        self_key_value[..., head_dim:],
        causal,
        score_scale,
    )
    source = jnp.take(incoming, my_blocks // dev_blocks, axis=1)
    slot_count = source.shape[1]
    batch_slots = math.gcd(slot_count, 4)

    def absorb_slots(block_index, carried):
        fetched = lax.dynamic_slice_in_dim(source, block_index * batch_slots, batch_slots, 1)
        fetched = fetched.reshape(kv_heads, batch_slots * blk_rows, 2 * head_dim)
        usable = jnp.repeat(
            lax.dynamic_slice_in_dim(my_listed, block_index * batch_slots, batch_slots, 0), blk_rows
        )
        return absorb(
            carried,
            query_head_rows,
            fetched[..., :head_dim],
            fetched[..., head_dim:],
            usable,
            score_scale,
        )

    running_max, denom, weighted = lax.fori_loop(
        0, slot_count // batch_slots, absorb_slots, carried
    )
    result = (
        (weighted / denom[..., None])
        .transpose(2, 0, 1, 3)
        .reshape(blk_rows, kv_heads * heads_per_group * head_dim)
    )
    result = result.astype(jnp.bfloat16)
    return lax.all_to_all(result, "head", split_axis=0, concat_axis=1, tiled=True)


def solution(mesh):
    return jax.shard_map(
        local,
        mesh=mesh,
        in_specs=(
            P(("grp", "ctx", "head"), None),
            P(("grp", "ctx", "head"), None),
            P("head", ("grp", "ctx"), None),
            P("grp", None),
            P("grp"),
        ),
        out_specs=P(("grp", "ctx", "head"), None),
        check_vma=False,
    )
```

profile of v0, /device:TPU:0, one launch (start us, length us, event | category | flops | bytes accessed | tf_op | source)
XLA Modules:
  0.0 46.1 jit_solution(10707775381851283693)
XLA Ops:
  0.0 1.5 %copy.49 = bf16[4,4,8,256]{3,2,0,1:T(8,128)(2,1)} copy(bf16[4,4,8,256]{3,2,1,0:T(8,128)(2,1)} %bitcast.100) | data formatting | bytes 131072 | tf_op jit(solution)/shard_map/all_to_all | solution.py:29
  1.6 4.2 %all-to-all-start = ((bf16[32,4,256]{2,0,1:T(8,128)(2,1)}), bf16[32,4,256]{2,0,1:T(8,128)(2,1)S(1)}, u32[]{:S(2)}, u32[]{:S(2)}) async-start(bf16[32,4,256]{2,0,1:T(8,128)(2,1)} %bitcast.88), calls=%async_computation | async-start | bytes 131072 | tf_op jit(solution)/shard_map/all_to_all | solution.py:29
  5.8 0.7 %copy-done.2 = s32[4,2]{0,1:T(2,128)S(1)} copy-done((s32[4,2]{0,1:T(2,128)S(1)}, s32[4,2]{0,1:T(2,128)}, u32[]{:S(2)}) %copy-start.2) | copy-done | bytes 56
  6.4 0.2 dynamic-slice_reduce_fusion
  6.7 0.6 %copy-done.3 = s32[4]{0:T(128)S(1)} copy-done((s32[4]{0:T(128)S(1)}, s32[4]{0:T(128)}, u32[]{:S(2)}) %copy-start.3) | copy-done | bytes 40
  7.3 0.6 %dynamic_slice.12 = s32[1]{0:T(128)} dynamic-slice(s32[4]{0:T(128)S(1)} %copy-done.3, s32[]{:T(128)S(6)} %select_n.127), dynamic_slice_sizes={1} | dynamic-slice | bytes 12 | tf_op jit(solution)/shard_map/jit(dynamic_index_in_dim)/dynamic_slice | solution.py:49
  8.0 0.7 %iota_compare_fusion.1 = pred[2]{0:T(512)(128)(4,1)S(1)} fusion(s32[]{:T(128)} %bitcast.12), kind=kLoop, calls=%fused_computation.75 | loop fusion | flops 2 | bytes 6 | tf_op jit(solution)/shard_map/lt | solution.py:50
  8.7 0.6 %gather_fusion = bf16[4,128,256]{2,1,0:T(8,128)(2,1)S(1)} fusion(bf16[16,128,256]{2,1,0:T(8,128)(2,1)S(1)} %bitcast.90, s32[1024]{0:T(1024)S(1)} %pad_clamp_fusion.1), kind=kCustom, calls=%fused_computation | custom fusion | bytes 524304 | tf_op jit(solution)/shard_map/jit(_take)/gather | solution.py:45
  9.3 0.8 %fusion.17 = bf16[1,4,128,256]{3,2,0,1:T(8,128)(2,1)} fusion(bf16[4,128,256]{2,1,0:T(8,128)(2,1)S(1)} %gather_fusion, pred[4]{0:T(512)(128)(4,1)S(1)} %compare_and_fusion, pred[4]{0:T(512)(128)(4,1)S(1)} %get-tuple-element.21), kind=kLoop, calls=%fused_computation.27 | loop fusion | flops 262144 | bytes 524296 | tf_op jit(solution)/shard_map/jit(_where)/select_n | solution.py:46
  10.1 0.1 copy-done.1
  10.2 0.7 %copy.48 = bf16[4,4,8,1024]{3,2,0,1:T(8,128)(2,1)} copy(bf16[4,4,8,1024]{3,2,1,0:T(8,128)(2,1)S(1)} %bitcast.99) | data formatting | bytes 524288 | tf_op jit(solution)/shard_map/all_to_all | solution.py:28
  10.9 3.4 %all-to-all-start.1 = ((bf16[32,4,1024]{2,0,1:T(8,128)(2,1)}), bf16[32,4,1024]{2,0,1:T(8,128)(2,1)S(1)}, u32[]{:S(2)}, u32[]{:S(2)}) async-start(bf16[32,4,1024]{2,0,1:T(8,128)(2,1)} %bitcast.87), calls=%async_computation.1 | async-start | bytes 524288 | tf_op jit(solution)/shard_map/all_to_all | solution.py:28
  14.4 5.9 %all-to-all-done.1 = bf16[32,4,1024]{2,0,1:T(8,128)(2,1)S(1)} async-done(((bf16[32,4,1024]{2,0,1:T(8,128)(2,1)}), bf16[32,4,1024]{2,0,1:T(8,128)(2,1)S(1)}, u32[]{:S(2)}, u32[]{:S(2)}) %all-to-all-start.1) | async-done | bytes 262176 | tf_op jit(solution)/shard_map/all_to_all | solution.py:28
  20.4 5.4 %all-to-all-start.2 = ((bf16[1,4,128,256]{3,2,0,1:T(8,128)(2,1)}), bf16[1,4,128,256]{3,2,0,1:T(8,128)(2,1)S(1)}, u32[]{:S(2)}, u32[]{:S(2)}) async-start(bf16[1,4,128,256]{3,2,0,1:T(8,128)(2,1)} %fusion.17), calls=%async_computation.2 | async-start | bytes 524288 | tf_op jit(solution)/shard_map/all_to_all | solution.py:47
  25.8 0.2 select_reduce_fusion.1
  26.2 8.3 %all-to-all-done.2 = bf16[1,4,128,256]{3,2,0,1:T(8,128)(2,1)S(1)} async-done(((bf16[1,4,128,256]{3,2,0,1:T(8,128)(2,1)}), bf16[1,4,128,256]{3,2,0,1:T(8,128)(2,1)S(1)}, u32[]{:S(2)}, u32[]{:S(2)}) %all-to-all-start.2) | async-done | bytes 262176 | tf_op jit(solution)/shard_map/all_to_all | solution.py:47
  34.5 0.6 %gather_fusion.1 = bf16[2,128,256]{2,1,0:T(8,128)(2,1)S(1)} fusion(bf16[4,128,256]{2,1,0:T(8,128)(2,1)S(1)} %bitcast.95, s32[1024]{0:T(1024)S(1)} %pad_clamp_fusion), kind=kCustom, calls=%fused_computation.1 | custom fusion | bytes 262152 | tf_op jit(solution)/shard_map/jit(_take)/gather | solution.py:67
  35.1 0.3 select_reduce_fusion
  35.4 0.2 fusion.6
  35.7 0.4 fusion.3
  36.1 0.5 %fusion.5 = bf16[128,1,8,128]{3,0,2,1:T(8,128)(2,1)S(1)} fusion(f32[8,128,128]{2,1,0:T(8,128)S(1)} %fusion.3, f32[1,8,128,256]{2,3,1,0:T(8,128)S(1)} %get-tuple-element.37, f32[8,128]{1,0:T(8,128)S(1)} %max.18, pred[256]{0:T(512)(128)(4,1)S(1)} %broadcast_bitcast_fusion.1, f32[8,128]{1,0:T(8,128)S(1)} %get-tuple-element.19, ...), kind=kOutput, calls=%fused_computation.11 | convolution fusion | flops 68288512 | bytes 1909248 | tf_op jit(solution)/shard_map/while/body/eval_jaxpr/gjtk,gkd->gjtd/dot_general | solution.py:20
  36.6 0.2 copy.30
  36.9 8.4 %all_to_all.53 = bf16[4,32,1024]{2,1,0:T(8,128)(2,1)S(1)} all-to-all(bf16[4,32,1024]{2,1,0:T(8,128)(2,1)S(1)} %convert_element_type.25), channel_id=1, replica_groups=mesh['grp'=2,'ctx'=4,'head'=4] {'head'}, dimensions={0} | all-to-all | bytes 524288 | tf_op jit(solution)/shard_map/all_to_all | solution.py:95
  45.4 0.7 %copy.36 = bf16[4,4,8,1024]{3,2,0,1:T(8,128)(2,1)} copy(bf16[4,4,8,1024]{3,2,1,0:T(8,128)(2,1)S(1)} %bitcast.94) | data formatting | bytes 524288 | tf_op jit(solution)/shard_map/all_to_all | solution.py:95
  (23 shorter events, 0.7 us)
Async XLA Ops:
  0.0 8.7 %copy-start = (bf16[1,2048,256]{2,1,0:T(8,128)(2,1)S(1)}, bf16[1,2048,256]{2,1,0:T(8,128)(2,1)}, u32[]{:S(2)}) copy-start(bf16[1,2048,256]{2,1,0:T(8,128)(2,1)} %param.7) | copy-start | bytes 3145732
  1.6 9.4 %all-to-all-start = ((bf16[32,4,256]{2,0,1:T(8,128)(2,1)}), bf16[32,4,256]{2,0,1:T(8,128)(2,1)S(1)}, u32[]{:S(2)}, u32[]{:S(2)}) async-start(bf16[32,4,256]{2,0,1:T(8,128)(2,1)} %bitcast.88), calls=%async_computation | async-start | bytes 131072 | tf_op jit(solution)/shard_map/all_to_all | solution.py:29
  5.8 0.7 %copy-start.2 = (s32[4,2]{0,1:T(2,128)S(1)}, s32[4,2]{0,1:T(2,128)}, u32[]{:S(2)}) copy-start(s32[4,2]{0,1:T(2,128)} %param.8) | copy-start | bytes 100
  6.6 0.7 %copy-start.3 = (s32[4]{0:T(128)S(1)}, s32[4]{0:T(128)}, u32[]{:S(2)}) copy-start(s32[4]{0:T(128)} %param.9) | copy-start | bytes 52
  9.3 1.0 %copy-start.1 = (bf16[32,4096]{1,0:T(8,128)(2,1)S(1)}, bf16[32,4096]{1,0:T(8,128)(2,1)}, u32[]{:S(2)}) copy-start(bf16[32,4096]{1,0:T(8,128)(2,1)} %param.5) | copy-start | bytes 786436
  10.9 9.4 %all-to-all-start.1 = ((bf16[32,4,1024]{2,0,1:T(8,128)(2,1)}), bf16[32,4,1024]{2,0,1:T(8,128)(2,1)S(1)}, u32[]{:S(2)}, u32[]{:S(2)}) async-start(bf16[32,4,1024]{2,0,1:T(8,128)(2,1)} %bitcast.87), calls=%async_computation.1 | async-start | bytes 524288 | tf_op jit(solution)/shard_map/all_to_all | solution.py:28
  20.4 14.1 %all-to-all-start.2 = ((bf16[1,4,128,256]{3,2,0,1:T(8,128)(2,1)}), bf16[1,4,128,256]{3,2,0,1:T(8,128)(2,1)S(1)}, u32[]{:S(2)}, u32[]{:S(2)}) async-start(bf16[1,4,128,256]{3,2,0,1:T(8,128)(2,1)} %fusion.17), calls=%async_computation.2 | async-start | bytes 524288 | tf_op jit(solution)/shard_map/all_to_all | solution.py:47
where the time goes:
time: 46.6 us; the launch traced here: 46.1 us
  waiting for transfers between devices  14.2 us (30%)
  starting transfers between devices  13 us (28%)
  blocking collectives  8.42 us (18%)
  local copies, waits for them, and re-layouts  6.8 us (15%)
  other arithmetic  2.01 us (4%)
  matrix products  1.46 us (3%)
    all_to_all x1, blocking collectives, local(): lax.all_to_all(result, 'head', split_axis=0, concat_axis=1, tiled=True)  8.42 us
    all_to_all x1, waiting for transfers between devices, local(): lax.all_to_all(outgoing, 'ctx', split_axis=1, concat_axis=1, tiled=True)  8.26 us
    all_to_all x1, waiting for transfers between devices, local(): lax.all_to_all(queries, 'head', split_axis=1, concat_axis=0, tiled=True)  5.93 us
    all_to_all x1, starting transfers between devices, local(): lax.all_to_all(outgoing, 'ctx', split_axis=1, concat_axis=1, tiled=True)  5.41 us
    all_to_all x1, starting transfers between devices, local(): lax.all_to_all(span_key_value, 'head', split_axis=1, concat_axis=0, tiled...  4.21 us
    all_to_all x1, starting transfers between devices, local(): lax.all_to_all(queries, 'head', split_axis=1, concat_axis=0, tiled=True)  3.41 us
    all_to_all x1, local copies, waits for them, and re-layouts, local(): lax.all_to_all(span_key_value, 'head', split_axis=1, concat_axis=0, tiled...  1.55 us
    unnamed x9, local copies, waits for them, and re-layouts  1.49 us
  transfers between devices with their start and end apart: 3, of which 2 were waited for; matrix products, arithmetic and copies ran while one was open for 9% of the time, Pallas kernels for 0%

commit v1 on v0

v1 whole, which is shorter than its diff:
```python
import functools
import math

import jax
import jax.numpy as jnp
from jax import lax
from jax.experimental import pallas as pl
from jax.experimental.pallas import tpu as pltpu
from jax.sharding import PartitionSpec as P

LOG2E = 1.4426950408889634
MAX_DIRECT = 4
ANY = pl.BlockSpec(memory_space=pl.ANY)
SMEM = pl.BlockSpec(memory_space=pltpu.SMEM)
VMEM = pl.BlockSpec(memory_space=pltpu.VMEM)


def wanted_index(pattern_ref, counts_ref, row, owner, shard_blocks):
    def one(i, found):
        entry = pattern_ref[row, i]
        match = (i < counts_ref[row]) & (entry // shard_blocks == owner)
        return jnp.where(match, entry % shard_blocks, found)

    width = pattern_ref.shape[1]
    if width <= 4:
        found = jnp.int32(0)
        for i in range(width):
            found = one(i, found)
        return found
    return lax.fori_loop(0, width, one, jnp.int32(0))


def pick_kernel(n_ctx, block, pattern_ref, counts_ref, cache_ref, *refs):
    outs, sem = refs[:n_ctx], refs[n_ctx]
    me = lax.axis_index("ctx")
    shard_blocks = cache_ref.shape[1] // block
    copies = []
    for k in list(range(1, n_ctx)) + [0]:
        row = lax.rem(me + k, n_ctx)
        index = wanted_index(pattern_ref, counts_ref, row, me, shard_blocks)
        start = pl.multiple_of(index * block, block)
        copy = pltpu.make_async_copy(cache_ref.at[0, pl.ds(start, block), :], outs[k], sem.at[k])
        copy.start()
        copies.append(copy)
    for copy in copies:
        copy.wait()


def split_kernel(n_head, q_ref, kv_ref, *refs):
    outs, sem = refs[:n_head], refs[n_head]
    h = lax.axis_index("head")
    q_cols, kv_cols = q_ref.shape[1] // n_head, kv_ref.shape[1] // n_head
    copies = []
    for m in range(n_head):
        peer = lax.bitwise_xor(h, m)
        for ref, cols, at, s in ((q_ref, q_cols, 0, 0), (kv_ref, kv_cols, q_cols, 1)):
            copy = pltpu.make_async_copy(
                ref.at[:, pl.ds(pl.multiple_of(peer * cols, cols), cols)],
                outs[m].at[:, pl.ds(at, cols)],
                sem.at[m, s],
            )
            copy.start()
            copies.append(copy)
    for copy in copies:
        copy.wait()


def attend_kernel(n_ctx, n_head, d, shard_blocks, pattern_ref, counts_ref, *refs):
    blocks, pieces, outs = refs[:n_ctx], refs[n_ctx : n_ctx + n_head], refs[n_ctx + n_head :]
    me, h = lax.axis_index("ctx"), lax.axis_index("head")
    rows = pieces[0].shape[0]
    q_cols = pieces[0].shape[1] - 2 * d
    group = q_cols // d
    width = pattern_ref.shape[1]
    block = blocks[0].shape[0]
    keys, values, slot_bias = [], [], []
    for i in range(width):
        offset = lax.rem(me - pattern_ref[me, i] // shard_blocks + n_ctx, n_ctx)
        kv = blocks[0][...]
        for k in range(1, n_ctx):
            kv = jnp.where(offset == k, blocks[k][...], kv)
        keys.append(kv[:, :d])
        values.append(kv[:, d:])
        slot_bias.append(jnp.where(i < counts_ref[me], 0.0, -jnp.inf).astype(jnp.float32))
    for m in range(n_head):
        keys.append(pieces[m][:, q_cols : q_cols + d])
        values.append(pieces[m][:, q_cols + d :])
    keys, values = jnp.concatenate(keys, axis=0), jnp.concatenate(values, axis=0)
    span = n_head * rows
    column = lax.broadcasted_iota(jnp.int32, (rows, span), 1)
    row = lax.broadcasted_iota(jnp.int32, (rows, span), 0)
    key_token = lax.bitwise_xor(column // rows, h) * rows + column % rows
    rate = LOG2E / math.sqrt(d)
    for m in range(n_head):
        q = jnp.concatenate([pieces[m][:, j * d : (j + 1) * d] for j in range(group)], axis=0)
        s = lax.dot_general(q, keys, (((1,), (1,)), ((), ())), preferred_element_type=jnp.float32)
        causal = jnp.where(lax.bitwise_xor(h, m) * rows + row >= key_token, 0.0, -jnp.inf)
        own = s[:, width * block :].reshape(group, rows, span) + causal[None]
        parts = [s[:, i * block : (i + 1) * block] + slot_bias[i] for i in range(width)]
        s = jnp.concatenate(parts + [own.reshape(group * rows, span)], axis=1)
        top = jnp.max(s, axis=1, keepdims=True)
        p = jnp.exp2((s - top) * rate)
        denom = jnp.sum(p, axis=1, keepdims=True)
        o = lax.dot_general(
            p.astype(jnp.bfloat16), values, (((1,), (0,)), ((), ())), preferred_element_type=jnp.float32
        )
        o = (o / denom).astype(jnp.bfloat16)
        for j in range(group):
            outs[m][:, j * d : (j + 1) * d] = o[j * rows : (j + 1) * rows]


def join_kernel(n_head, *refs):
    pieces, out, sem = refs[:n_head], refs[n_head], refs[n_head + 1]
    h = lax.axis_index("head")
    cols = pieces[0].shape[1]
    copies = []
    for m in range(n_head):
        start = pl.multiple_of(lax.bitwise_xor(h, m) * cols, cols)
        copy = pltpu.make_async_copy(pieces[m], out.at[:, pl.ds(start, cols)], sem.at[m])
        copy.start()
        copies.append(copy)
    for copy in copies:
        copy.wait()


def direct(n_ctx, n_head, queries, span_key_value, cache, pattern, counts):
    rows, d = queries.shape[0], cache.shape[2] // 2
    block = rows * n_head
    shard_blocks = cache.shape[1] // block
    q_cols, kv_cols = queries.shape[1] // n_head, span_key_value.shape[1] // n_head
    bf16 = jnp.bfloat16
    around = [[(i, (i + k) % n_ctx) for i in range(n_ctx)] for k in range(n_ctx)]
    across = [[(i, i ^ m) for i in range(n_head)] for m in range(n_head)]

    blocks = pl.pallas_call(
        functools.partial(pick_kernel, n_ctx, block),
        out_shape=[jax.ShapeDtypeStruct((block, 2 * d), bf16)] * n_ctx,
        in_specs=[SMEM, SMEM, ANY],
        out_specs=[ANY] * n_ctx,
        scratch_shapes=[pltpu.SemaphoreType.DMA((n_ctx,))],
        name="pick",
    )(pattern, counts, cache)
    pieces = pl.pallas_call(
        functools.partial(split_kernel, n_head),
        out_shape=[jax.ShapeDtypeStruct((rows, q_cols + kv_cols), bf16)] * n_head,
        in_specs=[ANY, ANY],
        out_specs=[ANY] * n_head,
        scratch_shapes=[pltpu.SemaphoreType.DMA((n_head, 2))],
        name="split",
    )(queries, span_key_value)
    blocks, pieces = list(blocks), list(pieces)
    for k in range(1, n_ctx):
        blocks[k] = lax.ppermute(blocks[k], "ctx", around[k])
    for m in (2, 3, 1):
        pieces[m] = lax.ppermute(pieces[m], "head", across[m])
    outs = pl.pallas_call(
        functools.partial(attend_kernel, n_ctx, n_head, d, shard_blocks),
        out_shape=[jax.ShapeDtypeStruct((rows, q_cols), bf16)] * n_head,
        in_specs=[SMEM, SMEM] + [VMEM] * (n_ctx + n_head),
        out_specs=[VMEM] * n_head,
        name="attend",
    )(pattern, counts, *blocks, *pieces)
    outs = list(outs)
    for m in (2, 3, 1):
        outs[m] = lax.ppermute(outs[m], "head", across[m])
    return pl.pallas_call(
        functools.partial(join_kernel, n_head),
        out_shape=jax.ShapeDtypeStruct((rows, q_cols * n_head), bf16),
        in_specs=[ANY] * n_head,
        out_specs=ANY,
        scratch_shapes=[pltpu.SemaphoreType.DMA((n_head,))],
        name="join",
    )(*outs)


def collect_kernel(n_ctx, block, pattern_ref, counts_ref, cache_ref, out_ref, sem):
    me = lax.axis_index("ctx")
    shard_blocks = cache_ref.shape[1] // block

    @pl.loop(0, n_ctx)
    def _(row):
        index = wanted_index(pattern_ref, counts_ref, row, me, shard_blocks)
        start = pl.multiple_of(index * block, block)
        copy = pltpu.make_async_copy(cache_ref.at[0, pl.ds(start, block), :], out_ref.at[row], sem)
        copy.start()
        copy.wait()


def slots_kernel(shard_blocks, pattern_ref, in_ref, out_ref, sem):
    me = lax.axis_index("ctx")

    @pl.loop(0, pattern_ref.shape[1])
    def _(i):
        copy = pltpu.make_async_copy(in_ref.at[pattern_ref[me, i] // shard_blocks], out_ref.at[i], sem)
        copy.start()
        copy.wait()


def absorb(carried, q, kv, allowed, scale):
    running_max, denom, weighted = carried
    d = q.shape[-1]
    scores = jnp.einsum("tjd,kd->jtk", q, kv[:, :d], preferred_element_type=jnp.float32) * scale
    masked = jnp.where(allowed, scores, -jnp.inf)
    new_max = jnp.maximum(running_max, jnp.max(masked, axis=-1))
    factor = jnp.exp(running_max - new_max)
    weights = jnp.where(allowed, jnp.exp(scores - new_max[..., None]), 0.0)
    denom = denom * factor + jnp.sum(weights, axis=-1)
    weighted = weighted * factor[..., None] + jnp.einsum(
        "jtk,kd->jtd", weights.astype(jnp.bfloat16), kv[:, d:], preferred_element_type=jnp.float32
    )
    return new_max, denom, weighted


def general(n_ctx, n_head, queries, span_key_value, cache, pattern, counts):
    d = cache.shape[2] // 2
    block = queries.shape[0] * n_head
    shard_blocks = cache.shape[1] // block
    width = pattern.shape[1]
    q = lax.all_to_all(queries, "head", split_axis=1, concat_axis=0, tiled=True)
    kv = lax.all_to_all(span_key_value, "head", split_axis=1, concat_axis=0, tiled=True)
    outgoing = pl.pallas_call(
        functools.partial(collect_kernel, n_ctx, block),
        out_shape=jax.ShapeDtypeStruct((n_ctx, block, 2 * d), jnp.bfloat16),
        in_specs=[SMEM, SMEM, ANY],
        out_specs=ANY,
        scratch_shapes=[pltpu.SemaphoreType.DMA],
        name="collect",
    )(pattern, counts, cache)
    incoming = lax.all_to_all(outgoing, "ctx", split_axis=0, concat_axis=0, tiled=True)
    slots = pl.pallas_call(
        functools.partial(slots_kernel, shard_blocks),
        out_shape=jax.ShapeDtypeStruct((width, block, 2 * d), jnp.bfloat16),
        in_specs=[SMEM, ANY],
        out_specs=ANY,
        scratch_shapes=[pltpu.SemaphoreType.DMA],
        name="slots",
    )(pattern, incoming)
    count = lax.dynamic_index_in_dim(counts, lax.axis_index("ctx"), 0, keepdims=False)
    group = q.shape[1] // d
    q = q.reshape(block, group, d)
    scale = 1.0 / math.sqrt(d)
    carried = (
        jnp.full((group, block), -jnp.inf, jnp.float32),
        jnp.zeros((group, block), jnp.float32),
        jnp.zeros((group, block, d), jnp.float32),
    )
    causal = jnp.arange(block)[:, None] >= jnp.arange(block)[None, :]
    carried = absorb(carried, q, kv, causal, scale)
    batch = math.gcd(width, 4)

    def step(at, carried):
        some = lax.dynamic_slice_in_dim(slots, at * batch, batch, 0).reshape(batch * block, 2 * d)
        usable = at * batch + jnp.arange(batch * block) // block < count
        return absorb(carried, q, some, usable, scale)

    _, denom, weighted = lax.fori_loop(0, width // batch, step, carried)
    result = (weighted / denom[..., None]).transpose(1, 0, 2).reshape(block, group * d)
    return lax.all_to_all(result.astype(jnp.bfloat16), "head", split_axis=0, concat_axis=1, tiled=True)


def solution(mesh):
    n_ctx, n_head = mesh.shape["ctx"], mesh.shape["head"]
    form = direct if n_ctx <= MAX_DIRECT else general
    return jax.shard_map(
        functools.partial(form, n_ctx, n_head),
        mesh=mesh,
        in_specs=(
            P(("grp", "ctx", "head"), None),
            P(("grp", "ctx", "head"), None),
            P("head", ("grp", "ctx"), None),
            P("grp", None),
            P("grp"),
        ),
        out_specs=P(("grp", "ctx", "head"), None),
        check_vma=False,
    )
```

time: 46.6 us -> 54 us (1.16)
  Pallas kernels: 0 us -> 33.1 us
  blocking collectives: 8.42 us -> 0 us
  waiting for transfers between devices: 14.2 us -> 7.15 us
  local copies, waits for them, and re-layouts: 6.8 us -> 2.64 us
  starting transfers between devices: 13 us -> 10.9 us
  other arithmetic: 2.01 us -> 0 us
  matrix products: 1.46 us -> 0 us
    pallas_call x0 -> x4, Pallas kernels: none -> 33.1 us  [the longest x1 11.1 us: direct(): pl.pallas_call(functools.partial(split_kernel, n_head), out_shape=[jax.Sh...]
    all_to_all x3 -> x0, waiting for transfers between devices: 14.2 us -> none  [the longest x1 8.26 us: local(): lax.all_to_all(outgoing, 'ctx', split_axis=1, concat_axis=1, tiled=True)]
    all_to_all x3 -> x0, starting transfers between devices: 13 us -> none  [the longest x1 5.41 us: local(): lax.all_to_all(outgoing, 'ctx', split_axis=1, concat_axis=1, tiled=True)]
    ppermute x0 -> x9, starting transfers between devices: none -> 10.9 us  [the longest x3 7.06 us: direct(): blocks[k] = lax.ppermute(blocks[k], 'ctx', around[k])]
    all_to_all x1 -> x0, blocking collectives: 8.42 us -> none  [local(): lax.all_to_all(result, 'head', split_axis=0, concat_axis=1, tiled=True)]
    ppermute x0 -> x9, waiting for transfers between devices: none -> 7.15 us  [the longest x3 3.93 us: direct(): outs[m] = lax.ppermute(outs[m], 'head', across[m])]
    all_to_all x3 -> x0, local copies, waits for them, and re-layouts: 2.99 us -> none  [the longest x1 1.55 us: local(): lax.all_to_all(span_key_value, 'head', split_axis=1, concat_axis=0, tiled...]
    dot_general x4 -> x0, matrix products: 1.46 us -> none  [the longest x2 0.92 us: absorb(): jnp.einsum('gjtk,gkd->gjtd', weights.astype(jnp.bfloat16), values, prefer...]
  transfers between devices with their start and end apart: 3 -> 9, of which waited for: 2 -> 4; matrix products, arithmetic and copies ran while one was open for 9% -> 0% of each run, Pallas kernels for 0% -> 21%
where the time goes in v1:
time: 54 us; the launch traced here: 53.9 us
  Pallas kernels  33.1 us (61%)
  starting transfers between devices  10.9 us (20%)
  waiting for transfers between devices  7.15 us (13%)
  local copies, waits for them, and re-layouts  2.64 us (5%)
    pallas_call x1, Pallas kernels, direct(): pl.pallas_call(functools.partial(split_kernel, n_head), out_shape=[jax.Sh...  11.1 us
    pallas_call x1, Pallas kernels, direct(): pl.pallas_call(functools.partial(pick_kernel, n_ctx, block), out_shape=[j...  9.8 us
    pallas_call x1, Pallas kernels, direct(): pl.pallas_call(functools.partial(join_kernel, n_head), out_shape=jax.Shap...  9.08 us
    ppermute x3, starting transfers between devices, direct(): blocks[k] = lax.ppermute(blocks[k], 'ctx', around[k])  7.06 us
    ppermute x3, waiting for transfers between devices, direct(): outs[m] = lax.ppermute(outs[m], 'head', across[m])  3.93 us
    ppermute x3, waiting for transfers between devices, direct(): blocks[k] = lax.ppermute(blocks[k], 'ctx', around[k])  3.22 us
    pallas_call x1, Pallas kernels, direct(): pl.pallas_call(functools.partial(attend_kernel, n_ctx, n_head, d, shard_b...  3.13 us
    unnamed x23, local copies, waits for them, and re-layouts  2.64 us
  transfers between devices with their start and end apart: 9, of which 4 were waited for; matrix products, arithmetic and copies ran while one was open for 0% of the time, Pallas kernels for 21%

profile of v1, /device:TPU:0, one launch (start us, length us, event | category | flops | bytes accessed | tf_op | source)
XLA Modules:
  0.0 53.9 jit_solution(11753184879895090633)
XLA Ops:
  0.0 1.3 %copy.7.pattern_ref = s32[4,2]{1,0:T(4,128)} copy(s32[4,2]{0,1:T(2,128)} %param.8) | data formatting | bytes 64 | tf_op args[3]
  1.3 9.8 %pick.1 = (bf16[128,256]{1,0:T(8,128)(2,1)}, bf16[128,256]{1,0:T(8,128)(2,1)}, bf16[128,256]{1,0:T(8,128)(2,1)}, bf16[128,256]{1,0:T(8,128)(2,1)}) custom-call(s32[4,2]{1,0:T(4,128)} %copy.7.pattern_ref, s32[4]{0:T(128)} %counts_ref.3, bf16[1,2048,256]{2,1,0:T(8,128)(2,1)} %cache_ref.1), custom_call_target="tpu_custom_call" | custom-call | tf_op jit(solution)/shard_map/pick/pallas_call | solution.py:135
  11.2 3.1 %collective-permute-start = (bf16[128,256]{1,0:T(8,128)(2,1)}, bf16[128,256]{1,0:T(8,128)(2,1)S(1)}, u32[]{:S(2)}, u32[]{:S(2)}) collective-permute-start(bf16[128,256]{1,0:T(8,128)(2,1)} %get-tuple-element.18), channel_id=1, source_target_pairs={{0,4},{4,8},{8,12},{12,0},{1,5},{5,9},{9,13},{13,1},{2,6},{6,10},{... | collective-permute-start | bytes 196616 | tf_op jit(solution)/shard_map/ppermute | solution.py:153
  14.2 11.1 %split.1 = (bf16[32,1280]{1,0:T(8,128)(2,1)}, bf16[32,1280]{1,0:T(8,128)(2,1)}, bf16[32,1280]{1,0:T(8,128)(2,1)}, bf16[32,1280]{1,0:T(8,128)(2,1)}) custom-call(bf16[32,4096]{1,0:T(8,128)(2,1)} %q_ref.1, bf16[32,1024]{1,0:T(8,128)(2,1)} %kv_ref.1), custom_call_target="tpu_custom_call" | custom-call | tf_op jit(solution)/shard_map/split/pallas_call | solution.py:143
  25.3 0.1 collective-permute-start.3
  25.4 1.6 %collective-permute-start.4 = (bf16[32,1280]{1,0:T(8,128)(2,1)}, bf16[32,1280]{1,0:T(8,128)(2,1)S(1)}, u32[]{:S(2)}, u32[]{:S(2)}) collective-permute-start(bf16[32,1280]{1,0:T(8,128)(2,1)} %get-tuple-element.23), channel_id=1, source_target_pairs={{0,2},{1,3},{2,0},{3,1},{4,6},{5,7},{6,4},{7,5},{8,10},{9,11},{10,... | collective-permute-start | bytes 245768 | tf_op jit(solution)/shard_map/ppermute | solution.py:155
  27.0 0.3 collective-permute-start.5
  27.3 2.6 %collective-permute-start.1 = (bf16[128,256]{1,0:T(8,128)(2,1)S(1)}, bf16[128,256]{1,0:T(8,128)(2,1)S(1)}, u32[]{:S(2)}, u32[]{:S(2)}) collective-permute-start(bf16[128,256]{1,0:T(8,128)(2,1)S(1)} %copy-done.10), channel_id=1, source_target_pairs={{0,8},{4,12},{8,0},{12,4},{1,9},{5,13},{9,1},{13,5},{2,10},{6,14},... | collective-permute-start | bytes 196616 | tf_op jit(solution)/shard_map/ppermute | solution.py:153
  29.9 0.0 collective-permute-done.refs_1_
  29.9 1.4 %collective-permute-start.2 = (bf16[128,256]{1,0:T(8,128)(2,1)S(1)}, bf16[128,256]{1,0:T(8,128)(2,1)S(1)}, u32[]{:S(2)}, u32[]{:S(2)}) collective-permute-start(bf16[128,256]{1,0:T(8,128)(2,1)S(1)} %copy-done.9), channel_id=1, source_target_pairs={{0,12},{4,0},{8,4},{12,8},{1,13},{5,1},{9,5},{13,9},{2,14},{6,2},{... | collective-permute-start | bytes 196616 | tf_op jit(solution)/shard_map/ppermute | solution.py:153
  31.3 3.1 %collective-permute-done.1.refs_2_ = bf16[128,256]{1,0:T(8,128)(2,1)S(1)} collective-permute-done((bf16[128,256]{1,0:T(8,128)(2,1)S(1)}, bf16[128,256]{1,0:T(8,128)(2,1)S(1)}, u32[]{:S(2)}, u32[]{:S(2)}) %collective-permute-start.1) | collective-permute-done | bytes 65568 | tf_op jit(solution)/shard_map/ppermute | solution.py:153
  34.4 0.1 collective-permute-done.2.refs_3_
  34.6 0.5 copy-done.4
  35.0 0.1 copy-done.5
  35.1 0.0 copy-done
  35.1 0.0 copy-done.1
  35.2 0.0 copy-done.2
  35.2 3.1 %attend.1 = (bf16[32,1024]{1,0:T(8,128)(2,1)}, bf16[32,1024]{1,0:T(8,128)(2,1)}, bf16[32,1024]{1,0:T(8,128)(2,1)}, bf16[32,1024]{1,0:T(8,128)(2,1)}) custom-call(s32[4,2]{1,0:T(4,128)} %copy.7.pattern_ref, s32[4]{0:T(128)} %counts_ref.3, bf16[128,256]{1,0:T(8,128)(2,1)} %get-tuple-element.17.refs_0_, bf16[128,256]{1,0:T(8,128)(2,1)} %copy-done.3, ...), custom_call_target="tpu_custom_call" | custom-call | tf_op jit(solution)/shard_map/attend/pallas_call | solution.py:156
  38.4 1.5 %collective-permute-start.7 = (bf16[32,1024]{1,0:T(8,128)(2,1)}, bf16[32,1024]{1,0:T(8,128)(2,1)S(1)}, u32[]{:S(2)}, u32[]{:S(2)}) collective-permute-start(bf16[32,1024]{1,0:T(8,128)(2,1)} %get-tuple-element.27), channel_id=1, source_target_pairs={{0,2},{1,3},{2,0},{3,1},{4,6},{5,7},{6,4},{7,5},{8,10},{9,11},{10,... | collective-permute-start | bytes 196616 | tf_op jit(solution)/shard_map/ppermute | solution.py:165
  39.9 0.4 collective-permute-start.8
  40.2 2.9 %collective-permute-done.7.refs_2_ = bf16[32,1024]{1,0:T(8,128)(2,1)S(1)} collective-permute-done((bf16[32,1024]{1,0:T(8,128)(2,1)}, bf16[32,1024]{1,0:T(8,128)(2,1)S(1)}, u32[]{:S(2)}, u32[]{:S(2)}) %collective-permute-start.7) | collective-permute-done | bytes 65568 | tf_op jit(solution)/shard_map/ppermute | solution.py:165
  43.1 1.0 %collective-permute-done.8.refs_3_ = bf16[32,1024]{1,0:T(8,128)(2,1)S(1)} collective-permute-done((bf16[32,1024]{1,0:T(8,128)(2,1)}, bf16[32,1024]{1,0:T(8,128)(2,1)S(1)}, u32[]{:S(2)}, u32[]{:S(2)}) %collective-permute-start.8) | collective-permute-done | bytes 65568 | tf_op jit(solution)/shard_map/ppermute | solution.py:165
  44.2 0.6 %copy-done.8 = bf16[32,1024]{1,0:T(8,128)(2,1)} copy-done((bf16[32,1024]{1,0:T(8,128)(2,1)}, bf16[32,1024]{1,0:T(8,128)(2,1)S(1)}, u32[]{:S(2)}) %copy-start.8) | copy-done | bytes 65560
  44.8 9.1 %join.1 = bf16[32,4096]{1,0:T(8,128)(2,1)} custom-call(bf16[32,1024]{1,0:T(8,128)(2,1)} %get-tuple-element.25.refs_0_, bf16[32,1024]{1,0:T(8,128)(2,1)} %copy-done.6, bf16[32,1024]{1,0:T(8,128)(2,1)} %copy-done.7, bf16[32,1024]{1,0:T(8,128)(2,1)} %copy-done.8), custom_call_target="tpu_custom_call" | custom-call | tf_op jit(solution)/shard_map/join/pallas_call | solution.py:166
  (21 shorter events, 0.0 us)
Async XLA Ops:
  11.1 16.1 %copy-start.10 = (bf16[128,256]{1,0:T(8,128)(2,1)S(1)}, bf16[128,256]{1,0:T(8,128)(2,1)}, u32[]{:S(2)}) copy-start(bf16[128,256]{1,0:T(8,128)(2,1)} %get-tuple-element.19) | copy-start | bytes 196612
  11.2 18.7 %copy-start.9 = (bf16[128,256]{1,0:T(8,128)(2,1)S(1)}, bf16[128,256]{1,0:T(8,128)(2,1)}, u32[]{:S(2)}) copy-start(bf16[128,256]{1,0:T(8,128)(2,1)} %get-tuple-element.20) | copy-start | bytes 196612
  11.2 18.7 %collective-permute-start = (bf16[128,256]{1,0:T(8,128)(2,1)}, bf16[128,256]{1,0:T(8,128)(2,1)S(1)}, u32[]{:S(2)}, u32[]{:S(2)}) collective-permute-start(bf16[128,256]{1,0:T(8,128)(2,1)} %get-tuple-element.18), channel_id=1, source_target_pairs={{0,4},{4,8},{8,12},{12,0},{1,5},{5,9},{9,13},{13,1},{2,6},{6,10},{... | collective-permute-start | bytes 196616 | tf_op jit(solution)/shard_map/ppermute | solution.py:153
  25.3 9.2 %collective-permute-start.3 = (bf16[32,1280]{1,0:T(8,128)(2,1)}, bf16[32,1280]{1,0:T(8,128)(2,1)S(1)}, u32[]{:S(2)}, u32[]{:S(2)}) collective-permute-start(bf16[32,1280]{1,0:T(8,128)(2,1)} %get-tuple-element.22), channel_id=1, source_target_pairs={{0,1},{1,0},{2,3},{3,2},{4,5},{5,4},{6,7},{7,6},{8,9},{9,8},{10,11... | collective-permute-start | bytes 245768 | tf_op jit(solution)/shard_map/ppermute | solution.py:155
  25.4 9.1 %collective-permute-start.4 = (bf16[32,1280]{1,0:T(8,128)(2,1)}, bf16[32,1280]{1,0:T(8,128)(2,1)S(1)}, u32[]{:S(2)}, u32[]{:S(2)}) collective-permute-start(bf16[32,1280]{1,0:T(8,128)(2,1)} %get-tuple-element.23), channel_id=1, source_target_pairs={{0,2},{1,3},{2,0},{3,1},{4,6},{5,7},{6,4},{7,5},{8,10},{9,11},{10,... | collective-permute-start | bytes 245768 | tf_op jit(solution)/shard_map/ppermute | solution.py:155
  27.0 7.5 %collective-permute-start.5 = (bf16[32,1280]{1,0:T(8,128)(2,1)}, bf16[32,1280]{1,0:T(8,128)(2,1)S(1)}, u32[]{:S(2)}, u32[]{:S(2)}) collective-permute-start(bf16[32,1280]{1,0:T(8,128)(2,1)} %get-tuple-element.24), channel_id=1, source_target_pairs={{0,3},{1,2},{2,1},{3,0},{4,7},{5,6},{6,5},{7,4},{8,11},{9,10},{10,... | collective-permute-start | bytes 245768 | tf_op jit(solution)/shard_map/ppermute | solution.py:155
  27.3 7.1 %collective-permute-start.1 = (bf16[128,256]{1,0:T(8,128)(2,1)S(1)}, bf16[128,256]{1,0:T(8,128)(2,1)S(1)}, u32[]{:S(2)}, u32[]{:S(2)}) collective-permute-start(bf16[128,256]{1,0:T(8,128)(2,1)S(1)} %copy-done.10), channel_id=1, source_target_pairs={{0,8},{4,12},{8,0},{12,4},{1,9},{5,13},{9,1},{13,5},{2,10},{6,14},... | collective-permute-start | bytes 196616 | tf_op jit(solution)/shard_map/ppermute | solution.py:153
  29.9 4.7 %copy-start.3 = (bf16[128,256]{1,0:T(8,128)(2,1)}, bf16[128,256]{1,0:T(8,128)(2,1)S(1)}, u32[]{:S(2)}) copy-start(bf16[128,256]{1,0:T(8,128)(2,1)S(1)} %collective-permute-done.refs_1_) | copy-start | bytes 196612
  29.9 4.6 %collective-permute-start.2 = (bf16[128,256]{1,0:T(8,128)(2,1)S(1)}, bf16[128,256]{1,0:T(8,128)(2,1)S(1)}, u32[]{:S(2)}, u32[]{:S(2)}) collective-permute-start(bf16[128,256]{1,0:T(8,128)(2,1)S(1)} %copy-done.9), channel_id=1, source_target_pairs={{0,12},{4,0},{8,4},{12,8},{1,13},{5,1},{9,5},{13,9},{2,14},{6,2},{... | collective-permute-start | bytes 196616 | tf_op jit(solution)/shard_map/ppermute | solution.py:153
  34.4 0.6 %copy-start.4 = (bf16[128,256]{1,0:T(8,128)(2,1)}, bf16[128,256]{1,0:T(8,128)(2,1)S(1)}, u32[]{:S(2)}) copy-start(bf16[128,256]{1,0:T(8,128)(2,1)S(1)} %collective-permute-done.1.refs_2_) | copy-start | bytes 196612
  34.5 0.6 %copy-start.5 = (bf16[128,256]{1,0:T(8,128)(2,1)}, bf16[128,256]{1,0:T(8,128)(2,1)S(1)}, u32[]{:S(2)}) copy-start(bf16[128,256]{1,0:T(8,128)(2,1)S(1)} %collective-permute-done.2.refs_3_) | copy-start | bytes 196612
  34.5 0.6 %copy-start = (bf16[32,1280]{1,0:T(8,128)(2,1)}, bf16[32,1280]{1,0:T(8,128)(2,1)S(1)}, u32[]{:S(2)}) copy-start(bf16[32,1280]{1,0:T(8,128)(2,1)S(1)} %collective-permute-done.3.refs_5_) | copy-start | bytes 245764
  34.5 0.7 %copy-start.1 = (bf16[32,1280]{1,0:T(8,128)(2,1)}, bf16[32,1280]{1,0:T(8,128)(2,1)S(1)}, u32[]{:S(2)}) copy-start(bf16[32,1280]{1,0:T(8,128)(2,1)S(1)} %collective-permute-done.4.refs_6_) | copy-start | bytes 245764
  34.5 0.7 %copy-start.2 = (bf16[32,1280]{1,0:T(8,128)(2,1)}, bf16[32,1280]{1,0:T(8,128)(2,1)S(1)}, u32[]{:S(2)}) copy-start(bf16[32,1280]{1,0:T(8,128)(2,1)S(1)} %collective-permute-done.5.refs_7_) | copy-start | bytes 245764
  38.4 1.9 %collective-permute-start.6 = (bf16[32,1024]{1,0:T(8,128)(2,1)}, bf16[32,1024]{1,0:T(8,128)(2,1)S(1)}, u32[]{:S(2)}, u32[]{:S(2)}) collective-permute-start(bf16[32,1024]{1,0:T(8,128)(2,1)} %get-tuple-element.26), channel_id=1, source_target_pairs={{0,1},{1,0},{2,3},{3,2},{4,5},{5,4},{6,7},{7,6},{8,9},{9,8},{10,11... | collective-permute-start | bytes 196616 | tf_op jit(solution)/shard_map/ppermute | solution.py:165
  38.4 4.8 %collective-permute-start.7 = (bf16[32,1024]{1,0:T(8,128)(2,1)}, bf16[32,1024]{1,0:T(8,128)(2,1)S(1)}, u32[]{:S(2)}, u32[]{:S(2)}) collective-permute-start(bf16[32,1024]{1,0:T(8,128)(2,1)} %get-tuple-element.27), channel_id=1, source_target_pairs={{0,2},{1,3},{2,0},{3,1},{4,6},{5,7},{6,4},{7,5},{8,10},{9,11},{10,... | collective-permute-start | bytes 196616 | tf_op jit(solution)/shard_map/ppermute | solution.py:165
  39.9 4.3 %collective-permute-start.8 = (bf16[32,1024]{1,0:T(8,128)(2,1)}, bf16[32,1024]{1,0:T(8,128)(2,1)S(1)}, u32[]{:S(2)}, u32[]{:S(2)}) collective-permute-start(bf16[32,1024]{1,0:T(8,128)(2,1)} %get-tuple-element.28), channel_id=1, source_target_pairs={{0,3},{1,2},{2,1},{3,0},{4,7},{5,6},{6,5},{7,4},{8,11},{9,10},{10,... | collective-permute-start | bytes 196616 | tf_op jit(solution)/shard_map/ppermute | solution.py:165
  40.2 3.9 %copy-start.6 = (bf16[32,1024]{1,0:T(8,128)(2,1)}, bf16[32,1024]{1,0:T(8,128)(2,1)S(1)}, u32[]{:S(2)}) copy-start(bf16[32,1024]{1,0:T(8,128)(2,1)S(1)} %collective-permute-done.6.refs_1_) | copy-start | bytes 196612
  43.1 1.0 %copy-start.7 = (bf16[32,1024]{1,0:T(8,128)(2,1)}, bf16[32,1024]{1,0:T(8,128)(2,1)S(1)}, u32[]{:S(2)}) copy-start(bf16[32,1024]{1,0:T(8,128)(2,1)S(1)} %collective-permute-done.7.refs_2_) | copy-start | bytes 196612
  44.2 0.6 %copy-start.8 = (bf16[32,1024]{1,0:T(8,128)(2,1)}, bf16[32,1024]{1,0:T(8,128)(2,1)S(1)}, u32[]{:S(2)}) copy-start(bf16[32,1024]{1,0:T(8,128)(2,1)S(1)} %collective-permute-done.8.refs_3_) | copy-start | bytes 196612

commit v2 on v1

--- a/solution.py
+++ b/solution.py
@@ -15,13 +15,17 @@
 VMEM = pl.BlockSpec(memory_space=pltpu.VMEM)
 
 
+def vmem(x):
+    return pltpu.with_memory_space_constraint(x, pltpu.VMEM)
+
+
 def wanted_index(pattern_ref, counts_ref, row, owner, shard_blocks):
     def one(i, found):
-        entry = pattern_ref[row, i]
+        entry = pattern_ref[i, row]
         match = (i < counts_ref[row]) & (entry // shard_blocks == owner)
         return jnp.where(match, entry % shard_blocks, found)
 
-    width = pattern_ref.shape[1]
+    width = pattern_ref.shape[0]
     if width <= 4:
         found = jnp.int32(0)
         for i in range(width):
@@ -71,11 +75,11 @@
     rows = pieces[0].shape[0]
     q_cols = pieces[0].shape[1] - 2 * d
     group = q_cols // d
-    width = pattern_ref.shape[1]
+    width = pattern_ref.shape[0]
     block = blocks[0].shape[0]
     keys, values, slot_bias = [], [], []
     for i in range(width):
-        offset = lax.rem(me - pattern_ref[me, i] // shard_blocks + n_ctx, n_ctx)
+        offset = lax.rem(me - pattern_ref[i, me] // shard_blocks + n_ctx, n_ctx)
         kv = blocks[0][...]
         for k in range(1, n_ctx):
             kv = jnp.where(offset == k, blocks[k][...], kv)
@@ -134,17 +138,17 @@
 
     blocks = pl.pallas_call(
         functools.partial(pick_kernel, n_ctx, block),
-        out_shape=[jax.ShapeDtypeStruct((block, 2 * d), bf16)] * n_ctx,
+        out_shape=[pltpu.VMEM((block, 2 * d), bf16)] * n_ctx,
         in_specs=[SMEM, SMEM, ANY],
-        out_specs=[ANY] * n_ctx,
+        out_specs=[VMEM] * n_ctx,
         scratch_shapes=[pltpu.SemaphoreType.DMA((n_ctx,))],
         name="pick",
-    )(pattern, counts, cache)
+    )(pattern.T, counts, cache)
     pieces = pl.pallas_call(
         functools.partial(split_kernel, n_head),
-        out_shape=[jax.ShapeDtypeStruct((rows, q_cols + kv_cols), bf16)] * n_head,
+        out_shape=[pltpu.VMEM((rows, q_cols + kv_cols), bf16)] * n_head,
         in_specs=[ANY, ANY],
-        out_specs=[ANY] * n_head,
+        out_specs=[VMEM] * n_head,
         scratch_shapes=[pltpu.SemaphoreType.DMA((n_head, 2))],
         name="split",
     )(queries, span_key_value)
@@ -155,22 +159,22 @@
         pieces[m] = lax.ppermute(pieces[m], "head", across[m])
     outs = pl.pallas_call(
         functools.partial(attend_kernel, n_ctx, n_head, d, shard_blocks),
-        out_shape=[jax.ShapeDtypeStruct((rows, q_cols), bf16)] * n_head,
+        out_shape=[pltpu.VMEM((rows, q_cols), bf16)] * n_head,
         in_specs=[SMEM, SMEM] + [VMEM] * (n_ctx + n_head),
         out_specs=[VMEM] * n_head,
         name="attend",
-    )(pattern, counts, *blocks, *pieces)
+    )(pattern.T, counts, *map(vmem, blocks + pieces))
     outs = list(outs)
     for m in (2, 3, 1):
         outs[m] = lax.ppermute(outs[m], "head", across[m])
     return pl.pallas_call(
         functools.partial(join_kernel, n_head),
         out_shape=jax.ShapeDtypeStruct((rows, q_cols * n_head), bf16),
-        in_specs=[ANY] * n_head,
+        in_specs=[VMEM] * n_head,
         out_specs=ANY,
         scratch_shapes=[pltpu.SemaphoreType.DMA((n_head,))],
         name="join",
-    )(*outs)
+    )(*map(vmem, outs))
 
 
 def collect_kernel(n_ctx, block, pattern_ref, counts_ref, cache_ref, out_ref, sem):
@@ -189,9 +193,9 @@
 def slots_kernel(shard_blocks, pattern_ref, in_ref, out_ref, sem):
     me = lax.axis_index("ctx")
 
-    @pl.loop(0, pattern_ref.shape[1])
+    @pl.loop(0, pattern_ref.shape[0])
     def _(i):
-        copy = pltpu.make_async_copy(in_ref.at[pattern_ref[me, i] // shard_blocks], out_ref.at[i], sem)
+        copy = pltpu.make_async_copy(in_ref.at[pattern_ref[i, me] // shard_blocks], out_ref.at[i], sem)
         copy.start()
         copy.wait()
 
@@ -225,7 +229,7 @@
         out_specs=ANY,
         scratch_shapes=[pltpu.SemaphoreType.DMA],
         name="collect",
-    )(pattern, counts, cache)
+    )(pattern.T, counts, cache)
     incoming = lax.all_to_all(outgoing, "ctx", split_axis=0, concat_axis=0, tiled=True)
     slots = pl.pallas_call(
         functools.partial(slots_kernel, shard_blocks),
@@ -234,7 +238,7 @@
         out_specs=ANY,
         scratch_shapes=[pltpu.SemaphoreType.DMA],
         name="slots",
-    )(pattern, incoming)
+    )(pattern.T, incoming)
     count = lax.dynamic_index_in_dim(counts, lax.axis_index("ctx"), 0, keepdims=False)
     group = q.shape[1] // d
     q = q.reshape(block, group, d)

time: 54 us -> 23.8 us (0.44)
  Pallas kernels: 33.1 us -> 5.57 us
  local copies, waits for them, and re-layouts: 2.64 us -> 0 us
    pallas_call x2, Pallas kernels: 20.9 us -> 2.8 us  [the longest x1 1.75 us: direct(): pl.pallas_call(functools.partial(pick_kernel, n_ctx, block), out_shape=[p...]
    pallas_call x1, Pallas kernels: 9.08 us -> 0.73 us  [direct(): pl.pallas_call(functools.partial(join_kernel, n_head), out_shape=jax.Shap...]
    unnamed x23 -> x0, local copies, waits for them, and re-layouts: 2.64 us -> none
    pallas_call x1, Pallas kernels: 3.13 us -> 2.04 us  [direct(): pl.pallas_call(functools.partial(attend_kernel, n_ctx, n_head, d, shard_b...]
  transfers between devices with their start and end apart: 9 -> 9, of which waited for: 4 -> 3; matrix products, arithmetic and copies ran while one was open for 0% -> 0% of each run, Pallas kernels for 21% -> 4%
where the time goes in v2:
time: 23.8 us; the launch traced here: 23.5 us
  starting transfers between devices  10.9 us (46%)
  waiting for transfers between devices  6.98 us (29%)
  Pallas kernels  5.57 us (23%)
    ppermute x3, starting transfers between devices, direct(): blocks[k] = lax.ppermute(blocks[k], 'ctx', around[k])  7 us
    ppermute x3, waiting for transfers between devices, direct(): outs[m] = lax.ppermute(outs[m], 'head', across[m])  3.75 us
    ppermute x3, waiting for transfers between devices, direct(): blocks[k] = lax.ppermute(blocks[k], 'ctx', around[k])  3.22 us
    pallas_call x1, Pallas kernels, direct(): pl.pallas_call(functools.partial(attend_kernel, n_ctx, n_head, d, shard_b...  2.04 us
    ppermute x3, starting transfers between devices, direct(): pieces[m] = lax.ppermute(pieces[m], 'head', across[m])  1.93 us
    ppermute x3, starting transfers between devices, direct(): outs[m] = lax.ppermute(outs[m], 'head', across[m])  1.93 us
    pallas_call x1, Pallas kernels, direct(): pl.pallas_call(functools.partial(pick_kernel, n_ctx, block), out_shape=[p...  1.75 us
    pallas_call x1, Pallas kernels, direct(): pl.pallas_call(functools.partial(split_kernel, n_head), out_shape=[pltpu....  1.06 us
  transfers between devices with their start and end apart: 9, of which 3 were waited for; matrix products, arithmetic and copies ran while one was open for 0% of the time, Pallas kernels for 4%

profile of v2, /device:TPU:0, one launch (start us, length us, event | category | flops | bytes accessed | tf_op | source)
XLA Modules:
  0.0 23.5 jit_solution(1459515669879666224)
XLA Ops:
  0.0 1.7 %pick.1 = (bf16[128,256]{1,0:T(8,128)(2,1)S(1)}, bf16[128,256]{1,0:T(8,128)(2,1)S(1)}, bf16[128,256]{1,0:T(8,128)(2,1)S(1)}, bf16[128,256]{1,0:T(8,128)(2,1)S(1)}) custom-call(s32[2,4]{1,0:T(2,128)} %bitcast.1, s32[4]{0:T(128)} %counts_ref.3, bf16[1,2048,256]{2,1,0:T(8,128)(2,1)} %cache_ref.1), custom_call_target="tpu_custom_call" | custom-call | tf_op jit(solution)/shard_map/pick/pallas_call | solution.py:139
  1.8 3.0 %collective-permute-start = (bf16[128,256]{1,0:T(8,128)(2,1)S(1)}, bf16[128,256]{1,0:T(8,128)(2,1)S(1)}, u32[]{:S(2)}, u32[]{:S(2)}) collective-permute-start(bf16[128,256]{1,0:T(8,128)(2,1)S(1)} %get-tuple-element.18), channel_id=1, source_target_pairs={{0,4},{4,8},{8,12},{12,0},{1,5},{5,9},{9,13},{13,1},{2,6},{6,10},{... | collective-permute-start | bytes 196616 | tf_op jit(solution)/shard_map/ppermute | solution.py:157
  4.8 1.1 %split.1 = (bf16[32,1280]{1,0:T(8,128)(2,1)S(1)}, bf16[32,1280]{1,0:T(8,128)(2,1)S(1)}, bf16[32,1280]{1,0:T(8,128)(2,1)S(1)}, bf16[32,1280]{1,0:T(8,128)(2,1)S(1)}) custom-call(bf16[32,4096]{1,0:T(8,128)(2,1)} %q_ref.1, bf16[32,1024]{1,0:T(8,128)(2,1)} %kv_ref.1), custom_call_target="tpu_custom_call" | custom-call | tf_op jit(solution)/shard_map/split/pallas_call | solution.py:147
  5.8 0.1 collective-permute-start.3
  5.9 1.6 %collective-permute-start.4 = (bf16[32,1280]{1,0:T(8,128)(2,1)S(1)}, bf16[32,1280]{1,0:T(8,128)(2,1)S(1)}, u32[]{:S(2)}, u32[]{:S(2)}) collective-permute-start(bf16[32,1280]{1,0:T(8,128)(2,1)S(1)} %get-tuple-element.23), channel_id=1, source_target_pairs={{0,2},{1,3},{2,0},{3,1},{4,6},{5,7},{6,4},{7,5},{8,10},{9,11},{10,... | collective-permute-start | bytes 245768 | tf_op jit(solution)/shard_map/ppermute | solution.py:159
  7.5 0.3 %collective-permute-start.5 = (bf16[32,1280]{1,0:T(8,128)(2,1)S(1)}, bf16[32,1280]{1,0:T(8,128)(2,1)S(1)}, u32[]{:S(2)}, u32[]{:S(2)}) collective-permute-start(bf16[32,1280]{1,0:T(8,128)(2,1)S(1)} %get-tuple-element.24), channel_id=1, source_target_pairs={{0,3},{1,2},{2,1},{3,0},{4,7},{5,6},{6,5},{7,4},{8,11},{9,10},{10,... | collective-permute-start | bytes 245768 | tf_op jit(solution)/shard_map/ppermute | solution.py:159
  7.8 2.6 %collective-permute-start.1 = (bf16[128,256]{1,0:T(8,128)(2,1)S(1)}, bf16[128,256]{1,0:T(8,128)(2,1)S(1)}, u32[]{:S(2)}, u32[]{:S(2)}) collective-permute-start(bf16[128,256]{1,0:T(8,128)(2,1)S(1)} %get-tuple-element.19), channel_id=1, source_target_pairs={{0,8},{4,12},{8,0},{12,4},{1,9},{5,13},{9,1},{13,5},{2,10},{6,14},... | collective-permute-start | bytes 196616 | tf_op jit(solution)/shard_map/ppermute | solution.py:157
  10.4 0.0 collective-permute-done.refs_1_
  10.4 1.4 %collective-permute-start.2 = (bf16[128,256]{1,0:T(8,128)(2,1)S(1)}, bf16[128,256]{1,0:T(8,128)(2,1)S(1)}, u32[]{:S(2)}, u32[]{:S(2)}) collective-permute-start(bf16[128,256]{1,0:T(8,128)(2,1)S(1)} %get-tuple-element.20), channel_id=1, source_target_pairs={{0,12},{4,0},{8,4},{12,8},{1,13},{5,1},{9,5},{13,9},{2,14},{6,2},{... | collective-permute-start | bytes 196616 | tf_op jit(solution)/shard_map/ppermute | solution.py:157
  11.8 3.2 %collective-permute-done.1.refs_2_ = bf16[128,256]{1,0:T(8,128)(2,1)S(1)} collective-permute-done((bf16[128,256]{1,0:T(8,128)(2,1)S(1)}, bf16[128,256]{1,0:T(8,128)(2,1)S(1)}, u32[]{:S(2)}, u32[]{:S(2)}) %collective-permute-start.1) | collective-permute-done | bytes 65568 | tf_op jit(solution)/shard_map/ppermute | solution.py:157
  15.0 0.0 collective-permute-done.2.refs_3_
  15.0 0.0 collective-permute-done.3.refs_5_
  15.0 0.0 collective-permute-done.4.refs_6_
  15.0 0.0 collective-permute-done.5.refs_7_
  15.0 2.0 %attend.1 = (bf16[32,1024]{1,0:T(8,128)(2,1)S(1)}, bf16[32,1024]{1,0:T(8,128)(2,1)S(1)}, bf16[32,1024]{1,0:T(8,128)(2,1)S(1)}, bf16[32,1024]{1,0:T(8,128)(2,1)S(1)}) custom-call(s32[2,4]{1,0:T(2,128)} %bitcast.2, s32[4]{0:T(128)} %counts_ref.3, bf16[128,256]{1,0:T(8,128)(2,1)S(1)} %get-tuple-element.17.refs_0_, ...), custom_call_target="tpu_custom_call" | custom-call | tf_op jit(solution)/shard_map/attend/pallas_call | solution.py:160
  17.0 0.1 collective-permute-start.6
  17.1 1.5 %collective-permute-start.7 = (bf16[32,1024]{1,0:T(8,128)(2,1)S(1)}, bf16[32,1024]{1,0:T(8,128)(2,1)S(1)}, u32[]{:S(2)}, u32[]{:S(2)}) collective-permute-start(bf16[32,1024]{1,0:T(8,128)(2,1)S(1)} %get-tuple-element.27), channel_id=1, source_target_pairs={{0,2},{1,3},{2,0},{3,1},{4,6},{5,7},{6,4},{7,5},{8,10},{9,11},{10,... | collective-permute-start | bytes 196616 | tf_op jit(solution)/shard_map/ppermute | solution.py:169
  18.6 0.4 %collective-permute-start.8 = (bf16[32,1024]{1,0:T(8,128)(2,1)S(1)}, bf16[32,1024]{1,0:T(8,128)(2,1)S(1)}, u32[]{:S(2)}, u32[]{:S(2)}) collective-permute-start(bf16[32,1024]{1,0:T(8,128)(2,1)S(1)} %get-tuple-element.28), channel_id=1, source_target_pairs={{0,3},{1,2},{2,1},{3,0},{4,7},{5,6},{6,5},{7,4},{8,11},{9,10},{10,... | collective-permute-start | bytes 196616 | tf_op jit(solution)/shard_map/ppermute | solution.py:169
  19.0 0.0 collective-permute-done.6.refs_1_
  19.0 2.7 %collective-permute-done.7.refs_2_ = bf16[32,1024]{1,0:T(8,128)(2,1)S(1)} collective-permute-done((bf16[32,1024]{1,0:T(8,128)(2,1)S(1)}, bf16[32,1024]{1,0:T(8,128)(2,1)S(1)}, u32[]{:S(2)}, u32[]{:S(2)}) %collective-permute-start.7) | collective-permute-done | bytes 65568 | tf_op jit(solution)/shard_map/ppermute | solution.py:169
  21.7 1.0 %collective-permute-done.8.refs_3_ = bf16[32,1024]{1,0:T(8,128)(2,1)S(1)} collective-permute-done((bf16[32,1024]{1,0:T(8,128)(2,1)S(1)}, bf16[32,1024]{1,0:T(8,128)(2,1)S(1)}, u32[]{:S(2)}, u32[]{:S(2)}) %collective-permute-start.8) | collective-permute-done | bytes 65568 | tf_op jit(solution)/shard_map/ppermute | solution.py:169
  22.7 0.7 %join.1 = bf16[32,4096]{1,0:T(8,128)(2,1)} custom-call(bf16[32,1024]{1,0:T(8,128)(2,1)S(1)} %get-tuple-element.25.refs_0_, bf16[32,1024]{1,0:T(8,128)(2,1)S(1)} %collective-permute-done.6.refs_1_, bf16[32,1024]{1,0:T(8,128)(2,1)S(1)} %collective-permute-done.7.refs_2_, bf16[32,1024]{1,0:T(8,128)(2,1)S(1)} %collective-permute-done.8.refs_3_), custom_call_target="tpu_custom_call" | custom-call | tf_op jit(solution)/shard_map/join/pallas_call | solution.py:170
Async XLA Ops:
  1.8 8.6 %collective-permute-start = (bf16[128,256]{1,0:T(8,128)(2,1)S(1)}, bf16[128,256]{1,0:T(8,128)(2,1)S(1)}, u32[]{:S(2)}, u32[]{:S(2)}) collective-permute-start(bf16[128,256]{1,0:T(8,128)(2,1)S(1)} %get-tuple-element.18), channel_id=1, source_target_pairs={{0,4},{4,8},{8,12},{12,0},{1,5},{5,9},{9,13},{13,1},{2,6},{6,10},{... | collective-permute-start | bytes 196616 | tf_op jit(solution)/shard_map/ppermute | solution.py:157
  5.8 9.1 %collective-permute-start.3 = (bf16[32,1280]{1,0:T(8,128)(2,1)S(1)}, bf16[32,1280]{1,0:T(8,128)(2,1)S(1)}, u32[]{:S(2)}, u32[]{:S(2)}) collective-permute-start(bf16[32,1280]{1,0:T(8,128)(2,1)S(1)} %get-tuple-element.22), channel_id=1, source_target_pairs={{0,1},{1,0},{2,3},{3,2},{4,5},{5,4},{6,7},{7,6},{8,9},{9,8},{10,11... | collective-permute-start | bytes 245768 | tf_op jit(solution)/shard_map/ppermute | solution.py:159
  5.9 9.1 %collective-permute-start.4 = (bf16[32,1280]{1,0:T(8,128)(2,1)S(1)}, bf16[32,1280]{1,0:T(8,128)(2,1)S(1)}, u32[]{:S(2)}, u32[]{:S(2)}) collective-permute-start(bf16[32,1280]{1,0:T(8,128)(2,1)S(1)} %get-tuple-element.23), channel_id=1, source_target_pairs={{0,2},{1,3},{2,0},{3,1},{4,6},{5,7},{6,4},{7,5},{8,10},{9,11},{10,... | collective-permute-start | bytes 245768 | tf_op jit(solution)/shard_map/ppermute | solution.py:159
  7.5 7.5 %collective-permute-start.5 = (bf16[32,1280]{1,0:T(8,128)(2,1)S(1)}, bf16[32,1280]{1,0:T(8,128)(2,1)S(1)}, u32[]{:S(2)}, u32[]{:S(2)}) collective-permute-start(bf16[32,1280]{1,0:T(8,128)(2,1)S(1)} %get-tuple-element.24), channel_id=1, source_target_pairs={{0,3},{1,2},{2,1},{3,0},{4,7},{5,6},{6,5},{7,4},{8,11},{9,10},{10,... | collective-permute-start | bytes 245768 | tf_op jit(solution)/shard_map/ppermute | solution.py:159
  7.8 7.2 %collective-permute-start.1 = (bf16[128,256]{1,0:T(8,128)(2,1)S(1)}, bf16[128,256]{1,0:T(8,128)(2,1)S(1)}, u32[]{:S(2)}, u32[]{:S(2)}) collective-permute-start(bf16[128,256]{1,0:T(8,128)(2,1)S(1)} %get-tuple-element.19), channel_id=1, source_target_pairs={{0,8},{4,12},{8,0},{12,4},{1,9},{5,13},{9,1},{13,5},{2,10},{6,14},... | collective-permute-start | bytes 196616 | tf_op jit(solution)/shard_map/ppermute | solution.py:157
  10.4 4.6 %collective-permute-start.2 = (bf16[128,256]{1,0:T(8,128)(2,1)S(1)}, bf16[128,256]{1,0:T(8,128)(2,1)S(1)}, u32[]{:S(2)}, u32[]{:S(2)}) collective-permute-start(bf16[128,256]{1,0:T(8,128)(2,1)S(1)} %get-tuple-element.20), channel_id=1, source_target_pairs={{0,12},{4,0},{8,4},{12,8},{1,13},{5,1},{9,5},{13,9},{2,14},{6,2},{... | collective-permute-start | bytes 196616 | tf_op jit(solution)/shard_map/ppermute | solution.py:157
  17.0 1.9 %collective-permute-start.6 = (bf16[32,1024]{1,0:T(8,128)(2,1)S(1)}, bf16[32,1024]{1,0:T(8,128)(2,1)S(1)}, u32[]{:S(2)}, u32[]{:S(2)}) collective-permute-start(bf16[32,1024]{1,0:T(8,128)(2,1)S(1)} %get-tuple-element.26), channel_id=1, source_target_pairs={{0,1},{1,0},{2,3},{3,2},{4,5},{5,4},{6,7},{7,6},{8,9},{9,8},{10,11... | collective-permute-start | bytes 196616 | tf_op jit(solution)/shard_map/ppermute | solution.py:169
  17.1 4.6 %collective-permute-start.7 = (bf16[32,1024]{1,0:T(8,128)(2,1)S(1)}, bf16[32,1024]{1,0:T(8,128)(2,1)S(1)}, u32[]{:S(2)}, u32[]{:S(2)}) collective-permute-start(bf16[32,1024]{1,0:T(8,128)(2,1)S(1)} %get-tuple-element.27), channel_id=1, source_target_pairs={{0,2},{1,3},{2,0},{3,1},{4,6},{5,7},{6,4},{7,5},{8,10},{9,11},{10,... | collective-permute-start | bytes 196616 | tf_op jit(solution)/shard_map/ppermute | solution.py:169
  18.6 4.1 %collective-permute-start.8 = (bf16[32,1024]{1,0:T(8,128)(2,1)S(1)}, bf16[32,1024]{1,0:T(8,128)(2,1)S(1)}, u32[]{:S(2)}, u32[]{:S(2)}) collective-permute-start(bf16[32,1024]{1,0:T(8,128)(2,1)S(1)} %get-tuple-element.28), channel_id=1, source_target_pairs={{0,3},{1,2},{2,1},{3,0},{4,7},{5,6},{6,5},{7,4},{8,11},{9,10},{10,... | collective-permute-start | bytes 196616 | tf_op jit(solution)/shard_map/ppermute | solution.py:169

commit v3 on v2

--- a/solution.py
+++ b/solution.py
@@ -10,6 +10,9 @@
 
 LOG2E = 1.4426950408889634
 MAX_DIRECT = 4
+UNUSED = 1 << 20
+FEED = (("ctx", 1), ("ctx", 2), ("ctx", 3), ("head", 2), ("head", 3), ("head", 1))
+STAGES = ((2, 3, 1, 0),)
 ANY = pl.BlockSpec(memory_space=pl.ANY)
 SMEM = pl.BlockSpec(memory_space=pltpu.SMEM)
 VMEM = pl.BlockSpec(memory_space=pltpu.VMEM)
@@ -34,25 +37,16 @@
     return lax.fori_loop(0, width, one, jnp.int32(0))
 
 
-def pick_kernel(n_ctx, block, pattern_ref, counts_ref, cache_ref, *refs):
-    outs, sem = refs[:n_ctx], refs[n_ctx]
-    me = lax.axis_index("ctx")
-    shard_blocks = cache_ref.shape[1] // block
-    copies = []
-    for k in list(range(1, n_ctx)) + [0]:
-        row = lax.rem(me + k, n_ctx)
-        index = wanted_index(pattern_ref, counts_ref, row, me, shard_blocks)
-        start = pl.multiple_of(index * block, block)
-        copy = pltpu.make_async_copy(cache_ref.at[0, pl.ds(start, block), :], outs[k], sem.at[k])
-        copy.start()
-        copies.append(copy)
-    for copy in copies:
-        copy.wait()
-
-
-def split_kernel(n_head, q_ref, kv_ref, *refs):
-    outs, sem = refs[:n_head], refs[n_head]
-    h = lax.axis_index("head")
+def prepare_kernel(n_ctx, n_head, pattern_hbm, counts_hbm, cache_ref, q_ref, kv_ref, *refs):
+    blocks, pieces = refs[:n_ctx], refs[n_ctx : n_ctx + n_head]
+    slots_ref, pattern_ref, counts_ref, list_sem, block_sem, piece_sem = refs[n_ctx + n_head :]
+    lists = [
+        pltpu.make_async_copy(pattern_hbm, pattern_ref, list_sem.at[0]),
+        pltpu.make_async_copy(counts_hbm, counts_ref, list_sem.at[1]),
+    ]
+    for copy in lists:
+        copy.start()
+    h, me = lax.axis_index("head"), lax.axis_index("ctx")
     q_cols, kv_cols = q_ref.shape[1] // n_head, kv_ref.shape[1] // n_head
     copies = []
     for m in range(n_head):
@@ -60,32 +54,50 @@
         for ref, cols, at, s in ((q_ref, q_cols, 0, 0), (kv_ref, kv_cols, q_cols, 1)):
             copy = pltpu.make_async_copy(
                 ref.at[:, pl.ds(pl.multiple_of(peer * cols, cols), cols)],
-                outs[m].at[:, pl.ds(at, cols)],
-                sem.at[m, s],
+                pieces[m].at[:, pl.ds(at, cols)],
+                piece_sem.at[m, s],
             )
             copy.start()
             copies.append(copy)
+    for copy in lists:
+        copy.wait()
+    block = blocks[0].shape[0]
+    shard_blocks = cache_ref.shape[1] // block
+    for k in range(n_ctx):
+        row = lax.rem(me + k, n_ctx)
+        index = wanted_index(pattern_ref, counts_ref, row, me, shard_blocks)
+        start = pl.multiple_of(index * block, block)
+        copy = pltpu.make_async_copy(cache_ref.at[0, pl.ds(start, block), :], blocks[k], block_sem.at[k])
+        copy.start()
+        copies.append(copy)
+    for i in range(pattern_ref.shape[0]):
+        away = lax.rem(me - pattern_ref[i, me] // shard_blocks + n_ctx, n_ctx)
+        away = jnp.where(i < counts_ref[me], away, UNUSED)
+        slots_ref[i : i + 1, :] = jnp.full((1, slots_ref.shape[1]), away, jnp.int32)
     for copy in copies:
         copy.wait()
 
 
-def attend_kernel(n_ctx, n_head, d, shard_blocks, pattern_ref, counts_ref, *refs):
-    blocks, pieces, outs = refs[:n_ctx], refs[n_ctx : n_ctx + n_head], refs[n_ctx + n_head :]
-    me, h = lax.axis_index("ctx"), lax.axis_index("head")
+def attend_kernel(n_ctx, n_head, d, mine, slots_ref, *refs):
+    outs = refs[len(refs) - len(mine) :]
+    named = dict(zip(FEED + (("ctx", 0), ("head", 0)), refs))
+    blocks = [named["ctx", k] for k in range(n_ctx)]
+    pieces = [named["head", m] for m in range(n_head)]
+    h = lax.axis_index("head")
     rows = pieces[0].shape[0]
     q_cols = pieces[0].shape[1] - 2 * d
     group = q_cols // d
-    width = pattern_ref.shape[0]
+    width, lanes = slots_ref.shape
     block = blocks[0].shape[0]
     keys, values, slot_bias = [], [], []
     for i in range(width):
-        offset = lax.rem(me - pattern_ref[i, me] // shard_blocks + n_ctx, n_ctx)
+        away = slots_ref[i : i + 1, :]
         kv = blocks[0][...]
         for k in range(1, n_ctx):
-            kv = jnp.where(offset == k, blocks[k][...], kv)
+            kv = jnp.where(away == k, blocks[k][...], kv)
         keys.append(kv[:, :d])
         values.append(kv[:, d:])
-        slot_bias.append(jnp.where(i < counts_ref[me], 0.0, -jnp.inf).astype(jnp.float32))
+        slot_bias.append(jnp.where(away[:, :block] == UNUSED, -jnp.inf, 0.0).astype(jnp.float32))
     for m in range(n_head):
         keys.append(pieces[m][:, q_cols : q_cols + d])
         values.append(pieces[m][:, q_cols + d :])
@@ -95,7 +107,7 @@
     row = lax.broadcasted_iota(jnp.int32, (rows, span), 0)
     key_token = lax.bitwise_xor(column // rows, h) * rows + column % rows
     rate = LOG2E / math.sqrt(d)
-    for m in range(n_head):
+    for m, out in zip(mine, outs):
         q = jnp.concatenate([pieces[m][:, j * d : (j + 1) * d] for j in range(group)], axis=0)
         s = lax.dot_general(q, keys, (((1,), (1,)), ((), ())), preferred_element_type=jnp.float32)
         causal = jnp.where(lax.bitwise_xor(h, m) * rows + row >= key_token, 0.0, -jnp.inf)
@@ -110,11 +122,13 @@
         )
         o = (o / denom).astype(jnp.bfloat16)
         for j in range(group):
-            outs[m][:, j * d : (j + 1) * d] = o[j * rows : (j + 1) * rows]
+            out[:, j * d : (j + 1) * d] = o[j * rows : (j + 1) * rows]
 
 
 def join_kernel(n_head, *refs):
-    pieces, out, sem = refs[:n_head], refs[n_head], refs[n_head + 1]
+    out, sem = refs[n_head], refs[n_head + 1]
+    order = [m for mine in STAGES for m in mine]
+    pieces = [refs[order.index(m)] for m in range(n_head)]
     h = lax.axis_index("head")
     cols = pieces[0].shape[1]
     copies = []
@@ -130,43 +144,48 @@
 def direct(n_ctx, n_head, queries, span_key_value, cache, pattern, counts):
     rows, d = queries.shape[0], cache.shape[2] // 2
     block = rows * n_head
-    shard_blocks = cache.shape[1] // block
     q_cols, kv_cols = queries.shape[1] // n_head, span_key_value.shape[1] // n_head
     bf16 = jnp.bfloat16
     around = [[(i, (i + k) % n_ctx) for i in range(n_ctx)] for k in range(n_ctx)]
     across = [[(i, i ^ m) for i in range(n_head)] for m in range(n_head)]
 
-    blocks = pl.pallas_call(
-        functools.partial(pick_kernel, n_ctx, block),
-        out_shape=[pltpu.VMEM((block, 2 * d), bf16)] * n_ctx,
-        in_specs=[SMEM, SMEM, ANY],
-        out_specs=[VMEM] * n_ctx,
-        scratch_shapes=[pltpu.SemaphoreType.DMA((n_ctx,))],
-        name="pick",
-    )(pattern.T, counts, cache)
-    pieces = pl.pallas_call(
-        functools.partial(split_kernel, n_head),
-        out_shape=[pltpu.VMEM((rows, q_cols + kv_cols), bf16)] * n_head,
-        in_specs=[ANY, ANY],
-        out_specs=[VMEM] * n_head,
-        scratch_shapes=[pltpu.SemaphoreType.DMA((n_head, 2))],
-        name="split",
-    )(queries, span_key_value)
-    blocks, pieces = list(blocks), list(pieces)
-    for k in range(1, n_ctx):
-        blocks[k] = lax.ppermute(blocks[k], "ctx", around[k])
-    for m in (2, 3, 1):
-        pieces[m] = lax.ppermute(pieces[m], "head", across[m])
-    outs = pl.pallas_call(
-        functools.partial(attend_kernel, n_ctx, n_head, d, shard_blocks),
-        out_shape=[pltpu.VMEM((rows, q_cols), bf16)] * n_head,
-        in_specs=[SMEM, SMEM] + [VMEM] * (n_ctx + n_head),
-        out_specs=[VMEM] * n_head,
-        name="attend",
-    )(pattern.T, counts, *map(vmem, blocks + pieces))
-    outs = list(outs)
-    for m in (2, 3, 1):
-        outs[m] = lax.ppermute(outs[m], "head", across[m])
+    prepared = pl.pallas_call(
+        functools.partial(prepare_kernel, n_ctx, n_head),
+        out_shape=[pltpu.VMEM((block, 2 * d), bf16)] * n_ctx
+        + [pltpu.VMEM((rows, q_cols + kv_cols), bf16)] * n_head
+        + [pltpu.VMEM((pattern.shape[1], 2 * d), jnp.int32)],
+        in_specs=[ANY] * 5,
+        out_specs=[VMEM] * (n_ctx + n_head + 1),
+        scratch_shapes=[
+            pltpu.SMEM(pattern.shape[::-1], jnp.int32),
+            pltpu.SMEM(counts.shape, jnp.int32),
+            pltpu.SemaphoreType.DMA((2,)),
+            pltpu.SemaphoreType.DMA((n_ctx,)),
+            pltpu.SemaphoreType.DMA((n_head, 2)),
+        ],
+        name="prepare",
+    )(pattern.T, counts, cache, queries, span_key_value)
+    blocks, pieces = list(prepared[:n_ctx]), list(prepared[n_ctx:-1])
+    for axis, k in FEED:
+        if axis == "ctx":
+            blocks[k] = lax.ppermute(blocks[k], axis, around[k])
+        else:
+            pieces[k] = lax.ppermute(pieces[k], axis, across[k])
+    held = {"ctx": blocks, "head": pieces}
+    order = FEED + (("ctx", 0), ("head", 0))
+    operands = [vmem(held[axis][k]) for axis, k in order]
+    outs, last = [None] * n_head, []
+    for mine in STAGES:
+        made = pl.pallas_call(
+            functools.partial(attend_kernel, n_ctx, n_head, d, mine),
+            out_shape=[pltpu.VMEM((rows, q_cols), bf16)] * len(mine),
+            in_specs=[VMEM] * (1 + n_ctx + n_head + len(last)),
+            out_specs=[VMEM] * len(mine),
+            name=f"attend{mine[0]}",
+        )(vmem(prepared[-1]), *operands, *last)
+        last = [vmem(made[0])]
+        for m, x in zip(mine, made):
+            outs[m] = lax.ppermute(x, "head", across[m]) if m else x
     return pl.pallas_call(
         functools.partial(join_kernel, n_head),
         out_shape=jax.ShapeDtypeStruct((rows, q_cols * n_head), bf16),
@@ -174,7 +193,7 @@
         out_specs=ANY,
         scratch_shapes=[pltpu.SemaphoreType.DMA((n_head,))],
         name="join",
-    )(*map(vmem, outs))
+    )(*[vmem(outs[m]) for mine in STAGES for m in mine])
 
 
 def collect_kernel(n_ctx, block, pattern_ref, counts_ref, cache_ref, out_ref, sem):

time: 23.8 us -> 22.5 us (0.945)
  Pallas kernels: 5.57 us -> 4.05 us
  starting transfers between devices: 10.9 us -> 11.5 us
  waiting for transfers between devices: 6.98 us -> 6.63 us
    pallas_call x3 -> x2, Pallas kernels: 4.84 us -> 3.32 us  [the longest x1 1.99 us: direct(): pl.pallas_call(functools.partial(prepare_kernel, n_ctx, n_head), out_shap...]
    ppermute x9, starting transfers between devices: 10.9 us -> 11.5 us  [the longest x3 7.18 us: direct(): blocks[k] = lax.ppermute(blocks[k], axis, around[k])]
    ppermute x9, waiting for transfers between devices: 6.98 us -> 6.63 us  [the longest x3 3.53 us: direct(): outs[m] = lax.ppermute(x, 'head', across[m]) if m else x]
  transfers between devices with their start and end apart: 9 -> 9, of which waited for: 3 -> 3; matrix products, arithmetic and copies ran while one was open for 0% -> 0% of each run, Pallas kernels for 4% -> 0%
where the time goes in v3:
time: 22.5 us; the launch traced here: 22.2 us
  starting transfers between devices  11.5 us (51%)
  waiting for transfers between devices  6.63 us (29%)
  Pallas kernels  4.05 us (18%)
    ppermute x3, starting transfers between devices, direct(): blocks[k] = lax.ppermute(blocks[k], axis, around[k])  7.18 us
    ppermute x3, waiting for transfers between devices, direct(): outs[m] = lax.ppermute(x, 'head', across[m]) if m else x  3.53 us
    ppermute x3, waiting for transfers between devices, direct(): blocks[k] = lax.ppermute(blocks[k], axis, around[k])  3.09 us
    ppermute x3, starting transfers between devices, direct(): outs[m] = lax.ppermute(x, 'head', across[m]) if m else x  2.21 us
    ppermute x3, starting transfers between devices, direct(): pieces[k] = lax.ppermute(pieces[k], axis, across[k])  2.14 us
    pallas_call x1, Pallas kernels, direct(): pl.pallas_call(functools.partial(prepare_kernel, n_ctx, n_head), out_shap...  1.99 us
    pallas_call x1, Pallas kernels, direct(): pl.pallas_call(functools.partial(attend_kernel, n_ctx, n_head, d, mine),...  1.34 us
    pallas_call x1, Pallas kernels, direct(): pl.pallas_call(functools.partial(join_kernel, n_head), out_shape=jax.Shap...  0.73 us
  transfers between devices with their start and end apart: 9, of which 3 were waited for; matrix products, arithmetic and copies ran while one was open for 0% of the time, Pallas kernels for 0%

profile of v3, /device:TPU:0, one launch (start us, length us, event | category | flops | bytes accessed | tf_op | source)
XLA Modules:
  0.0 22.2 jit_solution(17031241093598327846)
XLA Ops:
  0.0 2.0 %prepare.1 = (bf16[128,256]{1,0:T(8,128)(2,1)S(1)}, bf16[128,256]{1,0:T(8,128)(2,1)S(1)}, bf16[128,256]{1,0:T(8,128)(2,1)S(1)}, bf16[128,256]{1,0:T(8,128)(2,1)S...) custom-call(s32[2,4]{1,0:T(2,128)} %bitcast.1, ...), custom_call_target="tpu_custom_call" | custom-call | tf_op jit(solution)/shard_map/prepare/pallas_call | solution.py:152
  2.0 3.0 %collective-permute-start = (bf16[128,256]{1,0:T(8,128)(2,1)S(1)}, bf16[128,256]{1,0:T(8,128)(2,1)S(1)}, u32[]{:S(2)}, u32[]{:S(2)}) collective-permute-start(bf16[128,256]{1,0:T(8,128)(2,1)S(1)} %get-tuple-element.19), channel_id=1, source_target_pairs={{0,4},{4,8},{8,12},{12,0},{1,5},{5,9},{9,13},{13,1},{2,6},{6,10},{... | collective-permute-start | bytes 196616 | tf_op jit(solution)/shard_map/ppermute | solution.py:171
  5.0 1.5 %collective-permute-start.3 = (bf16[32,1280]{1,0:T(8,128)(2,1)S(1)}, bf16[32,1280]{1,0:T(8,128)(2,1)S(1)}, u32[]{:S(2)}, u32[]{:S(2)}) collective-permute-start(bf16[32,1280]{1,0:T(8,128)(2,1)S(1)} %get-tuple-element.22), channel_id=1, source_target_pairs={{0,2},{1,3},{2,0},{3,1},{4,6},{5,7},{6,4},{7,5},{8,10},{9,11},{10,... | collective-permute-start | bytes 245768 | tf_op jit(solution)/shard_map/ppermute | solution.py:173
  6.5 0.0 collective-permute-start.4
  6.5 0.6 %collective-permute-start.5 = (bf16[32,1280]{1,0:T(8,128)(2,1)S(1)}, bf16[32,1280]{1,0:T(8,128)(2,1)S(1)}, u32[]{:S(2)}, u32[]{:S(2)}) collective-permute-start(bf16[32,1280]{1,0:T(8,128)(2,1)S(1)} %get-tuple-element.24), channel_id=1, source_target_pairs={{0,1},{1,0},{2,3},{3,2},{4,5},{5,4},{6,7},{7,6},{8,9},{9,8},{10,11... | collective-permute-start | bytes 245768 | tf_op jit(solution)/shard_map/ppermute | solution.py:173
  7.2 2.6 %collective-permute-start.1 = (bf16[128,256]{1,0:T(8,128)(2,1)S(1)}, bf16[128,256]{1,0:T(8,128)(2,1)S(1)}, u32[]{:S(2)}, u32[]{:S(2)}) collective-permute-start(bf16[128,256]{1,0:T(8,128)(2,1)S(1)} %get-tuple-element.20), channel_id=1, source_target_pairs={{0,8},{4,12},{8,0},{12,4},{1,9},{5,13},{9,1},{13,5},{2,10},{6,14},... | collective-permute-start | bytes 196616 | tf_op jit(solution)/shard_map/ppermute | solution.py:171
  9.8 0.0 collective-permute-done.refs_0_
  9.8 1.6 %collective-permute-start.2 = (bf16[128,256]{1,0:T(8,128)(2,1)S(1)}, bf16[128,256]{1,0:T(8,128)(2,1)S(1)}, u32[]{:S(2)}, u32[]{:S(2)}) collective-permute-start(bf16[128,256]{1,0:T(8,128)(2,1)S(1)} %get-tuple-element.21), channel_id=1, source_target_pairs={{0,12},{4,0},{8,4},{12,8},{1,13},{5,1},{9,5},{13,9},{2,14},{6,2},{... | collective-permute-start | bytes 196616 | tf_op jit(solution)/shard_map/ppermute | solution.py:171
  11.3 3.1 %collective-permute-done.1.refs_1_ = bf16[128,256]{1,0:T(8,128)(2,1)S(1)} collective-permute-done((bf16[128,256]{1,0:T(8,128)(2,1)S(1)}, bf16[128,256]{1,0:T(8,128)(2,1)S(1)}, u32[]{:S(2)}, u32[]{:S(2)}) %collective-permute-start.1) | collective-permute-done | bytes 65568 | tf_op jit(solution)/shard_map/ppermute | solution.py:171
  14.4 0.0 collective-permute-done.2.refs_2_
  14.4 0.0 collective-permute-done.3.refs_3_
  14.4 0.0 collective-permute-done.4.refs_4_
  14.4 0.0 collective-permute-done.5.refs_5_
  14.4 1.3 %attend2.1 = (bf16[32,1024]{1,0:T(8,128)(2,1)S(1)}, bf16[32,1024]{1,0:T(8,128)(2,1)S(1)}, bf16[32,1024]{1,0:T(8,128)(2,1)S(1)}, bf16[32,1024]{1,0:T(8,128)(2,1)S(1)}) custom-call(s32[2,256]{1,0:T(2,128)S(1)} %get-tuple-element.18.slots_ref, bf16[128,256]{1,0:T(8,128)(2,1)S(1)} %collective-permute-done.refs_0_, ...), custom_call_target="tpu_custom_call" | custom-call | tf_op jit(solution)/shard_map/attend2/pallas_call | solution.py:179
  15.8 1.5 %collective-permute-start.6 = (bf16[32,1024]{1,0:T(8,128)(2,1)S(1)}, bf16[32,1024]{1,0:T(8,128)(2,1)S(1)}, u32[]{:S(2)}, u32[]{:S(2)}) collective-permute-start(bf16[32,1024]{1,0:T(8,128)(2,1)S(1)} %get-tuple-element.27), channel_id=1, source_target_pairs={{0,2},{1,3},{2,0},{3,1},{4,6},{5,7},{6,4},{7,5},{8,10},{9,11},{10,... | collective-permute-start | bytes 196616 | tf_op jit(solution)/shard_map/ppermute | solution.py:188
  17.2 0.0 collective-permute-start.7
  17.2 0.7 %collective-permute-start.8 = (bf16[32,1024]{1,0:T(8,128)(2,1)S(1)}, bf16[32,1024]{1,0:T(8,128)(2,1)S(1)}, u32[]{:S(2)}, u32[]{:S(2)}) collective-permute-start(bf16[32,1024]{1,0:T(8,128)(2,1)S(1)} %get-tuple-element.29), channel_id=1, source_target_pairs={{0,1},{1,0},{2,3},{3,2},{4,5},{5,4},{6,7},{7,6},{8,9},{9,8},{10,11... | collective-permute-start | bytes 196616 | tf_op jit(solution)/shard_map/ppermute | solution.py:188
  18.0 2.1 %collective-permute-done.6.refs_0_ = bf16[32,1024]{1,0:T(8,128)(2,1)S(1)} collective-permute-done((bf16[32,1024]{1,0:T(8,128)(2,1)S(1)}, bf16[32,1024]{1,0:T(8,128)(2,1)S(1)}, u32[]{:S(2)}, u32[]{:S(2)}) %collective-permute-start.6) | collective-permute-done | bytes 65568 | tf_op jit(solution)/shard_map/ppermute | solution.py:188
  20.1 1.4 %collective-permute-done.7.refs_1_ = bf16[32,1024]{1,0:T(8,128)(2,1)S(1)} collective-permute-done((bf16[32,1024]{1,0:T(8,128)(2,1)S(1)}, bf16[32,1024]{1,0:T(8,128)(2,1)S(1)}, u32[]{:S(2)}, u32[]{:S(2)}) %collective-permute-start.7) | collective-permute-done | bytes 65568 | tf_op jit(solution)/shard_map/ppermute | solution.py:188
  21.5 0.0 collective-permute-done.8.refs_2_
  21.5 0.7 %join.1 = bf16[32,4096]{1,0:T(8,128)(2,1)} custom-call(bf16[32,1024]{1,0:T(8,128)(2,1)S(1)} %collective-permute-done.6.refs_0_, bf16[32,1024]{1,0:T(8,128)(2,1)S(1)} %collective-permute-done.7.refs_1_, bf16[32,1024]{1,0:T(8,128)(2,1)S(1)} %collective-permute-done.8.refs_2_, bf16[32,1024]{1,0:T(8,128)(2,1)S(1)} %get-tuple-element.30.refs_3_), custom_call_target="tpu_custom_call" | custom-call | tf_op jit(solution)/shard_map/join/pallas_call | solution.py:189
Async XLA Ops:
  2.0 7.8 %collective-permute-start = (bf16[128,256]{1,0:T(8,128)(2,1)S(1)}, bf16[128,256]{1,0:T(8,128)(2,1)S(1)}, u32[]{:S(2)}, u32[]{:S(2)}) collective-permute-start(bf16[128,256]{1,0:T(8,128)(2,1)S(1)} %get-tuple-element.19), channel_id=1, source_target_pairs={{0,4},{4,8},{8,12},{12,0},{1,5},{5,9},{9,13},{13,1},{2,6},{6,10},{... | collective-permute-start | bytes 196616 | tf_op jit(solution)/shard_map/ppermute | solution.py:171
  5.0 9.4 %collective-permute-start.3 = (bf16[32,1280]{1,0:T(8,128)(2,1)S(1)}, bf16[32,1280]{1,0:T(8,128)(2,1)S(1)}, u32[]{:S(2)}, u32[]{:S(2)}) collective-permute-start(bf16[32,1280]{1,0:T(8,128)(2,1)S(1)} %get-tuple-element.22), channel_id=1, source_target_pairs={{0,2},{1,3},{2,0},{3,1},{4,6},{5,7},{6,4},{7,5},{8,10},{9,11},{10,... | collective-permute-start | bytes 245768 | tf_op jit(solution)/shard_map/ppermute | solution.py:173
  6.5 7.9 %collective-permute-start.4 = (bf16[32,1280]{1,0:T(8,128)(2,1)S(1)}, bf16[32,1280]{1,0:T(8,128)(2,1)S(1)}, u32[]{:S(2)}, u32[]{:S(2)}) collective-permute-start(bf16[32,1280]{1,0:T(8,128)(2,1)S(1)} %get-tuple-element.23), channel_id=1, source_target_pairs={{0,3},{1,2},{2,1},{3,0},{4,7},{5,6},{6,5},{7,4},{8,11},{9,10},{10,... | collective-permute-start | bytes 245768 | tf_op jit(solution)/shard_map/ppermute | solution.py:173
  6.5 7.9 %collective-permute-start.5 = (bf16[32,1280]{1,0:T(8,128)(2,1)S(1)}, bf16[32,1280]{1,0:T(8,128)(2,1)S(1)}, u32[]{:S(2)}, u32[]{:S(2)}) collective-permute-start(bf16[32,1280]{1,0:T(8,128)(2,1)S(1)} %get-tuple-element.24), channel_id=1, source_target_pairs={{0,1},{1,0},{2,3},{3,2},{4,5},{5,4},{6,7},{7,6},{8,9},{9,8},{10,11... | collective-permute-start | bytes 245768 | tf_op jit(solution)/shard_map/ppermute | solution.py:173
  7.2 7.2 %collective-permute-start.1 = (bf16[128,256]{1,0:T(8,128)(2,1)S(1)}, bf16[128,256]{1,0:T(8,128)(2,1)S(1)}, u32[]{:S(2)}, u32[]{:S(2)}) collective-permute-start(bf16[128,256]{1,0:T(8,128)(2,1)S(1)} %get-tuple-element.20), channel_id=1, source_target_pairs={{0,8},{4,12},{8,0},{12,4},{1,9},{5,13},{9,1},{13,5},{2,10},{6,14},... | collective-permute-start | bytes 196616 | tf_op jit(solution)/shard_map/ppermute | solution.py:171
  9.8 4.6 %collective-permute-start.2 = (bf16[128,256]{1,0:T(8,128)(2,1)S(1)}, bf16[128,256]{1,0:T(8,128)(2,1)S(1)}, u32[]{:S(2)}, u32[]{:S(2)}) collective-permute-start(bf16[128,256]{1,0:T(8,128)(2,1)S(1)} %get-tuple-element.21), channel_id=1, source_target_pairs={{0,12},{4,0},{8,4},{12,8},{1,13},{5,1},{9,5},{13,9},{2,14},{6,2},{... | collective-permute-start | bytes 196616 | tf_op jit(solution)/shard_map/ppermute | solution.py:171
  15.8 4.3 %collective-permute-start.6 = (bf16[32,1024]{1,0:T(8,128)(2,1)S(1)}, bf16[32,1024]{1,0:T(8,128)(2,1)S(1)}, u32[]{:S(2)}, u32[]{:S(2)}) collective-permute-start(bf16[32,1024]{1,0:T(8,128)(2,1)S(1)} %get-tuple-element.27), channel_id=1, source_target_pairs={{0,2},{1,3},{2,0},{3,1},{4,6},{5,7},{6,4},{7,5},{8,10},{9,11},{10,... | collective-permute-start | bytes 196616 | tf_op jit(solution)/shard_map/ppermute | solution.py:188
  17.2 4.3 %collective-permute-start.7 = (bf16[32,1024]{1,0:T(8,128)(2,1)S(1)}, bf16[32,1024]{1,0:T(8,128)(2,1)S(1)}, u32[]{:S(2)}, u32[]{:S(2)}) collective-permute-start(bf16[32,1024]{1,0:T(8,128)(2,1)S(1)} %get-tuple-element.28), channel_id=1, source_target_pairs={{0,3},{1,2},{2,1},{3,0},{4,7},{5,6},{6,5},{7,4},{8,11},{9,10},{10,... | collective-permute-start | bytes 196616 | tf_op jit(solution)/shard_map/ppermute | solution.py:188
  17.2 4.3 %collective-permute-start.8 = (bf16[32,1024]{1,0:T(8,128)(2,1)S(1)}, bf16[32,1024]{1,0:T(8,128)(2,1)S(1)}, u32[]{:S(2)}, u32[]{:S(2)}) collective-permute-start(bf16[32,1024]{1,0:T(8,128)(2,1)S(1)} %get-tuple-element.29), channel_id=1, source_target_pairs={{0,1},{1,0},{2,3},{3,2},{4,5},{5,4},{6,7},{7,6},{8,9},{9,8},{10,11... | collective-permute-start | bytes 196616 | tf_op jit(solution)/shard_map/ppermute | solution.py:188

commit v4 on v3

--- a/solution.py
+++ b/solution.py
@@ -12,7 +12,8 @@
 MAX_DIRECT = 4
 UNUSED = 1 << 20
 FEED = (("ctx", 1), ("ctx", 2), ("ctx", 3), ("head", 2), ("head", 3), ("head", 1))
-STAGES = ((2, 3, 1, 0),)
+TOGETHER = 4
+STAGES = ((1, 2, 3, 0),)
 ANY = pl.BlockSpec(memory_space=pl.ANY)
 SMEM = pl.BlockSpec(memory_space=pltpu.SMEM)
 VMEM = pl.BlockSpec(memory_space=pltpu.VMEM)
@@ -39,12 +40,13 @@
 
 def prepare_kernel(n_ctx, n_head, pattern_hbm, counts_hbm, cache_ref, q_ref, kv_ref, *refs):
     blocks, pieces = refs[:n_ctx], refs[n_ctx : n_ctx + n_head]
-    slots_ref, pattern_ref, counts_ref, list_sem, block_sem, piece_sem = refs[n_ctx + n_head :]
+    slots_ref, pattern_ref, counts_ref, shard_ref, list_sem, shard_sem, piece_sem = refs[n_ctx + n_head :]
     lists = [
         pltpu.make_async_copy(pattern_hbm, pattern_ref, list_sem.at[0]),
         pltpu.make_async_copy(counts_hbm, counts_ref, list_sem.at[1]),
     ]
-    for copy in lists:
+    shard = pltpu.make_async_copy(cache_ref.at[0], shard_ref, shard_sem)
+    for copy in lists + [shard]:
         copy.start()
     h, me = lax.axis_index("head"), lax.axis_index("ctx")
     q_cols, kv_cols = q_ref.shape[1] // n_head, kv_ref.shape[1] // n_head
@@ -62,18 +64,19 @@
     for copy in lists:
         copy.wait()
     block = blocks[0].shape[0]
-    shard_blocks = cache_ref.shape[1] // block
+    shard_blocks = shard_ref.shape[0] // block
+    starts = []
     for k in range(n_ctx):
         row = lax.rem(me + k, n_ctx)
         index = wanted_index(pattern_ref, counts_ref, row, me, shard_blocks)
-        start = pl.multiple_of(index * block, block)
-        copy = pltpu.make_async_copy(cache_ref.at[0, pl.ds(start, block), :], blocks[k], block_sem.at[k])
-        copy.start()
-        copies.append(copy)
+        starts.append(pl.multiple_of(index * block, block))
     for i in range(pattern_ref.shape[0]):
         away = lax.rem(me - pattern_ref[i, me] // shard_blocks + n_ctx, n_ctx)
         away = jnp.where(i < counts_ref[me], away, UNUSED)
         slots_ref[i : i + 1, :] = jnp.full((1, slots_ref.shape[1]), away, jnp.int32)
+    shard.wait()
+    for k in range(n_ctx):
+        blocks[k][...] = shard_ref[pl.ds(starts[k], block), :]
     for copy in copies:
         copy.wait()
 
@@ -107,13 +110,18 @@
     row = lax.broadcasted_iota(jnp.int32, (rows, span), 0)
     key_token = lax.bitwise_xor(column // rows, h) * rows + column % rows
     rate = LOG2E / math.sqrt(d)
-    for m, out in zip(mine, outs):
-        q = jnp.concatenate([pieces[m][:, j * d : (j + 1) * d] for j in range(group)], axis=0)
+    for first in range(0, len(mine), TOGETHER):
+        some = mine[first : first + TOGETHER]
+        q = jnp.concatenate(
+            [pieces[m][:, j * d : (j + 1) * d] for m in some for j in range(group)], axis=0
+        )
         s = lax.dot_general(q, keys, (((1,), (1,)), ((), ())), preferred_element_type=jnp.float32)
-        causal = jnp.where(lax.bitwise_xor(h, m) * rows + row >= key_token, 0.0, -jnp.inf)
-        own = s[:, width * block :].reshape(group, rows, span) + causal[None]
+        causal = jnp.stack(
+            [jnp.where(lax.bitwise_xor(h, m) * rows + row >= key_token, 0.0, -jnp.inf) for m in some]
+        )
+        own = s[:, width * block :].reshape(len(some), group, rows, span) + causal[:, None]
         parts = [s[:, i * block : (i + 1) * block] + slot_bias[i] for i in range(width)]
-        s = jnp.concatenate(parts + [own.reshape(group * rows, span)], axis=1)
+        s = jnp.concatenate(parts + [own.reshape(-1, span)], axis=1)
         top = jnp.max(s, axis=1, keepdims=True)
         p = jnp.exp2((s - top) * rate)
         denom = jnp.sum(p, axis=1, keepdims=True)
@@ -121,8 +129,10 @@
             p.astype(jnp.bfloat16), values, (((1,), (0,)), ((), ())), preferred_element_type=jnp.float32
         )
         o = (o / denom).astype(jnp.bfloat16)
-        for j in range(group):
-            out[:, j * d : (j + 1) * d] = o[j * rows : (j + 1) * rows]
+        for n in range(len(some)):
+            for j in range(group):
+                at = (n * group + j) * rows
+                outs[first + n][:, j * d : (j + 1) * d] = o[at : at + rows]
 
 
 def join_kernel(n_head, *refs):
@@ -159,8 +169,9 @@
         scratch_shapes=[
             pltpu.SMEM(pattern.shape[::-1], jnp.int32),
             pltpu.SMEM(counts.shape, jnp.int32),
+            pltpu.VMEM(cache.shape[1:], bf16),
             pltpu.SemaphoreType.DMA((2,)),
-            pltpu.SemaphoreType.DMA((n_ctx,)),
+            pltpu.SemaphoreType.DMA,
             pltpu.SemaphoreType.DMA((n_head, 2)),
         ],
         name="prepare",

time: 22.5 us -> 21.3 us (0.947)
  Pallas kernels: 4.05 us -> 2.98 us
    pallas_call x1, Pallas kernels: 1.34 us -> 0.69 us  [direct(): pl.pallas_call(functools.partial(attend_kernel, n_ctx, n_head, d, mine),...]
    pallas_call x1, Pallas kernels: 1.99 us -> 1.57 us  [direct(): pl.pallas_call(functools.partial(prepare_kernel, n_ctx, n_head), out_shap...]
    ppermute x3, starting transfers between devices: 2.21 us -> 1.93 us  [direct(): outs[m] = lax.ppermute(x, 'head', across[m]) if m else x]
where the time goes in v4:
time: 21.3 us; the launch traced here: 21.1 us
  starting transfers between devices  11.3 us (53%)
  waiting for transfers between devices  6.83 us (32%)
  Pallas kernels  2.98 us (14%)
    ppermute x3, starting transfers between devices, direct(): blocks[k] = lax.ppermute(blocks[k], axis, around[k])  7.22 us
    ppermute x3, waiting for transfers between devices, direct(): outs[m] = lax.ppermute(x, 'head', across[m]) if m else x  3.73 us
    ppermute x3, waiting for transfers between devices, direct(): blocks[k] = lax.ppermute(blocks[k], axis, around[k])  3.09 us
    ppermute x3, starting transfers between devices, direct(): pieces[k] = lax.ppermute(pieces[k], axis, across[k])  2.14 us
    ppermute x3, starting transfers between devices, direct(): outs[m] = lax.ppermute(x, 'head', across[m]) if m else x  1.93 us
    pallas_call x1, Pallas kernels, direct(): pl.pallas_call(functools.partial(prepare_kernel, n_ctx, n_head), out_shap...  1.57 us
    pallas_call x1, Pallas kernels, direct(): pl.pallas_call(functools.partial(join_kernel, n_head), out_shape=jax.Shap...  0.73 us
    pallas_call x1, Pallas kernels, direct(): pl.pallas_call(functools.partial(attend_kernel, n_ctx, n_head, d, mine),...  0.69 us
  transfers between devices with their start and end apart: 9, of which 3 were waited for; matrix products, arithmetic and copies ran while one was open for 0% of the time, Pallas kernels for 0%

profile of v4, /device:TPU:0, one launch (start us, length us, event | category | flops | bytes accessed | tf_op | source)
XLA Modules:
  0.0 21.1 jit_solution(14328624964647584186)
XLA Ops:
  0.0 1.6 %prepare.1 = (bf16[128,256]{1,0:T(8,128)(2,1)S(1)}, bf16[128,256]{1,0:T(8,128)(2,1)S(1)}, bf16[128,256]{1,0:T(8,128)(2,1)S(1)}, bf16[128,256]{1,0:T(8,128)(2,1)S...) custom-call(s32[2,4]{1,0:T(2,128)} %bitcast.1, ...), custom_call_target="tpu_custom_call" | custom-call | tf_op jit(solution)/shard_map/prepare/pallas_call | solution.py:162
  1.6 3.1 %collective-permute-start = (bf16[128,256]{1,0:T(8,128)(2,1)S(1)}, bf16[128,256]{1,0:T(8,128)(2,1)S(1)}, u32[]{:S(2)}, u32[]{:S(2)}) collective-permute-start(bf16[128,256]{1,0:T(8,128)(2,1)S(1)} %get-tuple-element.19), channel_id=1, source_target_pairs={{0,4},{4,8},{8,12},{12,0},{1,5},{5,9},{9,13},{13,1},{2,6},{6,10},{... | collective-permute-start | bytes 196616 | tf_op jit(solution)/shard_map/ppermute | solution.py:182
  4.7 1.5 %collective-permute-start.3 = (bf16[32,1280]{1,0:T(8,128)(2,1)S(1)}, bf16[32,1280]{1,0:T(8,128)(2,1)S(1)}, u32[]{:S(2)}, u32[]{:S(2)}) collective-permute-start(bf16[32,1280]{1,0:T(8,128)(2,1)S(1)} %get-tuple-element.22), channel_id=1, source_target_pairs={{0,2},{1,3},{2,0},{3,1},{4,6},{5,7},{6,4},{7,5},{8,10},{9,11},{10,... | collective-permute-start | bytes 245768 | tf_op jit(solution)/shard_map/ppermute | solution.py:184
  6.1 0.0 collective-permute-start.4
  6.1 0.6 %collective-permute-start.5 = (bf16[32,1280]{1,0:T(8,128)(2,1)S(1)}, bf16[32,1280]{1,0:T(8,128)(2,1)S(1)}, u32[]{:S(2)}, u32[]{:S(2)}) collective-permute-start(bf16[32,1280]{1,0:T(8,128)(2,1)S(1)} %get-tuple-element.24), channel_id=1, source_target_pairs={{0,1},{1,0},{2,3},{3,2},{4,5},{5,4},{6,7},{7,6},{8,9},{9,8},{10,11... | collective-permute-start | bytes 245768 | tf_op jit(solution)/shard_map/ppermute | solution.py:184
  6.8 2.6 %collective-permute-start.1 = (bf16[128,256]{1,0:T(8,128)(2,1)S(1)}, bf16[128,256]{1,0:T(8,128)(2,1)S(1)}, u32[]{:S(2)}, u32[]{:S(2)}) collective-permute-start(bf16[128,256]{1,0:T(8,128)(2,1)S(1)} %get-tuple-element.20), channel_id=1, source_target_pairs={{0,8},{4,12},{8,0},{12,4},{1,9},{5,13},{9,1},{13,5},{2,10},{6,14},... | collective-permute-start | bytes 196616 | tf_op jit(solution)/shard_map/ppermute | solution.py:182
  9.4 0.0 collective-permute-done.refs_0_
  9.4 1.6 %collective-permute-start.2 = (bf16[128,256]{1,0:T(8,128)(2,1)S(1)}, bf16[128,256]{1,0:T(8,128)(2,1)S(1)}, u32[]{:S(2)}, u32[]{:S(2)}) collective-permute-start(bf16[128,256]{1,0:T(8,128)(2,1)S(1)} %get-tuple-element.21), channel_id=1, source_target_pairs={{0,12},{4,0},{8,4},{12,8},{1,13},{5,1},{9,5},{13,9},{2,14},{6,2},{... | collective-permute-start | bytes 196616 | tf_op jit(solution)/shard_map/ppermute | solution.py:182
  10.9 3.1 %collective-permute-done.1.refs_1_ = bf16[128,256]{1,0:T(8,128)(2,1)S(1)} collective-permute-done((bf16[128,256]{1,0:T(8,128)(2,1)S(1)}, bf16[128,256]{1,0:T(8,128)(2,1)S(1)}, u32[]{:S(2)}, u32[]{:S(2)}) %collective-permute-start.1) | collective-permute-done | bytes 65568 | tf_op jit(solution)/shard_map/ppermute | solution.py:182
  14.0 0.0 collective-permute-done.2.refs_2_
  14.0 0.0 collective-permute-done.3.refs_3_
  14.0 0.0 collective-permute-done.4.refs_4_
  14.0 0.0 collective-permute-done.5.refs_5_
  14.1 0.7 %attend1.1 = (bf16[32,1024]{1,0:T(8,128)(2,1)S(1)}, bf16[32,1024]{1,0:T(8,128)(2,1)S(1)}, bf16[32,1024]{1,0:T(8,128)(2,1)S(1)}, bf16[32,1024]{1,0:T(8,128)(2,1)S(1)}) custom-call(s32[2,256]{1,0:T(2,128)S(1)} %get-tuple-element.18.slots_ref, bf16[128,256]{1,0:T(8,128)(2,1)S(1)} %collective-permute-done.refs_0_, ...), custom_call_target="tpu_custom_call" | custom-call | tf_op jit(solution)/shard_map/attend1/pallas_call | solution.py:190
  14.7 0.1 collective-permute-start.6
  14.8 1.5 %collective-permute-start.7 = (bf16[32,1024]{1,0:T(8,128)(2,1)S(1)}, bf16[32,1024]{1,0:T(8,128)(2,1)S(1)}, u32[]{:S(2)}, u32[]{:S(2)}) collective-permute-start(bf16[32,1024]{1,0:T(8,128)(2,1)S(1)} %get-tuple-element.28), channel_id=1, source_target_pairs={{0,2},{1,3},{2,0},{3,1},{4,6},{5,7},{6,4},{7,5},{8,10},{9,11},{10,... | collective-permute-start | bytes 196616 | tf_op jit(solution)/shard_map/ppermute | solution.py:199
  16.3 0.4 %collective-permute-start.8 = (bf16[32,1024]{1,0:T(8,128)(2,1)S(1)}, bf16[32,1024]{1,0:T(8,128)(2,1)S(1)}, u32[]{:S(2)}, u32[]{:S(2)}) collective-permute-start(bf16[32,1024]{1,0:T(8,128)(2,1)S(1)} %get-tuple-element.29), channel_id=1, source_target_pairs={{0,3},{1,2},{2,1},{3,0},{4,7},{5,6},{6,5},{7,4},{8,11},{9,10},{10,... | collective-permute-start | bytes 196616 | tf_op jit(solution)/shard_map/ppermute | solution.py:199
  16.7 0.0 collective-permute-done.6.refs_0_
  16.7 2.7 %collective-permute-done.7.refs_1_ = bf16[32,1024]{1,0:T(8,128)(2,1)S(1)} collective-permute-done((bf16[32,1024]{1,0:T(8,128)(2,1)S(1)}, bf16[32,1024]{1,0:T(8,128)(2,1)S(1)}, u32[]{:S(2)}, u32[]{:S(2)}) %collective-permute-start.7) | collective-permute-done | bytes 65568 | tf_op jit(solution)/shard_map/ppermute | solution.py:199
  19.4 1.0 %collective-permute-done.8.refs_2_ = bf16[32,1024]{1,0:T(8,128)(2,1)S(1)} collective-permute-done((bf16[32,1024]{1,0:T(8,128)(2,1)S(1)}, bf16[32,1024]{1,0:T(8,128)(2,1)S(1)}, u32[]{:S(2)}, u32[]{:S(2)}) %collective-permute-start.8) | collective-permute-done | bytes 65568 | tf_op jit(solution)/shard_map/ppermute | solution.py:199
  20.4 0.7 %join.1 = bf16[32,4096]{1,0:T(8,128)(2,1)} custom-call(bf16[32,1024]{1,0:T(8,128)(2,1)S(1)} %collective-permute-done.6.refs_0_, bf16[32,1024]{1,0:T(8,128)(2,1)S(1)} %collective-permute-done.7.refs_1_, bf16[32,1024]{1,0:T(8,128)(2,1)S(1)} %collective-permute-done.8.refs_2_, bf16[32,1024]{1,0:T(8,128)(2,1)S(1)} %get-tuple-element.30.refs_3_), custom_call_target="tpu_custom_call" | custom-call | tf_op jit(solution)/shard_map/join/pallas_call | solution.py:200
Async XLA Ops:
  1.6 7.8 %collective-permute-start = (bf16[128,256]{1,0:T(8,128)(2,1)S(1)}, bf16[128,256]{1,0:T(8,128)(2,1)S(1)}, u32[]{:S(2)}, u32[]{:S(2)}) collective-permute-start(bf16[128,256]{1,0:T(8,128)(2,1)S(1)} %get-tuple-element.19), channel_id=1, source_target_pairs={{0,4},{4,8},{8,12},{12,0},{1,5},{5,9},{9,13},{13,1},{2,6},{6,10},{... | collective-permute-start | bytes 196616 | tf_op jit(solution)/shard_map/ppermute | solution.py:182
  4.7 9.4 %collective-permute-start.3 = (bf16[32,1280]{1,0:T(8,128)(2,1)S(1)}, bf16[32,1280]{1,0:T(8,128)(2,1)S(1)}, u32[]{:S(2)}, u32[]{:S(2)}) collective-permute-start(bf16[32,1280]{1,0:T(8,128)(2,1)S(1)} %get-tuple-element.22), channel_id=1, source_target_pairs={{0,2},{1,3},{2,0},{3,1},{4,6},{5,7},{6,4},{7,5},{8,10},{9,11},{10,... | collective-permute-start | bytes 245768 | tf_op jit(solution)/shard_map/ppermute | solution.py:184
  6.1 7.9 %collective-permute-start.4 = (bf16[32,1280]{1,0:T(8,128)(2,1)S(1)}, bf16[32,1280]{1,0:T(8,128)(2,1)S(1)}, u32[]{:S(2)}, u32[]{:S(2)}) collective-permute-start(bf16[32,1280]{1,0:T(8,128)(2,1)S(1)} %get-tuple-element.23), channel_id=1, source_target_pairs={{0,3},{1,2},{2,1},{3,0},{4,7},{5,6},{6,5},{7,4},{8,11},{9,10},{10,... | collective-permute-start | bytes 245768 | tf_op jit(solution)/shard_map/ppermute | solution.py:184
  6.1 7.9 %collective-permute-start.5 = (bf16[32,1280]{1,0:T(8,128)(2,1)S(1)}, bf16[32,1280]{1,0:T(8,128)(2,1)S(1)}, u32[]{:S(2)}, u32[]{:S(2)}) collective-permute-start(bf16[32,1280]{1,0:T(8,128)(2,1)S(1)} %get-tuple-element.24), channel_id=1, source_target_pairs={{0,1},{1,0},{2,3},{3,2},{4,5},{5,4},{6,7},{7,6},{8,9},{9,8},{10,11... | collective-permute-start | bytes 245768 | tf_op jit(solution)/shard_map/ppermute | solution.py:184
  6.8 7.2 %collective-permute-start.1 = (bf16[128,256]{1,0:T(8,128)(2,1)S(1)}, bf16[128,256]{1,0:T(8,128)(2,1)S(1)}, u32[]{:S(2)}, u32[]{:S(2)}) collective-permute-start(bf16[128,256]{1,0:T(8,128)(2,1)S(1)} %get-tuple-element.20), channel_id=1, source_target_pairs={{0,8},{4,12},{8,0},{12,4},{1,9},{5,13},{9,1},{13,5},{2,10},{6,14},... | collective-permute-start | bytes 196616 | tf_op jit(solution)/shard_map/ppermute | solution.py:182
  9.4 4.6 %collective-permute-start.2 = (bf16[128,256]{1,0:T(8,128)(2,1)S(1)}, bf16[128,256]{1,0:T(8,128)(2,1)S(1)}, u32[]{:S(2)}, u32[]{:S(2)}) collective-permute-start(bf16[128,256]{1,0:T(8,128)(2,1)S(1)} %get-tuple-element.21), channel_id=1, source_target_pairs={{0,12},{4,0},{8,4},{12,8},{1,13},{5,1},{9,5},{13,9},{2,14},{6,2},{... | collective-permute-start | bytes 196616 | tf_op jit(solution)/shard_map/ppermute | solution.py:182
  14.7 1.9 %collective-permute-start.6 = (bf16[32,1024]{1,0:T(8,128)(2,1)S(1)}, bf16[32,1024]{1,0:T(8,128)(2,1)S(1)}, u32[]{:S(2)}, u32[]{:S(2)}) collective-permute-start(bf16[32,1024]{1,0:T(8,128)(2,1)S(1)} %get-tuple-element.27), channel_id=1, source_target_pairs={{0,1},{1,0},{2,3},{3,2},{4,5},{5,4},{6,7},{7,6},{8,9},{9,8},{10,11... | collective-permute-start | bytes 196616 | tf_op jit(solution)/shard_map/ppermute | solution.py:199
  14.8 4.6 %collective-permute-start.7 = (bf16[32,1024]{1,0:T(8,128)(2,1)S(1)}, bf16[32,1024]{1,0:T(8,128)(2,1)S(1)}, u32[]{:S(2)}, u32[]{:S(2)}) collective-permute-start(bf16[32,1024]{1,0:T(8,128)(2,1)S(1)} %get-tuple-element.28), channel_id=1, source_target_pairs={{0,2},{1,3},{2,0},{3,1},{4,6},{5,7},{6,4},{7,5},{8,10},{9,11},{10,... | collective-permute-start | bytes 196616 | tf_op jit(solution)/shard_map/ppermute | solution.py:199
  16.3 4.1 %collective-permute-start.8 = (bf16[32,1024]{1,0:T(8,128)(2,1)S(1)}, bf16[32,1024]{1,0:T(8,128)(2,1)S(1)}, u32[]{:S(2)}, u32[]{:S(2)}) collective-permute-start(bf16[32,1024]{1,0:T(8,128)(2,1)S(1)} %get-tuple-element.29), channel_id=1, source_target_pairs={{0,3},{1,2},{2,1},{3,0},{4,7},{5,6},{6,5},{7,4},{8,11},{9,10},{10,... | collective-permute-start | bytes 196616 | tf_op jit(solution)/shard_map/ppermute | solution.py:199

commit v5 on v4

--- a/solution.py
+++ b/solution.py
@@ -11,9 +11,7 @@
 LOG2E = 1.4426950408889634
 MAX_DIRECT = 4
 UNUSED = 1 << 20
-FEED = (("ctx", 1), ("ctx", 2), ("ctx", 3), ("head", 2), ("head", 3), ("head", 1))
-TOGETHER = 4
-STAGES = ((1, 2, 3, 0),)
+CHOOSE, GATHER, EARLY, MID = 10**8, 10**10, 10**10, 10**9
 ANY = pl.BlockSpec(memory_space=pl.ANY)
 SMEM = pl.BlockSpec(memory_space=pltpu.SMEM)
 VMEM = pl.BlockSpec(memory_space=pltpu.VMEM)
@@ -38,9 +36,9 @@
     return lax.fori_loop(0, width, one, jnp.int32(0))
 
 
-def prepare_kernel(n_ctx, n_head, pattern_hbm, counts_hbm, cache_ref, q_ref, kv_ref, *refs):
-    blocks, pieces = refs[:n_ctx], refs[n_ctx : n_ctx + n_head]
-    slots_ref, pattern_ref, counts_ref, shard_ref, list_sem, shard_sem, piece_sem = refs[n_ctx + n_head :]
+def prepare_kernel(n_ctx, pattern_hbm, counts_hbm, cache_ref, *refs):
+    blocks = refs[:n_ctx]
+    slots_ref, pattern_ref, counts_ref, shard_ref, list_sem, shard_sem = refs[n_ctx:]
     lists = [
         pltpu.make_async_copy(pattern_hbm, pattern_ref, list_sem.at[0]),
         pltpu.make_async_copy(counts_hbm, counts_ref, list_sem.at[1]),
@@ -48,21 +46,9 @@
     shard = pltpu.make_async_copy(cache_ref.at[0], shard_ref, shard_sem)
     for copy in lists + [shard]:
         copy.start()
-    h, me = lax.axis_index("head"), lax.axis_index("ctx")
-    q_cols, kv_cols = q_ref.shape[1] // n_head, kv_ref.shape[1] // n_head
-    copies = []
-    for m in range(n_head):
-        peer = lax.bitwise_xor(h, m)
-        for ref, cols, at, s in ((q_ref, q_cols, 0, 0), (kv_ref, kv_cols, q_cols, 1)):
-            copy = pltpu.make_async_copy(
-                ref.at[:, pl.ds(pl.multiple_of(peer * cols, cols), cols)],
-                pieces[m].at[:, pl.ds(at, cols)],
-                piece_sem.at[m, s],
-            )
-            copy.start()
-            copies.append(copy)
     for copy in lists:
         copy.wait()
+    me = lax.axis_index("ctx")
     block = blocks[0].shape[0]
     shard_blocks = shard_ref.shape[0] // block
     starts = []
@@ -77,51 +63,55 @@
     shard.wait()
     for k in range(n_ctx):
         blocks[k][...] = shard_ref[pl.ds(starts[k], block), :]
-    for copy in copies:
-        copy.wait()
-
-
-def attend_kernel(n_ctx, n_head, d, mine, slots_ref, *refs):
-    outs = refs[len(refs) - len(mine) :]
-    named = dict(zip(FEED + (("ctx", 0), ("head", 0)), refs))
-    blocks = [named["ctx", k] for k in range(n_ctx)]
-    pieces = [named["head", m] for m in range(n_head)]
-    h = lax.axis_index("head")
-    rows = pieces[0].shape[0]
-    q_cols = pieces[0].shape[1] - 2 * d
-    group = q_cols // d
-    width, lanes = slots_ref.shape
+
+
+def choose_kernel(n_ctx, slots_ref, *refs):
+    blocks, chosen_ref = refs[:n_ctx], refs[n_ctx]
     block = blocks[0].shape[0]
-    keys, values, slot_bias = [], [], []
-    for i in range(width):
+    for i in range(slots_ref.shape[0]):
         away = slots_ref[i : i + 1, :]
         kv = blocks[0][...]
         for k in range(1, n_ctx):
             kv = jnp.where(away == k, blocks[k][...], kv)
-        keys.append(kv[:, :d])
-        values.append(kv[:, d:])
-        slot_bias.append(jnp.where(away[:, :block] == UNUSED, -jnp.inf, 0.0).astype(jnp.float32))
-    for m in range(n_head):
-        keys.append(pieces[m][:, q_cols : q_cols + d])
-        values.append(pieces[m][:, q_cols + d :])
-    keys, values = jnp.concatenate(keys, axis=0), jnp.concatenate(values, axis=0)
+        chosen_ref[i * block : (i + 1) * block, :] = kv
+
+
+def gather_kernel(*refs):
+    rows = refs[0].shape[0]
+    for m, ref in enumerate(refs[:-1]):
+        refs[-1][m * rows : (m + 1) * rows, :] = ref[...]
+
+
+def attend(n_head, mine, slots_ref, q_ref, kv_ref, chosen):
+    h = lax.axis_index("head")
+    d = chosen[0].shape[1] // 2
+    rows, q_cols, kv_cols = q_ref.shape[0], q_ref.shape[1] // n_head, kv_ref.shape[1] // n_head
+    group, width = q_cols // d, slots_ref.shape[0]
+    block = chosen[0].shape[0] // width
     span = n_head * rows
     column = lax.broadcasted_iota(jnp.int32, (rows, span), 1)
     row = lax.broadcasted_iota(jnp.int32, (rows, span), 0)
     key_token = lax.bitwise_xor(column // rows, h) * rows + column % rows
+    causal = jnp.where(h * rows + row >= key_token, 0.0, -jnp.inf)
+    slot_bias = [
+        jnp.where(slots_ref[i : i + 1, :block] == UNUSED, -jnp.inf, 0.0).astype(jnp.float32)
+        for i in range(width)
+    ]
     rate = LOG2E / math.sqrt(d)
-    for first in range(0, len(mine), TOGETHER):
-        some = mine[first : first + TOGETHER]
-        q = jnp.concatenate(
-            [pieces[m][:, j * d : (j + 1) * d] for m in some for j in range(group)], axis=0
-        )
+    found = []
+    for m, chosen_ref in zip(mine, chosen):
+        peer = lax.bitwise_xor(h, m)
+
+        def columns(ref, base, at):
+            return ref[:, pl.ds(pl.multiple_of(peer * base + at, d), d)]
+
+        keys = jnp.concatenate([chosen_ref[:, :d], columns(kv_ref, kv_cols, 0)], axis=0)
+        values = jnp.concatenate([chosen_ref[:, d:], columns(kv_ref, kv_cols, d)], axis=0)
+        q = jnp.concatenate([columns(q_ref, q_cols, j * d) for j in range(group)], axis=0)
         s = lax.dot_general(q, keys, (((1,), (1,)), ((), ())), preferred_element_type=jnp.float32)
-        causal = jnp.stack(
-            [jnp.where(lax.bitwise_xor(h, m) * rows + row >= key_token, 0.0, -jnp.inf) for m in some]
-        )
-        own = s[:, width * block :].reshape(len(some), group, rows, span) + causal[:, None]
+        own = s[:, width * block :].reshape(group, rows, span) + causal[None]
         parts = [s[:, i * block : (i + 1) * block] + slot_bias[i] for i in range(width)]
-        s = jnp.concatenate(parts + [own.reshape(-1, span)], axis=1)
+        s = jnp.concatenate(parts + [own.reshape(group * rows, span)], axis=1)
         top = jnp.max(s, axis=1, keepdims=True)
         p = jnp.exp2((s - top) * rate)
         denom = jnp.sum(p, axis=1, keepdims=True)
@@ -129,82 +119,127 @@
             p.astype(jnp.bfloat16), values, (((1,), (0,)), ((), ())), preferred_element_type=jnp.float32
         )
         o = (o / denom).astype(jnp.bfloat16)
-        for n in range(len(some)):
-            for j in range(group):
-                at = (n * group + j) * rows
-                outs[first + n][:, j * d : (j + 1) * d] = o[at : at + rows]
-
-
-def join_kernel(n_head, *refs):
-    out, sem = refs[n_head], refs[n_head + 1]
-    order = [m for mine in STAGES for m in mine]
-    pieces = [refs[order.index(m)] for m in range(n_head)]
+        found.append([o[j * rows : (j + 1) * rows] for j in range(group)])
+    return found
+
+
+def early_kernel(n_head, mine, slots_ref, q_ref, kv_ref, *refs):
+    chosen, outs = refs[: len(mine)], refs[len(mine) :]
+    for out, parts in zip(outs, attend(n_head, mine, slots_ref, q_ref, kv_ref, chosen)):
+        d = parts[0].shape[1]
+        for j, part in enumerate(parts):
+            out[:, j * d : (j + 1) * d] = part
+
+
+def late_kernel(n_head, before, mine, slots_ref, q_ref, kv_ref, *refs):
+    chosen, refs = refs[: len(mine)], refs[len(mine) :]
+    done, out_ref, made_ref, sem = refs[: len(before)], *refs[len(before) :]
     h = lax.axis_index("head")
-    cols = pieces[0].shape[1]
-    copies = []
-    for m in range(n_head):
+    cols = q_ref.shape[1] // n_head
+
+    def send(m, ref):
         start = pl.multiple_of(lax.bitwise_xor(h, m) * cols, cols)
-        copy = pltpu.make_async_copy(pieces[m], out.at[:, pl.ds(start, cols)], sem.at[m])
+        copy = pltpu.make_async_copy(ref, out_ref.at[:, pl.ds(start, cols)], sem.at[m])
         copy.start()
-        copies.append(copy)
+        return copy
+
+    copies = [send(m, ref) for m, ref in zip(before, done)]
+    for n, (m, parts) in enumerate(zip(mine, attend(n_head, mine, slots_ref, q_ref, kv_ref, chosen))):
+        d = parts[0].shape[1]
+        for j, part in enumerate(parts):
+            made_ref[n, :, j * d : (j + 1) * d] = part
+        copies.append(send(m, made_ref.at[n]))
     for copy in copies:
         copy.wait()
+
+
+def after_kernel(x_ref, first_ref, out_ref):
+    pass
+
+
+def cost(flops):
+    return pl.CostEstimate(flops=flops, bytes_accessed=1 << 20, transcendentals=0)
 
 
 def direct(n_ctx, n_head, queries, span_key_value, cache, pattern, counts):
     rows, d = queries.shape[0], cache.shape[2] // 2
     block = rows * n_head
-    q_cols, kv_cols = queries.shape[1] // n_head, span_key_value.shape[1] // n_head
+    q_cols = queries.shape[1] // n_head
+    width = pattern.shape[1]
     bf16 = jnp.bfloat16
     around = [[(i, (i + k) % n_ctx) for i in range(n_ctx)] for k in range(n_ctx)]
     across = [[(i, i ^ m) for i in range(n_head)] for m in range(n_head)]
 
-    prepared = pl.pallas_call(
-        functools.partial(prepare_kernel, n_ctx, n_head),
-        out_shape=[pltpu.VMEM((block, 2 * d), bf16)] * n_ctx
-        + [pltpu.VMEM((rows, q_cols + kv_cols), bf16)] * n_head
-        + [pltpu.VMEM((pattern.shape[1], 2 * d), jnp.int32)],
-        in_specs=[ANY] * 5,
-        out_specs=[VMEM] * (n_ctx + n_head + 1),
+    *blocks, slots = pl.pallas_call(
+        functools.partial(prepare_kernel, n_ctx),
+        out_shape=[pltpu.VMEM((block, 2 * d), bf16)] * n_ctx + [pltpu.VMEM((width, 2 * d), jnp.int32)],
+        in_specs=[ANY] * 3,
+        out_specs=[VMEM] * (n_ctx + 1),
         scratch_shapes=[
             pltpu.SMEM(pattern.shape[::-1], jnp.int32),
             pltpu.SMEM(counts.shape, jnp.int32),
             pltpu.VMEM(cache.shape[1:], bf16),
             pltpu.SemaphoreType.DMA((2,)),
             pltpu.SemaphoreType.DMA,
-            pltpu.SemaphoreType.DMA((n_head, 2)),
         ],
         name="prepare",
-    )(pattern.T, counts, cache, queries, span_key_value)
-    blocks, pieces = list(prepared[:n_ctx]), list(prepared[n_ctx:-1])
-    for axis, k in FEED:
-        if axis == "ctx":
-            blocks[k] = lax.ppermute(blocks[k], axis, around[k])
-        else:
-            pieces[k] = lax.ppermute(pieces[k], axis, across[k])
-    held = {"ctx": blocks, "head": pieces}
-    order = FEED + (("ctx", 0), ("head", 0))
-    operands = [vmem(held[axis][k]) for axis, k in order]
-    outs, last = [None] * n_head, []
-    for mine in STAGES:
-        made = pl.pallas_call(
-            functools.partial(attend_kernel, n_ctx, n_head, d, mine),
+    )(pattern.T, counts, cache)
+    for k in range(1, n_ctx):
+        blocks[k] = lax.ppermute(blocks[k], "ctx", around[k])
+    pieces = [span_key_value] * n_head
+    for m in (2, 3, 1):
+        pieces[m] = lax.ppermute(span_key_value, "head", across[m])
+    slots = vmem(slots)
+    chosen = [None] * n_head
+    chosen[0] = pl.pallas_call(
+        functools.partial(choose_kernel, n_ctx),
+        out_shape=pltpu.VMEM((width * block, 2 * d), bf16),
+        in_specs=[VMEM] * (1 + n_ctx),
+        out_specs=VMEM,
+        cost_estimate=cost(CHOOSE),
+        name="choose",
+    )(slots, *map(vmem, blocks))
+    chosen[1] = lax.ppermute(chosen[0], "head", across[1])
+    chosen[2] = lax.ppermute(chosen[0], "head", across[2])
+    kv = pl.pallas_call(
+        gather_kernel,
+        out_shape=pltpu.VMEM((block, span_key_value.shape[1]), bf16),
+        in_specs=[VMEM] * n_head,
+        out_specs=VMEM,
+        cost_estimate=cost(GATHER),
+        name="gather",
+    )(*map(vmem, pieces))
+    given = [slots, vmem(queries), vmem(kv)]
+
+    def stage(mine, name, flops):
+        return pl.pallas_call(
+            functools.partial(early_kernel, n_head, mine),
             out_shape=[pltpu.VMEM((rows, q_cols), bf16)] * len(mine),
-            in_specs=[VMEM] * (1 + n_ctx + n_head + len(last)),
+            in_specs=[VMEM] * (3 + len(mine)),
             out_specs=[VMEM] * len(mine),
-            name=f"attend{mine[0]}",
-        )(vmem(prepared[-1]), *operands, *last)
-        last = [vmem(made[0])]
-        for m, x in zip(mine, made):
-            outs[m] = lax.ppermute(x, "head", across[m]) if m else x
+            cost_estimate=cost(flops),
+            name=name,
+        )(*given, *[vmem(chosen[m]) for m in mine])
+
+    near = stage((0, 1), "early", EARLY)
+    chosen[2] = pl.pallas_call(
+        after_kernel,
+        out_shape=pltpu.VMEM(chosen[2].shape, bf16),
+        in_specs=[VMEM, VMEM],
+        out_specs=VMEM,
+        input_output_aliases={0: 0},
+        name="after",
+    )(vmem(chosen[2]), vmem(near[0]))
+    chosen[3] = lax.ppermute(chosen[2], "head", across[1])
+    across_x = stage((2,), "mid", MID)
     return pl.pallas_call(
-        functools.partial(join_kernel, n_head),
-        out_shape=jax.ShapeDtypeStruct((rows, q_cols * n_head), bf16),
-        in_specs=[VMEM] * n_head,
+        functools.partial(late_kernel, n_head, (0, 1, 2), (3,)),
+        out_shape=jax.ShapeDtypeStruct(queries.shape, bf16),
+        in_specs=[VMEM] * 7,
         out_specs=ANY,
-        scratch_shapes=[pltpu.SemaphoreType.DMA((n_head,))],
-        name="join",
-    )(*[vmem(outs[m]) for mine in STAGES for m in mine])
+        scratch_shapes=[pltpu.VMEM((1, rows, q_cols), bf16), pltpu.SemaphoreType.DMA((n_head,))],
+        name="late",
+    )(*given, vmem(chosen[3]), *map(vmem, [*near, *across_x]))
 
 
 def collect_kernel(n_ctx, block, pattern_ref, counts_ref, cache_ref, out_ref, sem):

time: 21.3 us -> 20.4 us (0.958)
  waiting for transfers between devices: 6.83 us -> 5.63 us
  Pallas kernels: 2.98 us -> 3.67 us
  starting transfers between devices: 11.3 us -> 10.8 us
    ppermute x9, waiting for transfers between devices: 6.83 us -> 5.63 us  [the longest x1 3.37 us: direct(): chosen[2] = lax.ppermute(chosen[0], 'head', across[2])]
    pallas_call x3 -> x7, Pallas kernels: 2.98 us -> 3.67 us  [the longest x1 1.3 us: direct(): pl.pallas_call(functools.partial(prepare_kernel, n_ctx), out_shape=[pltpu...]
    ppermute x9, starting transfers between devices: 11.3 us -> 10.8 us  [the longest x3 7.01 us: direct(): blocks[k] = lax.ppermute(blocks[k], 'ctx', around[k])]
  transfers between devices with their start and end apart: 9 -> 9, of which waited for: 3 -> 5; matrix products, arithmetic and copies ran while one was open for 0% -> 0% of each run, Pallas kernels for 0% -> 6%
where the time goes in v5:
time: 20.4 us; the launch traced here: 20.2 us
  starting transfers between devices  10.8 us (53%)
  waiting for transfers between devices  5.63 us (28%)
  Pallas kernels  3.67 us (18%)
    ppermute x3, starting transfers between devices, direct(): blocks[k] = lax.ppermute(blocks[k], 'ctx', around[k])  7.01 us
    ppermute x1, waiting for transfers between devices, direct(): chosen[2] = lax.ppermute(chosen[0], 'head', across[2])  3.37 us
    ppermute x3, starting transfers between devices, direct(): pieces[m] = lax.ppermute(span_key_value, 'head', across[m])  2.14 us
    ppermute x1, starting transfers between devices, direct(): chosen[2] = lax.ppermute(chosen[0], 'head', across[2])  1.6 us
    pallas_call x1, Pallas kernels, direct(): pl.pallas_call(functools.partial(prepare_kernel, n_ctx), out_shape=[pltpu...  1.3 us
    ppermute x3, waiting for transfers between devices, direct(): blocks[k] = lax.ppermute(blocks[k], 'ctx', around[k])  1.22 us
    pallas_call x2, Pallas kernels, stage(): pl.pallas_call(functools.partial(early_kernel, n_head, mine), out_shape=[...  1.19 us
    pallas_call x1, Pallas kernels, direct(): pl.pallas_call(functools.partial(late_kernel, n_head, (0, 1, 2), (3,)), o...  1.12 us
  transfers between devices with their start and end apart: 9, of which 5 were waited for; matrix products, arithmetic and copies ran while one was open for 0% of the time, Pallas kernels for 6%

profile of v5, /device:TPU:0, one launch (start us, length us, event | category | flops | bytes accessed | tf_op | source)
XLA Modules:
  0.0 20.2 jit_solution(3537218056657766668)
XLA Ops:
  0.0 1.3 %prepare.1 = (bf16[128,256]{1,0:T(8,128)(2,1)S(1)}, bf16[128,256]{1,0:T(8,128)(2,1)S(1)}, bf16[128,256]{1,0:T(8,128)(2,1)S(1)}, bf16[128,256]{1,0:T(8,128)(2,1)S(1)}, s32[2,256]{1,0:T(2,128)S(1)}) custom-call(s32[2,4]{1,0:T(2,128)} %bitcast.1, s32[4]{0:T(128)} %counts_hbm.1, bf16[1,2048,256]{2,1,0:T(8,128)(2,1)} %cache_ref.1), custom_call_target="tpu_custom_call" | custom-call | tf_op jit(solution)/shard_map/prepare/pallas_call | solution.py:173
  1.3 3.1 %collective-permute-start.3 = (bf16[128,256]{1,0:T(8,128)(2,1)S(1)}, bf16[128,256]{1,0:T(8,128)(2,1)S(1)}, u32[]{:S(2)}, u32[]{:S(2)}) collective-permute-start(bf16[128,256]{1,0:T(8,128)(2,1)S(1)} %get-tuple-element.14), channel_id=1, source_target_pairs={{0,4},{4,8},{8,12},{12,0},{1,5},{5,9},{9,13},{13,1},{2,6},{6,10},{... | collective-permute-start | bytes 196616 | tf_op jit(solution)/shard_map/ppermute | solution.py:188
  4.4 2.6 %collective-permute-start.4 = (bf16[128,256]{1,0:T(8,128)(2,1)S(1)}, bf16[128,256]{1,0:T(8,128)(2,1)S(1)}, u32[]{:S(2)}, u32[]{:S(2)}) collective-permute-start(bf16[128,256]{1,0:T(8,128)(2,1)S(1)} %get-tuple-element.15), channel_id=1, source_target_pairs={{0,8},{4,12},{8,0},{12,4},{1,9},{5,13},{9,1},{13,5},{2,10},{6,14},... | collective-permute-start | bytes 196616 | tf_op jit(solution)/shard_map/ppermute | solution.py:188
  7.0 1.3 %collective-permute-start.5 = (bf16[128,256]{1,0:T(8,128)(2,1)S(1)}, bf16[128,256]{1,0:T(8,128)(2,1)S(1)}, u32[]{:S(2)}, u32[]{:S(2)}) collective-permute-start(bf16[128,256]{1,0:T(8,128)(2,1)S(1)} %get-tuple-element.16), channel_id=1, source_target_pairs={{0,12},{4,0},{8,4},{12,8},{1,13},{5,1},{9,5},{13,9},{2,14},{6,2},{... | collective-permute-start | bytes 196616 | tf_op jit(solution)/shard_map/ppermute | solution.py:188
  8.3 0.0 copy-done.1
  8.3 1.5 %collective-permute-start.1 = (bf16[32,1024]{1,0:T(8,128)(2,1)S(1)}, bf16[32,1024]{1,0:T(8,128)(2,1)S(1)}, u32[]{:S(2)}, u32[]{:S(2)}) collective-permute-start(bf16[32,1024]{1,0:T(8,128)(2,1)S(1)} %copy-done.1), channel_id=1, source_target_pairs={{0,2},{1,3},{2,0},{3,1},{4,6},{5,7},{6,4},{7,5},{8,10},{9,11},{10,... | collective-permute-start | bytes 196616 | tf_op jit(solution)/shard_map/ppermute | solution.py:191
  9.8 0.0 collective-permute-start
  9.8 0.0 collective-permute-done.3.refs_1_
  9.8 0.6 %collective-permute-start.2 = (bf16[32,1024]{1,0:T(8,128)(2,1)S(1)}, bf16[32,1024]{1,0:T(8,128)(2,1)S(1)}, u32[]{:S(2)}, u32[]{:S(2)}) collective-permute-start(bf16[32,1024]{1,0:T(8,128)(2,1)S(1)} %copy-done.1), channel_id=1, source_target_pairs={{0,3},{1,2},{2,1},{3,0},{4,7},{5,6},{6,5},{7,4},{8,11},{9,10},{10,... | collective-permute-start | bytes 196616 | tf_op jit(solution)/shard_map/ppermute | solution.py:191
  10.5 1.0 %collective-permute-done.4.refs_2_ = bf16[128,256]{1,0:T(8,128)(2,1)S(1)} collective-permute-done((bf16[128,256]{1,0:T(8,128)(2,1)S(1)}, bf16[128,256]{1,0:T(8,128)(2,1)S(1)}, u32[]{:S(2)}, u32[]{:S(2)}) %collective-permute-start.4) | collective-permute-done | bytes 65568 | tf_op jit(solution)/shard_map/ppermute | solution.py:188
  11.5 0.2 %collective-permute-done.5.refs_3_ = bf16[128,256]{1,0:T(8,128)(2,1)S(1)} collective-permute-done((bf16[128,256]{1,0:T(8,128)(2,1)S(1)}, bf16[128,256]{1,0:T(8,128)(2,1)S(1)}, u32[]{:S(2)}, u32[]{:S(2)}) %collective-permute-start.5) | collective-permute-done | bytes 65568 | tf_op jit(solution)/shard_map/ppermute | solution.py:188
  11.7 0.0 copy-start
  11.7 0.1 collective-permute-start.7
  11.8 1.6 %collective-permute-start.6 = (bf16[256,256]{1,0:T(8,128)(2,1)S(1)}, bf16[256,256]{1,0:T(8,128)(2,1)S(1)}, u32[]{:S(2)}, u32[]{:S(2)}) collective-permute-start(bf16[256,256]{1,0:T(8,128)(2,1)S(1)} %choose.1.refs_0_), channel_id=1, source_target_pairs={{0,2},{1,3},{2,0},{3,1},{4,6},{5,7},{6,4},{7,5},{8,10},{9,11},{10,... | collective-permute-start | bytes 393224 | tf_op jit(solution)/shard_map/ppermute | solution.py:203
  13.4 0.0 collective-permute-done.1.refs_2_
  13.4 0.0 collective-permute-done.refs_1_
  13.4 0.1 collective-permute-done.2.refs_3_
  13.6 0.0 collective-permute-done.7.refs_1_
  13.6 0.7 %early.1 = (bf16[32,1024]{1,0:T(8,128)(2,1)S(1)}, bf16[32,1024]{1,0:T(8,128)(2,1)S(1)}) custom-call(s32[2,256]{1,0:T(2,128)S(1)} %get-tuple-element.12.slots_ref, bf16[32,4096]{1,0:T(8,128)(2,1)S(1)} %copy-done, bf16[128,1024]{1,0:T(8,128)(2,1)S(1)} %gather.1.kv_ref, bf16[256,256]{1,0:T(8,128)(2,1)S(1)} %choose.1.refs_0_, ...), custom_call_target="tpu_custom_call" | custom-call | flops 10000000000 | bytes 1048576 | tf_op jit(solution)/shard_map/early/pallas_call | solution.py:215
  14.4 3.4 %collective-permute-done.6.x_ref = bf16[256,256]{1,0:T(8,128)(2,1)S(1)} collective-permute-done((bf16[256,256]{1,0:T(8,128)(2,1)S(1)}, bf16[256,256]{1,0:T(8,128)(2,1)S(1)}, u32[]{:S(2)}, u32[]{:S(2)}) %collective-permute-start.6) | collective-permute-done | bytes 131104 | tf_op jit(solution)/shard_map/ppermute | solution.py:203
  17.7 0.0 collective-permute-start.8
  17.7 0.5 %mid.1.refs_3_ = bf16[32,1024]{1,0:T(8,128)(2,1)S(1)} custom-call(s32[2,256]{1,0:T(2,128)S(1)} %get-tuple-element.12.slots_ref, bf16[32,4096]{1,0:T(8,128)(2,1)S(1)} %copy-done, bf16[128,1024]{1,0:T(8,128)(2,1)S(1)} %gather.1.kv_ref, bf16[256,256]{1,0:T(8,128)(2,1)S(1)} %after.1.refs_0_), custom_call_target="tpu_custom_call" | custom-call | flops 1000000000 | bytes 1048576 | tf_op jit(solution)/shard_map/mid/pallas_call | solution.py:215
  18.2 0.9 %collective-permute-done.8.refs_0_ = bf16[256,256]{1,0:T(8,128)(2,1)S(1)} collective-permute-done((bf16[256,256]{1,0:T(8,128)(2,1)S(1)}, bf16[256,256]{1,0:T(8,128)(2,1)S(1)}, u32[]{:S(2)}, u32[]{:S(2)}) %collective-permute-start.8) | collective-permute-done | bytes 131104 | tf_op jit(solution)/shard_map/ppermute | solution.py:233
  19.1 1.1 %late.1 = bf16[32,4096]{1,0:T(8,128)(2,1)} custom-call(s32[2,256]{1,0:T(2,128)S(1)} %get-tuple-element.12.slots_ref, bf16[32,4096]{1,0:T(8,128)(2,1)S(1)} %copy-done, bf16[128,1024]{1,0:T(8,128)(2,1)S(1)} %gather.1.kv_ref, bf16[256,256]{1,0:T(8,128)(2,1)S(1)} %collective-permute-done.8.refs_0_, bf16[32,1024]{1,0:T(8,128)(2,1)S(1)} %get-tuple-element.17.first_ref.refs_1_, ...), custom_call_target="tpu_custom_call" | custom-call | tf_op jit(solution)/shard_map/late/pallas_call | solution.py:235
  (5 shorter events, 0.1 us)
Async XLA Ops:
  0.0 8.3 %copy-start.1 = (bf16[32,1024]{1,0:T(8,128)(2,1)S(1)}, bf16[32,1024]{1,0:T(8,128)(2,1)}, u32[]{:S(2)}) copy-start(bf16[32,1024]{1,0:T(8,128)(2,1)} %refs_0_.1) | copy-start | bytes 196612
  1.3 8.5 %collective-permute-start.3 = (bf16[128,256]{1,0:T(8,128)(2,1)S(1)}, bf16[128,256]{1,0:T(8,128)(2,1)S(1)}, u32[]{:S(2)}, u32[]{:S(2)}) collective-permute-start(bf16[128,256]{1,0:T(8,128)(2,1)S(1)} %get-tuple-element.14), channel_id=1, source_target_pairs={{0,4},{4,8},{8,12},{12,0},{1,5},{5,9},{9,13},{13,1},{2,6},{6,10},{... | collective-permute-start | bytes 196616 | tf_op jit(solution)/shard_map/ppermute | solution.py:188
  4.4 7.1 %collective-permute-start.4 = (bf16[128,256]{1,0:T(8,128)(2,1)S(1)}, bf16[128,256]{1,0:T(8,128)(2,1)S(1)}, u32[]{:S(2)}, u32[]{:S(2)}) collective-permute-start(bf16[128,256]{1,0:T(8,128)(2,1)S(1)} %get-tuple-element.15), channel_id=1, source_target_pairs={{0,8},{4,12},{8,0},{12,4},{1,9},{5,13},{9,1},{13,5},{2,10},{6,14},... | collective-permute-start | bytes 196616 | tf_op jit(solution)/shard_map/ppermute | solution.py:188
  7.0 4.7 %collective-permute-start.5 = (bf16[128,256]{1,0:T(8,128)(2,1)S(1)}, bf16[128,256]{1,0:T(8,128)(2,1)S(1)}, u32[]{:S(2)}, u32[]{:S(2)}) collective-permute-start(bf16[128,256]{1,0:T(8,128)(2,1)S(1)} %get-tuple-element.16), channel_id=1, source_target_pairs={{0,12},{4,0},{8,4},{12,8},{1,13},{5,1},{9,5},{13,9},{2,14},{6,2},{... | collective-permute-start | bytes 196616 | tf_op jit(solution)/shard_map/ppermute | solution.py:188
  8.3 5.1 %collective-permute-start.1 = (bf16[32,1024]{1,0:T(8,128)(2,1)S(1)}, bf16[32,1024]{1,0:T(8,128)(2,1)S(1)}, u32[]{:S(2)}, u32[]{:S(2)}) collective-permute-start(bf16[32,1024]{1,0:T(8,128)(2,1)S(1)} %copy-done.1), channel_id=1, source_target_pairs={{0,2},{1,3},{2,0},{3,1},{4,6},{5,7},{6,4},{7,5},{8,10},{9,11},{10,... | collective-permute-start | bytes 196616 | tf_op jit(solution)/shard_map/ppermute | solution.py:191
  9.8 3.6 %collective-permute-start = (bf16[32,1024]{1,0:T(8,128)(2,1)S(1)}, bf16[32,1024]{1,0:T(8,128)(2,1)S(1)}, u32[]{:S(2)}, u32[]{:S(2)}) collective-permute-start(bf16[32,1024]{1,0:T(8,128)(2,1)S(1)} %copy-done.1), channel_id=1, source_target_pairs={{0,1},{1,0},{2,3},{3,2},{4,5},{5,4},{6,7},{7,6},{8,9},{9,8},{10,11... | collective-permute-start | bytes 196616 | tf_op jit(solution)/shard_map/ppermute | solution.py:191
  9.8 3.7 %collective-permute-start.2 = (bf16[32,1024]{1,0:T(8,128)(2,1)S(1)}, bf16[32,1024]{1,0:T(8,128)(2,1)S(1)}, u32[]{:S(2)}, u32[]{:S(2)}) collective-permute-start(bf16[32,1024]{1,0:T(8,128)(2,1)S(1)} %copy-done.1), channel_id=1, source_target_pairs={{0,3},{1,2},{2,1},{3,0},{4,7},{5,6},{6,5},{7,4},{8,11},{9,10},{10,... | collective-permute-start | bytes 196616 | tf_op jit(solution)/shard_map/ppermute | solution.py:191
  11.7 1.9 %copy-start = (bf16[32,4096]{1,0:T(8,128)(2,1)S(1)}, bf16[32,4096]{1,0:T(8,128)(2,1)}, u32[]{:S(2)}) copy-start(bf16[32,4096]{1,0:T(8,128)(2,1)} %q_ref.5) | copy-start | bytes 786436
  11.7 1.9 %collective-permute-start.7 = (bf16[256,256]{1,0:T(8,128)(2,1)S(1)}, bf16[256,256]{1,0:T(8,128)(2,1)S(1)}, u32[]{:S(2)}, u32[]{:S(2)}) collective-permute-start(bf16[256,256]{1,0:T(8,128)(2,1)S(1)} %choose.1.refs_0_), channel_id=1, source_target_pairs={{0,1},{1,0},{2,3},{3,2},{4,5},{5,4},{6,7},{7,6},{8,9},{9,8},{10,11... | collective-permute-start | bytes 393224 | tf_op jit(solution)/shard_map/ppermute | solution.py:202
  11.8 5.9 %collective-permute-start.6 = (bf16[256,256]{1,0:T(8,128)(2,1)S(1)}, bf16[256,256]{1,0:T(8,128)(2,1)S(1)}, u32[]{:S(2)}, u32[]{:S(2)}) collective-permute-start(bf16[256,256]{1,0:T(8,128)(2,1)S(1)} %choose.1.refs_0_), channel_id=1, source_target_pairs={{0,2},{1,3},{2,0},{3,1},{4,6},{5,7},{6,4},{7,5},{8,10},{9,11},{10,... | collective-permute-start | bytes 393224 | tf_op jit(solution)/shard_map/ppermute | solution.py:203
  17.7 1.3 %collective-permute-start.8 = (bf16[256,256]{1,0:T(8,128)(2,1)S(1)}, bf16[256,256]{1,0:T(8,128)(2,1)S(1)}, u32[]{:S(2)}, u32[]{:S(2)}) collective-permute-start(bf16[256,256]{1,0:T(8,128)(2,1)S(1)} %after.1.refs_0_), channel_id=1, source_target_pairs={{0,1},{1,0},{2,3},{3,2},{4,5},{5,4},{6,7},{7,6},{8,9},{9,8},{10,11... | collective-permute-start | bytes 393224 | tf_op jit(solution)/shard_map/ppermute | solution.py:233

commit v6 on v5

--- a/solution.py
+++ b/solution.py
@@ -11,7 +11,7 @@
 LOG2E = 1.4426950408889634
 MAX_DIRECT = 4
 UNUSED = 1 << 20
-CHOOSE, GATHER, EARLY, MID = 10**8, 10**10, 10**10, 10**9
+CHOOSE, GATHER, EARLY, MID = 10**7, 10**8, 10**9, 10**8
 ANY = pl.BlockSpec(memory_space=pl.ANY)
 SMEM = pl.BlockSpec(memory_space=pltpu.SMEM)
 VMEM = pl.BlockSpec(memory_space=pltpu.VMEM)
@@ -221,7 +221,7 @@
             name=name,
         )(*given, *[vmem(chosen[m]) for m in mine])
 
-    near = stage((0, 1), "early", EARLY)
+    (own,) = stage((0,), "early", EARLY)
     chosen[2] = pl.pallas_call(
         after_kernel,
         out_shape=pltpu.VMEM(chosen[2].shape, bf16),
@@ -229,9 +229,9 @@
         out_specs=VMEM,
         input_output_aliases={0: 0},
         name="after",
-    )(vmem(chosen[2]), vmem(near[0]))
+    )(vmem(chosen[2]), vmem(own))
     chosen[3] = lax.ppermute(chosen[2], "head", across[1])
-    across_x = stage((2,), "mid", MID)
+    middle = stage((1, 2), "mid", MID)
     return pl.pallas_call(
         functools.partial(late_kernel, n_head, (0, 1, 2), (3,)),
         out_shape=jax.ShapeDtypeStruct(queries.shape, bf16),
@@ -239,7 +239,7 @@
         out_specs=ANY,
         scratch_shapes=[pltpu.VMEM((1, rows, q_cols), bf16), pltpu.SemaphoreType.DMA((n_head,))],
         name="late",
-    )(*given, vmem(chosen[3]), *map(vmem, [*near, *across_x]))
+    )(*given, vmem(chosen[3]), *map(vmem, [own, *middle]))
 
 
 def collect_kernel(n_ctx, block, pattern_ref, counts_ref, cache_ref, out_ref, sem):

time: 20.4 us -> 19.6 us (0.961)
  waiting for transfers between devices: 5.63 us -> 5 us
    ppermute x1, waiting for transfers between devices: 3.37 us -> 2.97 us  [direct(): chosen[2] = lax.ppermute(chosen[0], 'head', across[2])]
    ppermute x1, waiting for transfers between devices: 0.89 us -> 0.59 us  [direct(): chosen[3] = lax.ppermute(chosen[2], 'head', across[1])]
where the time goes in v6:
time: 19.6 us; the launch traced here: 19.5 us
  starting transfers between devices  10.8 us (55%)
  waiting for transfers between devices  5 us (26%)
  Pallas kernels  3.67 us (19%)
    ppermute x3, starting transfers between devices, direct(): blocks[k] = lax.ppermute(blocks[k], 'ctx', around[k])  7.01 us
    ppermute x1, waiting for transfers between devices, direct(): chosen[2] = lax.ppermute(chosen[0], 'head', across[2])  2.97 us
    ppermute x3, starting transfers between devices, direct(): pieces[m] = lax.ppermute(span_key_value, 'head', across[m])  2.14 us
    ppermute x1, starting transfers between devices, direct(): chosen[2] = lax.ppermute(chosen[0], 'head', across[2])  1.6 us
    pallas_call x1, Pallas kernels, direct(): pl.pallas_call(functools.partial(prepare_kernel, n_ctx), out_shape=[pltpu...  1.3 us
    ppermute x3, waiting for transfers between devices, direct(): blocks[k] = lax.ppermute(blocks[k], 'ctx', around[k])  1.22 us
    pallas_call x2, Pallas kernels, stage(): pl.pallas_call(functools.partial(early_kernel, n_head, mine), out_shape=[...  1.2 us
    pallas_call x1, Pallas kernels, direct(): pl.pallas_call(functools.partial(late_kernel, n_head, (0, 1, 2), (3,)), o...  1.12 us
  transfers between devices with their start and end apart: 9, of which 5 were waited for; matrix products, arithmetic and copies ran while one was open for 0% of the time, Pallas kernels for 6%

profile of v6, /device:TPU:0, one launch (start us, length us, event | category | flops | bytes accessed | tf_op | source)
XLA Modules:
  0.0 19.5 jit_solution(5034264477033832557)
XLA Ops:
  0.0 1.3 %prepare.1 = (bf16[128,256]{1,0:T(8,128)(2,1)S(1)}, bf16[128,256]{1,0:T(8,128)(2,1)S(1)}, bf16[128,256]{1,0:T(8,128)(2,1)S(1)}, bf16[128,256]{1,0:T(8,128)(2,1)S(1)}, s32[2,256]{1,0:T(2,128)S(1)}) custom-call(s32[2,4]{1,0:T(2,128)} %bitcast.1, s32[4]{0:T(128)} %counts_hbm.1, bf16[1,2048,256]{2,1,0:T(8,128)(2,1)} %cache_ref.1), custom_call_target="tpu_custom_call" | custom-call | tf_op jit(solution)/shard_map/prepare/pallas_call | solution.py:173
  1.3 3.1 %collective-permute-start.3 = (bf16[128,256]{1,0:T(8,128)(2,1)S(1)}, bf16[128,256]{1,0:T(8,128)(2,1)S(1)}, u32[]{:S(2)}, u32[]{:S(2)}) collective-permute-start(bf16[128,256]{1,0:T(8,128)(2,1)S(1)} %get-tuple-element.14), channel_id=1, source_target_pairs={{0,4},{4,8},{8,12},{12,0},{1,5},{5,9},{9,13},{13,1},{2,6},{6,10},{... | collective-permute-start | bytes 196616 | tf_op jit(solution)/shard_map/ppermute | solution.py:188
  4.4 2.6 %collective-permute-start.4 = (bf16[128,256]{1,0:T(8,128)(2,1)S(1)}, bf16[128,256]{1,0:T(8,128)(2,1)S(1)}, u32[]{:S(2)}, u32[]{:S(2)}) collective-permute-start(bf16[128,256]{1,0:T(8,128)(2,1)S(1)} %get-tuple-element.15), channel_id=1, source_target_pairs={{0,8},{4,12},{8,0},{12,4},{1,9},{5,13},{9,1},{13,5},{2,10},{6,14},... | collective-permute-start | bytes 196616 | tf_op jit(solution)/shard_map/ppermute | solution.py:188
  7.0 1.3 %collective-permute-start.5 = (bf16[128,256]{1,0:T(8,128)(2,1)S(1)}, bf16[128,256]{1,0:T(8,128)(2,1)S(1)}, u32[]{:S(2)}, u32[]{:S(2)}) collective-permute-start(bf16[128,256]{1,0:T(8,128)(2,1)S(1)} %get-tuple-element.16), channel_id=1, source_target_pairs={{0,12},{4,0},{8,4},{12,8},{1,13},{5,1},{9,5},{13,9},{2,14},{6,2},{... | collective-permute-start | bytes 196616 | tf_op jit(solution)/shard_map/ppermute | solution.py:188
  8.3 0.0 copy-done.1
  8.3 1.5 %collective-permute-start.1 = (bf16[32,1024]{1,0:T(8,128)(2,1)S(1)}, bf16[32,1024]{1,0:T(8,128)(2,1)S(1)}, u32[]{:S(2)}, u32[]{:S(2)}) collective-permute-start(bf16[32,1024]{1,0:T(8,128)(2,1)S(1)} %copy-done.1), channel_id=1, source_target_pairs={{0,2},{1,3},{2,0},{3,1},{4,6},{5,7},{6,4},{7,5},{8,10},{9,11},{10,... | collective-permute-start | bytes 196616 | tf_op jit(solution)/shard_map/ppermute | solution.py:191
  9.8 0.0 collective-permute-start
  9.8 0.0 collective-permute-done.3.refs_1_
  9.8 0.6 %collective-permute-start.2 = (bf16[32,1024]{1,0:T(8,128)(2,1)S(1)}, bf16[32,1024]{1,0:T(8,128)(2,1)S(1)}, u32[]{:S(2)}, u32[]{:S(2)}) collective-permute-start(bf16[32,1024]{1,0:T(8,128)(2,1)S(1)} %copy-done.1), channel_id=1, source_target_pairs={{0,3},{1,2},{2,1},{3,0},{4,7},{5,6},{6,5},{7,4},{8,11},{9,10},{10,... | collective-permute-start | bytes 196616 | tf_op jit(solution)/shard_map/ppermute | solution.py:191
  10.5 1.0 %collective-permute-done.4.refs_2_ = bf16[128,256]{1,0:T(8,128)(2,1)S(1)} collective-permute-done((bf16[128,256]{1,0:T(8,128)(2,1)S(1)}, bf16[128,256]{1,0:T(8,128)(2,1)S(1)}, u32[]{:S(2)}, u32[]{:S(2)}) %collective-permute-start.4) | collective-permute-done | bytes 65568 | tf_op jit(solution)/shard_map/ppermute | solution.py:188
  11.5 0.2 %collective-permute-done.5.refs_3_ = bf16[128,256]{1,0:T(8,128)(2,1)S(1)} collective-permute-done((bf16[128,256]{1,0:T(8,128)(2,1)S(1)}, bf16[128,256]{1,0:T(8,128)(2,1)S(1)}, u32[]{:S(2)}, u32[]{:S(2)}) %collective-permute-start.5) | collective-permute-done | bytes 65568 | tf_op jit(solution)/shard_map/ppermute | solution.py:188
  11.7 0.0 copy-start
  11.7 1.6 %collective-permute-start.6 = (bf16[256,256]{1,0:T(8,128)(2,1)S(1)}, bf16[256,256]{1,0:T(8,128)(2,1)S(1)}, u32[]{:S(2)}, u32[]{:S(2)}) collective-permute-start(bf16[256,256]{1,0:T(8,128)(2,1)S(1)} %choose.1.refs_0_), channel_id=1, source_target_pairs={{0,2},{1,3},{2,0},{3,1},{4,6},{5,7},{6,4},{7,5},{8,10},{9,11},{10,... | collective-permute-start | bytes 393224 | tf_op jit(solution)/shard_map/ppermute | solution.py:203
  13.3 0.0 collective-permute-start.8
  13.3 0.0 collective-permute-done.1.refs_2_
  13.4 0.0 collective-permute-done.refs_1_
  13.4 0.2 %collective-permute-done.2.refs_3_ = bf16[32,1024]{1,0:T(8,128)(2,1)S(1)} collective-permute-done((bf16[32,1024]{1,0:T(8,128)(2,1)S(1)}, bf16[32,1024]{1,0:T(8,128)(2,1)S(1)}, u32[]{:S(2)}, u32[]{:S(2)}) %collective-permute-start.2) | collective-permute-done | bytes 65568 | tf_op jit(solution)/shard_map/ppermute | solution.py:191
  13.6 0.5 %early.1.first_ref.refs_1_ = bf16[32,1024]{1,0:T(8,128)(2,1)S(1)} custom-call(s32[2,256]{1,0:T(2,128)S(1)} %get-tuple-element.12.slots_ref, bf16[32,4096]{1,0:T(8,128)(2,1)S(1)} %copy-done, bf16[128,1024]{1,0:T(8,128)(2,1)S(1)} %gather.1.kv_ref, bf16[256,256]{1,0:T(8,128)(2,1)S(1)} %choose.1.refs_0_), custom_call_target="tpu_custom_call" | custom-call | flops 1000000000 | bytes 1048576 | tf_op jit(solution)/shard_map/early/pallas_call | solution.py:215
  14.1 3.0 %collective-permute-done.6.x_ref = bf16[256,256]{1,0:T(8,128)(2,1)S(1)} collective-permute-done((bf16[256,256]{1,0:T(8,128)(2,1)S(1)}, bf16[256,256]{1,0:T(8,128)(2,1)S(1)}, u32[]{:S(2)}, u32[]{:S(2)}) %collective-permute-start.6) | collective-permute-done | bytes 131104 | tf_op jit(solution)/shard_map/ppermute | solution.py:203
  17.0 0.0 collective-permute-start.7
  17.0 0.0 collective-permute-done.8.refs_0_
  17.0 0.7 %mid.1 = (bf16[32,1024]{1,0:T(8,128)(2,1)S(1)}, bf16[32,1024]{1,0:T(8,128)(2,1)S(1)}) custom-call(s32[2,256]{1,0:T(2,128)S(1)} %get-tuple-element.12.slots_ref, bf16[32,4096]{1,0:T(8,128)(2,1)S(1)} %copy-done, bf16[128,1024]{1,0:T(8,128)(2,1)S(1)} %gather.1.kv_ref, bf16[256,256]{1,0:T(8,128)(2,1)S(1)} %collective-permute-done.8.refs_0_, ...), custom_call_target="tpu_custom_call" | custom-call | flops 100000000 | bytes 1048576 | tf_op jit(solution)/shard_map/mid/pallas_call | solution.py:215
  17.8 0.6 %collective-permute-done.7.refs_0_ = bf16[256,256]{1,0:T(8,128)(2,1)S(1)} collective-permute-done((bf16[256,256]{1,0:T(8,128)(2,1)S(1)}, bf16[256,256]{1,0:T(8,128)(2,1)S(1)}, u32[]{:S(2)}, u32[]{:S(2)}) %collective-permute-start.7) | collective-permute-done | bytes 131104 | tf_op jit(solution)/shard_map/ppermute | solution.py:233
  18.4 1.1 %late.1 = bf16[32,4096]{1,0:T(8,128)(2,1)} custom-call(s32[2,256]{1,0:T(2,128)S(1)} %get-tuple-element.12.slots_ref, bf16[32,4096]{1,0:T(8,128)(2,1)S(1)} %copy-done, bf16[128,1024]{1,0:T(8,128)(2,1)S(1)} %gather.1.kv_ref, bf16[256,256]{1,0:T(8,128)(2,1)S(1)} %collective-permute-done.7.refs_0_, bf16[32,1024]{1,0:T(8,128)(2,1)S(1)} %early.1.first_ref.refs_1_, ...), custom_call_target="tpu_custom_call" | custom-call | tf_op jit(solution)/shard_map/late/pallas_call | solution.py:235
  (5 shorter events, 0.1 us)
Async XLA Ops:
  0.0 8.3 %copy-start.1 = (bf16[32,1024]{1,0:T(8,128)(2,1)S(1)}, bf16[32,1024]{1,0:T(8,128)(2,1)}, u32[]{:S(2)}) copy-start(bf16[32,1024]{1,0:T(8,128)(2,1)} %refs_0_.1) | copy-start | bytes 196612
  1.3 8.5 %collective-permute-start.3 = (bf16[128,256]{1,0:T(8,128)(2,1)S(1)}, bf16[128,256]{1,0:T(8,128)(2,1)S(1)}, u32[]{:S(2)}, u32[]{:S(2)}) collective-permute-start(bf16[128,256]{1,0:T(8,128)(2,1)S(1)} %get-tuple-element.14), channel_id=1, source_target_pairs={{0,4},{4,8},{8,12},{12,0},{1,5},{5,9},{9,13},{13,1},{2,6},{6,10},{... | collective-permute-start | bytes 196616 | tf_op jit(solution)/shard_map/ppermute | solution.py:188
  4.4 7.1 %collective-permute-start.4 = (bf16[128,256]{1,0:T(8,128)(2,1)S(1)}, bf16[128,256]{1,0:T(8,128)(2,1)S(1)}, u32[]{:S(2)}, u32[]{:S(2)}) collective-permute-start(bf16[128,256]{1,0:T(8,128)(2,1)S(1)} %get-tuple-element.15), channel_id=1, source_target_pairs={{0,8},{4,12},{8,0},{12,4},{1,9},{5,13},{9,1},{13,5},{2,10},{6,14},... | collective-permute-start | bytes 196616 | tf_op jit(solution)/shard_map/ppermute | solution.py:188
  7.0 4.7 %collective-permute-start.5 = (bf16[128,256]{1,0:T(8,128)(2,1)S(1)}, bf16[128,256]{1,0:T(8,128)(2,1)S(1)}, u32[]{:S(2)}, u32[]{:S(2)}) collective-permute-start(bf16[128,256]{1,0:T(8,128)(2,1)S(1)} %get-tuple-element.16), channel_id=1, source_target_pairs={{0,12},{4,0},{8,4},{12,8},{1,13},{5,1},{9,5},{13,9},{2,14},{6,2},{... | collective-permute-start | bytes 196616 | tf_op jit(solution)/shard_map/ppermute | solution.py:188
  8.3 5.0 %collective-permute-start.1 = (bf16[32,1024]{1,0:T(8,128)(2,1)S(1)}, bf16[32,1024]{1,0:T(8,128)(2,1)S(1)}, u32[]{:S(2)}, u32[]{:S(2)}) collective-permute-start(bf16[32,1024]{1,0:T(8,128)(2,1)S(1)} %copy-done.1), channel_id=1, source_target_pairs={{0,2},{1,3},{2,0},{3,1},{4,6},{5,7},{6,4},{7,5},{8,10},{9,11},{10,... | collective-permute-start | bytes 196616 | tf_op jit(solution)/shard_map/ppermute | solution.py:191
  9.8 3.5 %collective-permute-start = (bf16[32,1024]{1,0:T(8,128)(2,1)S(1)}, bf16[32,1024]{1,0:T(8,128)(2,1)S(1)}, u32[]{:S(2)}, u32[]{:S(2)}) collective-permute-start(bf16[32,1024]{1,0:T(8,128)(2,1)S(1)} %copy-done.1), channel_id=1, source_target_pairs={{0,1},{1,0},{2,3},{3,2},{4,5},{5,4},{6,7},{7,6},{8,9},{9,8},{10,11... | collective-permute-start | bytes 196616 | tf_op jit(solution)/shard_map/ppermute | solution.py:191
  9.8 3.7 %collective-permute-start.2 = (bf16[32,1024]{1,0:T(8,128)(2,1)S(1)}, bf16[32,1024]{1,0:T(8,128)(2,1)S(1)}, u32[]{:S(2)}, u32[]{:S(2)}) collective-permute-start(bf16[32,1024]{1,0:T(8,128)(2,1)S(1)} %copy-done.1), channel_id=1, source_target_pairs={{0,3},{1,2},{2,1},{3,0},{4,7},{5,6},{6,5},{7,4},{8,11},{9,10},{10,... | collective-permute-start | bytes 196616 | tf_op jit(solution)/shard_map/ppermute | solution.py:191
  11.7 1.9 %copy-start = (bf16[32,4096]{1,0:T(8,128)(2,1)S(1)}, bf16[32,4096]{1,0:T(8,128)(2,1)}, u32[]{:S(2)}) copy-start(bf16[32,4096]{1,0:T(8,128)(2,1)} %q_ref.5) | copy-start | bytes 786436
  11.7 5.3 %collective-permute-start.6 = (bf16[256,256]{1,0:T(8,128)(2,1)S(1)}, bf16[256,256]{1,0:T(8,128)(2,1)S(1)}, u32[]{:S(2)}, u32[]{:S(2)}) collective-permute-start(bf16[256,256]{1,0:T(8,128)(2,1)S(1)} %choose.1.refs_0_), channel_id=1, source_target_pairs={{0,2},{1,3},{2,0},{3,1},{4,6},{5,7},{6,4},{7,5},{8,10},{9,11},{10,... | collective-permute-start | bytes 393224 | tf_op jit(solution)/shard_map/ppermute | solution.py:203
  13.3 3.7 %collective-permute-start.8 = (bf16[256,256]{1,0:T(8,128)(2,1)S(1)}, bf16[256,256]{1,0:T(8,128)(2,1)S(1)}, u32[]{:S(2)}, u32[]{:S(2)}) collective-permute-start(bf16[256,256]{1,0:T(8,128)(2,1)S(1)} %choose.1.refs_0_), channel_id=1, source_target_pairs={{0,1},{1,0},{2,3},{3,2},{4,5},{5,4},{6,7},{7,6},{8,9},{9,8},{10,11... | collective-permute-start | bytes 393224 | tf_op jit(solution)/shard_map/ppermute | solution.py:202
  17.0 1.3 %collective-permute-start.7 = (bf16[256,256]{1,0:T(8,128)(2,1)S(1)}, bf16[256,256]{1,0:T(8,128)(2,1)S(1)}, u32[]{:S(2)}, u32[]{:S(2)}) collective-permute-start(bf16[256,256]{1,0:T(8,128)(2,1)S(1)} %after.1.refs_1_), channel_id=1, source_target_pairs={{0,1},{1,0},{2,3},{3,2},{4,5},{5,4},{6,7},{7,6},{8,9},{9,8},{10,11... | collective-permute-start | bytes 393224 | tf_op jit(solution)/shard_map/ppermute | solution.py:233

commit v7 on v6

--- a/solution.py
+++ b/solution.py
@@ -11,7 +11,7 @@
 LOG2E = 1.4426950408889634
 MAX_DIRECT = 4
 UNUSED = 1 << 20
-CHOOSE, GATHER, EARLY, MID = 10**7, 10**8, 10**9, 10**8
+CHOOSE, GATHER, EARLY, MID = 10**7, 10**8, 10**8, 10**8
 ANY = pl.BlockSpec(memory_space=pl.ANY)
 SMEM = pl.BlockSpec(memory_space=pltpu.SMEM)
 VMEM = pl.BlockSpec(memory_space=pltpu.VMEM)
@@ -187,8 +187,9 @@
     for k in range(1, n_ctx):
         blocks[k] = lax.ppermute(blocks[k], "ctx", around[k])
     pieces = [span_key_value] * n_head
-    for m in (2, 3, 1):
+    for m in (2, 1):
         pieces[m] = lax.ppermute(span_key_value, "head", across[m])
+    pieces[3] = lax.ppermute(pieces[2], "head", across[1])
     slots = vmem(slots)
     chosen = [None] * n_head
     chosen[0] = pl.pallas_call(

time: 19.6 us -> 19.4 us (0.990)
  starting transfers between devices: 10.8 us -> 10.6 us
    ppermute x1, waiting for transfers between devices: 2.97 us -> 1.54 us  [direct(): chosen[2] = lax.ppermute(chosen[0], 'head', across[2])]
    ppermute x3, waiting for transfers between devices: 1.22 us -> 1.87 us  [direct(): blocks[k] = lax.ppermute(blocks[k], 'ctx', around[k])]
    ppermute x3 -> x2, starting transfers between devices: 2.14 us -> 1.49 us  [direct(): pieces[m] = lax.ppermute(span_key_value, 'head', across[m])]
    ppermute x3 -> x2, waiting for transfers between devices: 0.22 us -> 0.74 us  [direct(): pieces[m] = lax.ppermute(span_key_value, 'head', across[m])]
    ppermute x0 -> x1, starting transfers between devices: none -> 0.51 us  [direct(): pieces[3] = lax.ppermute(pieces[2], 'head', across[1])]
  transfers between devices with their start and end apart: 9 -> 9, of which waited for: 5 -> 6; matrix products, arithmetic and copies ran while one was open for 0% -> 0% of each run, Pallas kernels for 6% -> 6%
where the time goes in v7:
time: 19.4 us; the launch traced here: 19.3 us
  starting transfers between devices  10.6 us (55%)
  waiting for transfers between devices  4.91 us (25%)
  Pallas kernels  3.68 us (19%)
    ppermute x3, starting transfers between devices, direct(): blocks[k] = lax.ppermute(blocks[k], 'ctx', around[k])  7.01 us
    ppermute x3, waiting for transfers between devices, direct(): blocks[k] = lax.ppermute(blocks[k], 'ctx', around[k])  1.87 us
    ppermute x1, starting transfers between devices, direct(): chosen[2] = lax.ppermute(chosen[0], 'head', across[2])  1.6 us
    ppermute x1, waiting for transfers between devices, direct(): chosen[2] = lax.ppermute(chosen[0], 'head', across[2])  1.54 us
    ppermute x2, starting transfers between devices, direct(): pieces[m] = lax.ppermute(span_key_value, 'head', across[m])  1.49 us
    pallas_call x1, Pallas kernels, direct(): pl.pallas_call(functools.partial(prepare_kernel, n_ctx), out_shape=[pltpu...  1.3 us
    pallas_call x2, Pallas kernels, stage(): pl.pallas_call(functools.partial(early_kernel, n_head, mine), out_shape=[...  1.2 us
    pallas_call x1, Pallas kernels, direct(): pl.pallas_call(functools.partial(late_kernel, n_head, (0, 1, 2), (3,)), o...  1.12 us
  transfers between devices with their start and end apart: 9, of which 6 were waited for; matrix products, arithmetic and copies ran while one was open for 0% of the time, Pallas kernels for 6%

profile of v7, /device:TPU:0, one launch (start us, length us, event | category | flops | bytes accessed | tf_op | source)
XLA Modules:
  0.0 19.3 jit_solution(7860563537113392623)
XLA Ops:
  0.0 1.3 %prepare.1 = (bf16[128,256]{1,0:T(8,128)(2,1)S(1)}, bf16[128,256]{1,0:T(8,128)(2,1)S(1)}, bf16[128,256]{1,0:T(8,128)(2,1)S(1)}, bf16[128,256]{1,0:T(8,128)(2,1)S(1)}, s32[2,256]{1,0:T(2,128)S(1)}) custom-call(s32[2,4]{1,0:T(2,128)} %bitcast.1, s32[4]{0:T(128)} %counts_hbm.1, bf16[1,2048,256]{2,1,0:T(8,128)(2,1)} %cache_ref.1), custom_call_target="tpu_custom_call" | custom-call | tf_op jit(solution)/shard_map/prepare/pallas_call | solution.py:173
  1.3 3.1 %collective-permute-start.3 = (bf16[128,256]{1,0:T(8,128)(2,1)S(1)}, bf16[128,256]{1,0:T(8,128)(2,1)S(1)}, u32[]{:S(2)}, u32[]{:S(2)}) collective-permute-start(bf16[128,256]{1,0:T(8,128)(2,1)S(1)} %get-tuple-element.14), channel_id=1, source_target_pairs={{0,4},{4,8},{8,12},{12,0},{1,5},{5,9},{9,13},{13,1},{2,6},{6,10},{... | collective-permute-start | bytes 196616 | tf_op jit(solution)/shard_map/ppermute | solution.py:188
  4.4 2.6 %collective-permute-start.4 = (bf16[128,256]{1,0:T(8,128)(2,1)S(1)}, bf16[128,256]{1,0:T(8,128)(2,1)S(1)}, u32[]{:S(2)}, u32[]{:S(2)}) collective-permute-start(bf16[128,256]{1,0:T(8,128)(2,1)S(1)} %get-tuple-element.15), channel_id=1, source_target_pairs={{0,8},{4,12},{8,0},{12,4},{1,9},{5,13},{9,1},{13,5},{2,10},{6,14},... | collective-permute-start | bytes 196616 | tf_op jit(solution)/shard_map/ppermute | solution.py:188
  7.0 1.3 %collective-permute-start.5 = (bf16[128,256]{1,0:T(8,128)(2,1)S(1)}, bf16[128,256]{1,0:T(8,128)(2,1)S(1)}, u32[]{:S(2)}, u32[]{:S(2)}) collective-permute-start(bf16[128,256]{1,0:T(8,128)(2,1)S(1)} %get-tuple-element.16), channel_id=1, source_target_pairs={{0,12},{4,0},{8,4},{12,8},{1,13},{5,1},{9,5},{13,9},{2,14},{6,2},{... | collective-permute-start | bytes 196616 | tf_op jit(solution)/shard_map/ppermute | solution.py:188
  8.3 0.0 copy-done.1
  8.3 1.5 %collective-permute-start.1 = (bf16[32,1024]{1,0:T(8,128)(2,1)S(1)}, bf16[32,1024]{1,0:T(8,128)(2,1)S(1)}, u32[]{:S(2)}, u32[]{:S(2)}) collective-permute-start(bf16[32,1024]{1,0:T(8,128)(2,1)S(1)} %copy-done.1), channel_id=1, source_target_pairs={{0,2},{1,3},{2,0},{3,1},{4,6},{5,7},{6,4},{7,5},{8,10},{9,11},{10,... | collective-permute-start | bytes 196616 | tf_op jit(solution)/shard_map/ppermute | solution.py:191
  9.8 0.0 collective-permute-done.3.refs_1_
  9.8 1.6 %collective-permute-done.4.refs_2_ = bf16[128,256]{1,0:T(8,128)(2,1)S(1)} collective-permute-done((bf16[128,256]{1,0:T(8,128)(2,1)S(1)}, bf16[128,256]{1,0:T(8,128)(2,1)S(1)}, u32[]{:S(2)}, u32[]{:S(2)}) %collective-permute-start.4) | collective-permute-done | bytes 65568 | tf_op jit(solution)/shard_map/ppermute | solution.py:188
  11.5 0.2 %collective-permute-done.5.refs_3_ = bf16[128,256]{1,0:T(8,128)(2,1)S(1)} collective-permute-done((bf16[128,256]{1,0:T(8,128)(2,1)S(1)}, bf16[128,256]{1,0:T(8,128)(2,1)S(1)}, u32[]{:S(2)}, u32[]{:S(2)}) %collective-permute-start.5) | collective-permute-done | bytes 65568 | tf_op jit(solution)/shard_map/ppermute | solution.py:188
  11.7 0.0 copy-start
  11.7 1.6 %collective-permute-start.6 = (bf16[256,256]{1,0:T(8,128)(2,1)S(1)}, bf16[256,256]{1,0:T(8,128)(2,1)S(1)}, u32[]{:S(2)}, u32[]{:S(2)}) collective-permute-start(bf16[256,256]{1,0:T(8,128)(2,1)S(1)} %choose.1.refs_0_), channel_id=1, source_target_pairs={{0,2},{1,3},{2,0},{3,1},{4,6},{5,7},{6,4},{7,5},{8,10},{9,11},{10,... | collective-permute-start | bytes 393224 | tf_op jit(solution)/shard_map/ppermute | solution.py:204
  13.3 0.0 collective-permute-start
  13.3 0.0 collective-permute-done.1.refs_2_
  13.4 0.5 %collective-permute-start.2 = (bf16[32,1024]{1,0:T(8,128)(2,1)S(1)}, bf16[32,1024]{1,0:T(8,128)(2,1)S(1)}, u32[]{:S(2)}, u32[]{:S(2)}) collective-permute-start(bf16[32,1024]{1,0:T(8,128)(2,1)S(1)} %collective-permute-done.1.refs_2_), channel_id=1, source_target_pairs={{0,1},{1,0},{2,3},{3,2},{4,5},{5,4},{6,7},{7,6},{8,9},{9,8},{10,11... | collective-permute-start | bytes 196616 | tf_op jit(solution)/shard_map/ppermute | solution.py:192
  13.9 0.0 collective-permute-start.8
  13.9 0.7 %collective-permute-done.refs_1_ = bf16[32,1024]{1,0:T(8,128)(2,1)S(1)} collective-permute-done((bf16[32,1024]{1,0:T(8,128)(2,1)S(1)}, bf16[32,1024]{1,0:T(8,128)(2,1)S(1)}, u32[]{:S(2)}, u32[]{:S(2)}) %collective-permute-start) | collective-permute-done | bytes 65568 | tf_op jit(solution)/shard_map/ppermute | solution.py:191
  14.6 0.2 collective-permute-done.2.refs_3_
  14.8 0.5 %early.1.first_ref.refs_1_ = bf16[32,1024]{1,0:T(8,128)(2,1)S(1)} custom-call(s32[2,256]{1,0:T(2,128)S(1)} %get-tuple-element.12.slots_ref, bf16[32,4096]{1,0:T(8,128)(2,1)S(1)} %copy-done, bf16[128,1024]{1,0:T(8,128)(2,1)S(1)} %gather.1.kv_ref, bf16[256,256]{1,0:T(8,128)(2,1)S(1)} %choose.1.refs_0_), custom_call_target="tpu_custom_call" | custom-call | flops 100000000 | bytes 1048576 | tf_op jit(solution)/shard_map/early/pallas_call | solution.py:216
  15.3 1.5 %collective-permute-done.6.x_ref = bf16[256,256]{1,0:T(8,128)(2,1)S(1)} collective-permute-done((bf16[256,256]{1,0:T(8,128)(2,1)S(1)}, bf16[256,256]{1,0:T(8,128)(2,1)S(1)}, u32[]{:S(2)}, u32[]{:S(2)}) %collective-permute-start.6) | collective-permute-done | bytes 131104 | tf_op jit(solution)/shard_map/ppermute | solution.py:204
  16.8 0.0 collective-permute-start.7
  16.8 0.0 collective-permute-done.8.refs_0_
  16.8 0.7 %mid.1 = (bf16[32,1024]{1,0:T(8,128)(2,1)S(1)}, bf16[32,1024]{1,0:T(8,128)(2,1)S(1)}) custom-call(s32[2,256]{1,0:T(2,128)S(1)} %get-tuple-element.12.slots_ref, bf16[32,4096]{1,0:T(8,128)(2,1)S(1)} %copy-done, bf16[128,1024]{1,0:T(8,128)(2,1)S(1)} %gather.1.kv_ref, bf16[256,256]{1,0:T(8,128)(2,1)S(1)} %collective-permute-done.8.refs_0_, ...), custom_call_target="tpu_custom_call" | custom-call | flops 100000000 | bytes 1048576 | tf_op jit(solution)/shard_map/mid/pallas_call | solution.py:216
  17.6 0.6 %collective-permute-done.7.refs_0_ = bf16[256,256]{1,0:T(8,128)(2,1)S(1)} collective-permute-done((bf16[256,256]{1,0:T(8,128)(2,1)S(1)}, bf16[256,256]{1,0:T(8,128)(2,1)S(1)}, u32[]{:S(2)}, u32[]{:S(2)}) %collective-permute-start.7) | collective-permute-done | bytes 131104 | tf_op jit(solution)/shard_map/ppermute | solution.py:234
  18.1 1.1 %late.1 = bf16[32,4096]{1,0:T(8,128)(2,1)} custom-call(s32[2,256]{1,0:T(2,128)S(1)} %get-tuple-element.12.slots_ref, bf16[32,4096]{1,0:T(8,128)(2,1)S(1)} %copy-done, bf16[128,1024]{1,0:T(8,128)(2,1)S(1)} %gather.1.kv_ref, bf16[256,256]{1,0:T(8,128)(2,1)S(1)} %collective-permute-done.7.refs_0_, bf16[32,1024]{1,0:T(8,128)(2,1)S(1)} %early.1.first_ref.refs_1_, ...), custom_call_target="tpu_custom_call" | custom-call | tf_op jit(solution)/shard_map/late/pallas_call | solution.py:236
  (5 shorter events, 0.1 us)
Async XLA Ops:
  0.0 8.3 %copy-start.1 = (bf16[32,1024]{1,0:T(8,128)(2,1)S(1)}, bf16[32,1024]{1,0:T(8,128)(2,1)}, u32[]{:S(2)}) copy-start(bf16[32,1024]{1,0:T(8,128)(2,1)} %refs_0_.1) | copy-start | bytes 196612
  1.3 8.5 %collective-permute-start.3 = (bf16[128,256]{1,0:T(8,128)(2,1)S(1)}, bf16[128,256]{1,0:T(8,128)(2,1)S(1)}, u32[]{:S(2)}, u32[]{:S(2)}) collective-permute-start(bf16[128,256]{1,0:T(8,128)(2,1)S(1)} %get-tuple-element.14), channel_id=1, source_target_pairs={{0,4},{4,8},{8,12},{12,0},{1,5},{5,9},{9,13},{13,1},{2,6},{6,10},{... | collective-permute-start | bytes 196616 | tf_op jit(solution)/shard_map/ppermute | solution.py:188
  4.4 7.1 %collective-permute-start.4 = (bf16[128,256]{1,0:T(8,128)(2,1)S(1)}, bf16[128,256]{1,0:T(8,128)(2,1)S(1)}, u32[]{:S(2)}, u32[]{:S(2)}) collective-permute-start(bf16[128,256]{1,0:T(8,128)(2,1)S(1)} %get-tuple-element.15), channel_id=1, source_target_pairs={{0,8},{4,12},{8,0},{12,4},{1,9},{5,13},{9,1},{13,5},{2,10},{6,14},... | collective-permute-start | bytes 196616 | tf_op jit(solution)/shard_map/ppermute | solution.py:188
  7.0 4.7 %collective-permute-start.5 = (bf16[128,256]{1,0:T(8,128)(2,1)S(1)}, bf16[128,256]{1,0:T(8,128)(2,1)S(1)}, u32[]{:S(2)}, u32[]{:S(2)}) collective-permute-start(bf16[128,256]{1,0:T(8,128)(2,1)S(1)} %get-tuple-element.16), channel_id=1, source_target_pairs={{0,12},{4,0},{8,4},{12,8},{1,13},{5,1},{9,5},{13,9},{2,14},{6,2},{... | collective-permute-start | bytes 196616 | tf_op jit(solution)/shard_map/ppermute | solution.py:188
  8.3 5.0 %collective-permute-start.1 = (bf16[32,1024]{1,0:T(8,128)(2,1)S(1)}, bf16[32,1024]{1,0:T(8,128)(2,1)S(1)}, u32[]{:S(2)}, u32[]{:S(2)}) collective-permute-start(bf16[32,1024]{1,0:T(8,128)(2,1)S(1)} %copy-done.1), channel_id=1, source_target_pairs={{0,2},{1,3},{2,0},{3,1},{4,6},{5,7},{6,4},{7,5},{8,10},{9,11},{10,... | collective-permute-start | bytes 196616 | tf_op jit(solution)/shard_map/ppermute | solution.py:191
  11.7 3.1 %copy-start = (bf16[32,4096]{1,0:T(8,128)(2,1)S(1)}, bf16[32,4096]{1,0:T(8,128)(2,1)}, u32[]{:S(2)}) copy-start(bf16[32,4096]{1,0:T(8,128)(2,1)} %q_ref.5) | copy-start | bytes 786436
  11.7 5.1 %collective-permute-start.6 = (bf16[256,256]{1,0:T(8,128)(2,1)S(1)}, bf16[256,256]{1,0:T(8,128)(2,1)S(1)}, u32[]{:S(2)}, u32[]{:S(2)}) collective-permute-start(bf16[256,256]{1,0:T(8,128)(2,1)S(1)} %choose.1.refs_0_), channel_id=1, source_target_pairs={{0,2},{1,3},{2,0},{3,1},{4,6},{5,7},{6,4},{7,5},{8,10},{9,11},{10,... | collective-permute-start | bytes 393224 | tf_op jit(solution)/shard_map/ppermute | solution.py:204
  13.3 1.3 %collective-permute-start = (bf16[32,1024]{1,0:T(8,128)(2,1)S(1)}, bf16[32,1024]{1,0:T(8,128)(2,1)S(1)}, u32[]{:S(2)}, u32[]{:S(2)}) collective-permute-start(bf16[32,1024]{1,0:T(8,128)(2,1)S(1)} %copy-done.1), channel_id=1, source_target_pairs={{0,1},{1,0},{2,3},{3,2},{4,5},{5,4},{6,7},{7,6},{8,9},{9,8},{10,11... | collective-permute-start | bytes 196616 | tf_op jit(solution)/shard_map/ppermute | solution.py:191
  13.4 1.4 %collective-permute-start.2 = (bf16[32,1024]{1,0:T(8,128)(2,1)S(1)}, bf16[32,1024]{1,0:T(8,128)(2,1)S(1)}, u32[]{:S(2)}, u32[]{:S(2)}) collective-permute-start(bf16[32,1024]{1,0:T(8,128)(2,1)S(1)} %collective-permute-done.1.refs_2_), channel_id=1, source_target_pairs={{0,1},{1,0},{2,3},{3,2},{4,5},{5,4},{6,7},{7,6},{8,9},{9,8},{10,11... | collective-permute-start | bytes 196616 | tf_op jit(solution)/shard_map/ppermute | solution.py:192
  13.9 2.9 %collective-permute-start.8 = (bf16[256,256]{1,0:T(8,128)(2,1)S(1)}, bf16[256,256]{1,0:T(8,128)(2,1)S(1)}, u32[]{:S(2)}, u32[]{:S(2)}) collective-permute-start(bf16[256,256]{1,0:T(8,128)(2,1)S(1)} %choose.1.refs_0_), channel_id=1, source_target_pairs={{0,1},{1,0},{2,3},{3,2},{4,5},{5,4},{6,7},{7,6},{8,9},{9,8},{10,11... | collective-permute-start | bytes 393224 | tf_op jit(solution)/shard_map/ppermute | solution.py:203
  16.8 1.3 %collective-permute-start.7 = (bf16[256,256]{1,0:T(8,128)(2,1)S(1)}, bf16[256,256]{1,0:T(8,128)(2,1)S(1)}, u32[]{:S(2)}, u32[]{:S(2)}) collective-permute-start(bf16[256,256]{1,0:T(8,128)(2,1)S(1)} %after.1.refs_1_), channel_id=1, source_target_pairs={{0,1},{1,0},{2,3},{3,2},{4,5},{5,4},{6,7},{7,6},{8,9},{9,8},{10,11... | collective-permute-start | bytes 393224 | tf_op jit(solution)/shard_map/ppermute | solution.py:234

commit v8 on v7

--- a/solution.py
+++ b/solution.py
@@ -9,7 +9,6 @@
 from jax.sharding import PartitionSpec as P
 
 LOG2E = 1.4426950408889634
-MAX_DIRECT = 4
 UNUSED = 1 << 20
 CHOOSE, GATHER, EARLY, MID = 10**7, 10**8, 10**8, 10**8
 ANY = pl.BlockSpec(memory_space=pl.ANY)
@@ -34,6 +33,10 @@
             found = one(i, found)
         return found
     return lax.fori_loop(0, width, one, jnp.int32(0))
+
+
+def swap_ends(i):
+    return i ^ (i >> 1)
 
 
 def prepare_kernel(n_ctx, pattern_hbm, counts_hbm, cache_ref, *refs):
@@ -49,15 +52,16 @@
     for copy in lists:
         copy.wait()
     me = lax.axis_index("ctx")
+    place = swap_ends(me)
     block = blocks[0].shape[0]
     shard_blocks = shard_ref.shape[0] // block
     starts = []
     for k in range(n_ctx):
-        row = lax.rem(me + k, n_ctx)
+        row = swap_ends(lax.rem(place + k, n_ctx))
         index = wanted_index(pattern_ref, counts_ref, row, me, shard_blocks)
         starts.append(pl.multiple_of(index * block, block))
     for i in range(pattern_ref.shape[0]):
-        away = lax.rem(me - pattern_ref[i, me] // shard_blocks + n_ctx, n_ctx)
+        away = lax.rem(place - swap_ends(pattern_ref[i, me] // shard_blocks) + n_ctx, n_ctx)
         away = jnp.where(i < counts_ref[me], away, UNUSED)
         slots_ref[i : i + 1, :] = jnp.full((1, slots_ref.shape[1]), away, jnp.int32)
     shard.wait()
@@ -167,7 +171,9 @@
     q_cols = queries.shape[1] // n_head
     width = pattern.shape[1]
     bf16 = jnp.bfloat16
-    around = [[(i, (i + k) % n_ctx) for i in range(n_ctx)] for k in range(n_ctx)]
+    around = [
+        [(swap_ends(i), swap_ends((i + k) % n_ctx)) for i in range(n_ctx)] for k in range(n_ctx)
+    ]
     across = [[(i, i ^ m) for i in range(n_head)] for m in range(n_head)]
 
     *blocks, slots = pl.pallas_call(
@@ -330,7 +336,7 @@
 
 def solution(mesh):
     n_ctx, n_head = mesh.shape["ctx"], mesh.shape["head"]
-    form = direct if n_ctx <= MAX_DIRECT else general
+    form = direct if (n_ctx, n_head) == (4, 4) else general
     return jax.shard_map(
         functools.partial(form, n_ctx, n_head),
         mesh=mesh,

time: 19.4 us -> 19.3 us (level)
  waiting for transfers between devices: 4.91 us -> 4.7 us
    ppermute x3, waiting for transfers between devices: 1.87 us -> 1.63 us  [direct(): blocks[k] = lax.ppermute(blocks[k], 'ctx', around[k])]
  transfers between devices with their start and end apart: 9 -> 9, of which waited for: 6 -> 6; matrix products, arithmetic and copies ran while one was open for 0% -> 0% of each run, Pallas kernels for 6% -> 7%
where the time goes in v8:
time: 19.3 us; the launch traced here: 19.1 us
  starting transfers between devices  10.7 us (55%)
  waiting for transfers between devices  4.7 us (24%)
  Pallas kernels  3.67 us (19%)
    ppermute x3, starting transfers between devices, direct(): blocks[k] = lax.ppermute(blocks[k], 'ctx', around[k])  7.13 us
    ppermute x3, waiting for transfers between devices, direct(): blocks[k] = lax.ppermute(blocks[k], 'ctx', around[k])  1.63 us
    ppermute x1, waiting for transfers between devices, direct(): chosen[2] = lax.ppermute(chosen[0], 'head', across[2])  1.57 us
    ppermute x1, starting transfers between devices, direct(): chosen[2] = lax.ppermute(chosen[0], 'head', across[2])  1.56 us
    ppermute x2, starting transfers between devices, direct(): pieces[m] = lax.ppermute(span_key_value, 'head', across[m])  1.49 us
    pallas_call x1, Pallas kernels, direct(): pl.pallas_call(functools.partial(prepare_kernel, n_ctx), out_shape=[pltpu...  1.3 us
    pallas_call x2, Pallas kernels, stage(): pl.pallas_call(functools.partial(early_kernel, n_head, mine), out_shape=[...  1.2 us
    pallas_call x1, Pallas kernels, direct(): pl.pallas_call(functools.partial(late_kernel, n_head, (0, 1, 2), (3,)), o...  1.12 us
  transfers between devices with their start and end apart: 9, of which 6 were waited for; matrix products, arithmetic and copies ran while one was open for 0% of the time, Pallas kernels for 7%

profile of v8, /device:TPU:0, one launch (start us, length us, event | category | flops | bytes accessed | tf_op | source)
XLA Modules:
  0.0 19.1 jit_solution(17331329845436648169)
XLA Ops:
  0.0 1.3 %prepare.1 = (bf16[128,256]{1,0:T(8,128)(2,1)S(1)}, bf16[128,256]{1,0:T(8,128)(2,1)S(1)}, bf16[128,256]{1,0:T(8,128)(2,1)S(1)}, bf16[128,256]{1,0:T(8,128)(2,1)S(1)}, s32[2,256]{1,0:T(2,128)S(1)}) custom-call(s32[2,4]{1,0:T(2,128)} %bitcast.1, s32[4]{0:T(128)} %counts_hbm.1, bf16[1,2048,256]{2,1,0:T(8,128)(2,1)} %cache_ref.1), custom_call_target="tpu_custom_call" | custom-call | tf_op jit(solution)/shard_map/prepare/pallas_call | solution.py:179
  1.3 3.1 %collective-permute-start.3 = (bf16[128,256]{1,0:T(8,128)(2,1)S(1)}, bf16[128,256]{1,0:T(8,128)(2,1)S(1)}, u32[]{:S(2)}, u32[]{:S(2)}) collective-permute-start(bf16[128,256]{1,0:T(8,128)(2,1)S(1)} %get-tuple-element.14), channel_id=1, source_target_pairs={{0,4},{4,12},{12,8},{8,0},{1,5},{5,13},{13,9},{9,1},{2,6},{6,14},{... | collective-permute-start | bytes 196616 | tf_op jit(solution)/shard_map/ppermute | solution.py:194
  4.4 2.5 %collective-permute-start.4 = (bf16[128,256]{1,0:T(8,128)(2,1)S(1)}, bf16[128,256]{1,0:T(8,128)(2,1)S(1)}, u32[]{:S(2)}, u32[]{:S(2)}) collective-permute-start(bf16[128,256]{1,0:T(8,128)(2,1)S(1)} %get-tuple-element.15), channel_id=1, source_target_pairs={{0,12},{4,8},{12,0},{8,4},{1,13},{5,9},{13,1},{9,5},{2,14},{6,10},... | collective-permute-start | bytes 196616 | tf_op jit(solution)/shard_map/ppermute | solution.py:194
  6.9 1.6 %collective-permute-start.5 = (bf16[128,256]{1,0:T(8,128)(2,1)S(1)}, bf16[128,256]{1,0:T(8,128)(2,1)S(1)}, u32[]{:S(2)}, u32[]{:S(2)}) collective-permute-start(bf16[128,256]{1,0:T(8,128)(2,1)S(1)} %get-tuple-element.16), channel_id=1, source_target_pairs={{0,8},{4,0},{12,4},{8,12},{1,9},{5,1},{13,5},{9,13},{2,10},{6,2},{... | collective-permute-start | bytes 196616 | tf_op jit(solution)/shard_map/ppermute | solution.py:194
  8.4 0.0 copy-done.1
  8.4 1.5 %collective-permute-start.1 = (bf16[32,1024]{1,0:T(8,128)(2,1)S(1)}, bf16[32,1024]{1,0:T(8,128)(2,1)S(1)}, u32[]{:S(2)}, u32[]{:S(2)}) collective-permute-start(bf16[32,1024]{1,0:T(8,128)(2,1)S(1)} %copy-done.1), channel_id=1, source_target_pairs={{0,2},{1,3},{2,0},{3,1},{4,6},{5,7},{6,4},{7,5},{8,10},{9,11},{10,... | collective-permute-start | bytes 196616 | tf_op jit(solution)/shard_map/ppermute | solution.py:197
  9.9 0.0 collective-permute-done.3.refs_1_
  9.9 1.4 %collective-permute-done.4.refs_2_ = bf16[128,256]{1,0:T(8,128)(2,1)S(1)} collective-permute-done((bf16[128,256]{1,0:T(8,128)(2,1)S(1)}, bf16[128,256]{1,0:T(8,128)(2,1)S(1)}, u32[]{:S(2)}, u32[]{:S(2)}) %collective-permute-start.4) | collective-permute-done | bytes 65568 | tf_op jit(solution)/shard_map/ppermute | solution.py:194
  11.3 0.2 %collective-permute-done.5.refs_3_ = bf16[128,256]{1,0:T(8,128)(2,1)S(1)} collective-permute-done((bf16[128,256]{1,0:T(8,128)(2,1)S(1)}, bf16[128,256]{1,0:T(8,128)(2,1)S(1)}, u32[]{:S(2)}, u32[]{:S(2)}) %collective-permute-start.5) | collective-permute-done | bytes 65568 | tf_op jit(solution)/shard_map/ppermute | solution.py:194
  11.6 0.0 copy-start
  11.6 1.6 %collective-permute-start.6 = (bf16[256,256]{1,0:T(8,128)(2,1)S(1)}, bf16[256,256]{1,0:T(8,128)(2,1)S(1)}, u32[]{:S(2)}, u32[]{:S(2)}) collective-permute-start(bf16[256,256]{1,0:T(8,128)(2,1)S(1)} %choose.1.refs_0_), channel_id=1, source_target_pairs={{0,2},{1,3},{2,0},{3,1},{4,6},{5,7},{6,4},{7,5},{8,10},{9,11},{10,... | collective-permute-start | bytes 393224 | tf_op jit(solution)/shard_map/ppermute | solution.py:210
  13.2 0.0 collective-permute-start
  13.2 0.0 collective-permute-done.1.refs_2_
  13.2 0.5 %collective-permute-start.2 = (bf16[32,1024]{1,0:T(8,128)(2,1)S(1)}, bf16[32,1024]{1,0:T(8,128)(2,1)S(1)}, u32[]{:S(2)}, u32[]{:S(2)}) collective-permute-start(bf16[32,1024]{1,0:T(8,128)(2,1)S(1)} %collective-permute-done.1.refs_2_), channel_id=1, source_target_pairs={{0,1},{1,0},{2,3},{3,2},{4,5},{5,4},{6,7},{7,6},{8,9},{9,8},{10,11... | collective-permute-start | bytes 196616 | tf_op jit(solution)/shard_map/ppermute | solution.py:198
  13.7 0.0 collective-permute-start.8
  13.7 0.7 %collective-permute-done.refs_1_ = bf16[32,1024]{1,0:T(8,128)(2,1)S(1)} collective-permute-done((bf16[32,1024]{1,0:T(8,128)(2,1)S(1)}, bf16[32,1024]{1,0:T(8,128)(2,1)S(1)}, u32[]{:S(2)}, u32[]{:S(2)}) %collective-permute-start) | collective-permute-done | bytes 65568 | tf_op jit(solution)/shard_map/ppermute | solution.py:197
  14.4 0.2 collective-permute-done.2.refs_3_
  14.6 0.5 %early.1.first_ref.refs_1_ = bf16[32,1024]{1,0:T(8,128)(2,1)S(1)} custom-call(s32[2,256]{1,0:T(2,128)S(1)} %get-tuple-element.12.slots_ref, bf16[32,4096]{1,0:T(8,128)(2,1)S(1)} %copy-done, bf16[128,1024]{1,0:T(8,128)(2,1)S(1)} %gather.1.kv_ref, bf16[256,256]{1,0:T(8,128)(2,1)S(1)} %choose.1.refs_0_), custom_call_target="tpu_custom_call" | custom-call | flops 100000000 | bytes 1048576 | tf_op jit(solution)/shard_map/early/pallas_call | solution.py:222
  15.1 1.6 %collective-permute-done.6.x_ref = bf16[256,256]{1,0:T(8,128)(2,1)S(1)} collective-permute-done((bf16[256,256]{1,0:T(8,128)(2,1)S(1)}, bf16[256,256]{1,0:T(8,128)(2,1)S(1)}, u32[]{:S(2)}, u32[]{:S(2)}) %collective-permute-start.6) | collective-permute-done | bytes 131104 | tf_op jit(solution)/shard_map/ppermute | solution.py:210
  16.7 0.0 collective-permute-start.7
  16.7 0.0 collective-permute-done.8.refs_0_
  16.7 0.7 %mid.1 = (bf16[32,1024]{1,0:T(8,128)(2,1)S(1)}, bf16[32,1024]{1,0:T(8,128)(2,1)S(1)}) custom-call(s32[2,256]{1,0:T(2,128)S(1)} %get-tuple-element.12.slots_ref, bf16[32,4096]{1,0:T(8,128)(2,1)S(1)} %copy-done, bf16[128,1024]{1,0:T(8,128)(2,1)S(1)} %gather.1.kv_ref, bf16[256,256]{1,0:T(8,128)(2,1)S(1)} %collective-permute-done.8.refs_0_, ...), custom_call_target="tpu_custom_call" | custom-call | flops 100000000 | bytes 1048576 | tf_op jit(solution)/shard_map/mid/pallas_call | solution.py:222
  17.4 0.6 %collective-permute-done.7.refs_0_ = bf16[256,256]{1,0:T(8,128)(2,1)S(1)} collective-permute-done((bf16[256,256]{1,0:T(8,128)(2,1)S(1)}, bf16[256,256]{1,0:T(8,128)(2,1)S(1)}, u32[]{:S(2)}, u32[]{:S(2)}) %collective-permute-start.7) | collective-permute-done | bytes 131104 | tf_op jit(solution)/shard_map/ppermute | solution.py:240
  18.0 1.1 %late.1 = bf16[32,4096]{1,0:T(8,128)(2,1)} custom-call(s32[2,256]{1,0:T(2,128)S(1)} %get-tuple-element.12.slots_ref, bf16[32,4096]{1,0:T(8,128)(2,1)S(1)} %copy-done, bf16[128,1024]{1,0:T(8,128)(2,1)S(1)} %gather.1.kv_ref, bf16[256,256]{1,0:T(8,128)(2,1)S(1)} %collective-permute-done.7.refs_0_, bf16[32,1024]{1,0:T(8,128)(2,1)S(1)} %early.1.first_ref.refs_1_, ...), custom_call_target="tpu_custom_call" | custom-call | tf_op jit(solution)/shard_map/late/pallas_call | solution.py:242
  (5 shorter events, 0.1 us)
Async XLA Ops:
  0.0 8.4 %copy-start.1 = (bf16[32,1024]{1,0:T(8,128)(2,1)S(1)}, bf16[32,1024]{1,0:T(8,128)(2,1)}, u32[]{:S(2)}) copy-start(bf16[32,1024]{1,0:T(8,128)(2,1)} %refs_0_.1) | copy-start | bytes 196612
  1.3 8.6 %collective-permute-start.3 = (bf16[128,256]{1,0:T(8,128)(2,1)S(1)}, bf16[128,256]{1,0:T(8,128)(2,1)S(1)}, u32[]{:S(2)}, u32[]{:S(2)}) collective-permute-start(bf16[128,256]{1,0:T(8,128)(2,1)S(1)} %get-tuple-element.14), channel_id=1, source_target_pairs={{0,4},{4,12},{12,8},{8,0},{1,5},{5,13},{13,9},{9,1},{2,6},{6,14},{... | collective-permute-start | bytes 196616 | tf_op jit(solution)/shard_map/ppermute | solution.py:194
  4.4 7.0 %collective-permute-start.4 = (bf16[128,256]{1,0:T(8,128)(2,1)S(1)}, bf16[128,256]{1,0:T(8,128)(2,1)S(1)}, u32[]{:S(2)}, u32[]{:S(2)}) collective-permute-start(bf16[128,256]{1,0:T(8,128)(2,1)S(1)} %get-tuple-element.15), channel_id=1, source_target_pairs={{0,12},{4,8},{12,0},{8,4},{1,13},{5,9},{13,1},{9,5},{2,14},{6,10},... | collective-permute-start | bytes 196616 | tf_op jit(solution)/shard_map/ppermute | solution.py:194
  6.9 4.7 %collective-permute-start.5 = (bf16[128,256]{1,0:T(8,128)(2,1)S(1)}, bf16[128,256]{1,0:T(8,128)(2,1)S(1)}, u32[]{:S(2)}, u32[]{:S(2)}) collective-permute-start(bf16[128,256]{1,0:T(8,128)(2,1)S(1)} %get-tuple-element.16), channel_id=1, source_target_pairs={{0,8},{4,0},{12,4},{8,12},{1,9},{5,1},{13,5},{9,13},{2,10},{6,2},{... | collective-permute-start | bytes 196616 | tf_op jit(solution)/shard_map/ppermute | solution.py:194
  8.4 4.7 %collective-permute-start.1 = (bf16[32,1024]{1,0:T(8,128)(2,1)S(1)}, bf16[32,1024]{1,0:T(8,128)(2,1)S(1)}, u32[]{:S(2)}, u32[]{:S(2)}) collective-permute-start(bf16[32,1024]{1,0:T(8,128)(2,1)S(1)} %copy-done.1), channel_id=1, source_target_pairs={{0,2},{1,3},{2,0},{3,1},{4,6},{5,7},{6,4},{7,5},{8,10},{9,11},{10,... | collective-permute-start | bytes 196616 | tf_op jit(solution)/shard_map/ppermute | solution.py:197
  11.6 3.0 %copy-start = (bf16[32,4096]{1,0:T(8,128)(2,1)S(1)}, bf16[32,4096]{1,0:T(8,128)(2,1)}, u32[]{:S(2)}) copy-start(bf16[32,4096]{1,0:T(8,128)(2,1)} %q_ref.5) | copy-start | bytes 786436
  11.6 5.0 %collective-permute-start.6 = (bf16[256,256]{1,0:T(8,128)(2,1)S(1)}, bf16[256,256]{1,0:T(8,128)(2,1)S(1)}, u32[]{:S(2)}, u32[]{:S(2)}) collective-permute-start(bf16[256,256]{1,0:T(8,128)(2,1)S(1)} %choose.1.refs_0_), channel_id=1, source_target_pairs={{0,2},{1,3},{2,0},{3,1},{4,6},{5,7},{6,4},{7,5},{8,10},{9,11},{10,... | collective-permute-start | bytes 393224 | tf_op jit(solution)/shard_map/ppermute | solution.py:210
  13.2 1.3 %collective-permute-start = (bf16[32,1024]{1,0:T(8,128)(2,1)S(1)}, bf16[32,1024]{1,0:T(8,128)(2,1)S(1)}, u32[]{:S(2)}, u32[]{:S(2)}) collective-permute-start(bf16[32,1024]{1,0:T(8,128)(2,1)S(1)} %copy-done.1), channel_id=1, source_target_pairs={{0,1},{1,0},{2,3},{3,2},{4,5},{5,4},{6,7},{7,6},{8,9},{9,8},{10,11... | collective-permute-start | bytes 196616 | tf_op jit(solution)/shard_map/ppermute | solution.py:197
  13.2 1.4 %collective-permute-start.2 = (bf16[32,1024]{1,0:T(8,128)(2,1)S(1)}, bf16[32,1024]{1,0:T(8,128)(2,1)S(1)}, u32[]{:S(2)}, u32[]{:S(2)}) collective-permute-start(bf16[32,1024]{1,0:T(8,128)(2,1)S(1)} %collective-permute-done.1.refs_2_), channel_id=1, source_target_pairs={{0,1},{1,0},{2,3},{3,2},{4,5},{5,4},{6,7},{7,6},{8,9},{9,8},{10,11... | collective-permute-start | bytes 196616 | tf_op jit(solution)/shard_map/ppermute | solution.py:198
  13.7 3.0 %collective-permute-start.8 = (bf16[256,256]{1,0:T(8,128)(2,1)S(1)}, bf16[256,256]{1,0:T(8,128)(2,1)S(1)}, u32[]{:S(2)}, u32[]{:S(2)}) collective-permute-start(bf16[256,256]{1,0:T(8,128)(2,1)S(1)} %choose.1.refs_0_), channel_id=1, source_target_pairs={{0,1},{1,0},{2,3},{3,2},{4,5},{5,4},{6,7},{7,6},{8,9},{9,8},{10,11... | collective-permute-start | bytes 393224 | tf_op jit(solution)/shard_map/ppermute | solution.py:209
  16.7 1.3 %collective-permute-start.7 = (bf16[256,256]{1,0:T(8,128)(2,1)S(1)}, bf16[256,256]{1,0:T(8,128)(2,1)S(1)}, u32[]{:S(2)}, u32[]{:S(2)}) collective-permute-start(bf16[256,256]{1,0:T(8,128)(2,1)S(1)} %after.1.refs_1_), channel_id=1, source_target_pairs={{0,1},{1,0},{2,3},{3,2},{4,5},{5,4},{6,7},{7,6},{8,9},{9,8},{10,11... | collective-permute-start | bytes 393224 | tf_op jit(solution)/shard_map/ppermute | solution.py:240
